TPU v7x, 32 devices: a whole 2x2x4 slice. The times are simulated.
32 devices in a mesh: loop: 16 (over z, x, core), bcast: 2 (over y).
Axes of the slice: x: 2, y: 2, z: 4, core: 2. Of those that a mesh axis runs over, the one named last changes fastest.
Arguments:
- s_blocks: float32 [16, 2, 2, 10, 256, 256], P('loop', 'bcast'), may hold values from -6 to 6
- s_list: int32 [16, 2, 2, 10, 2], P('loop', 'bcast'), may hold values from 0 to 3, as said below
- x_blocks: float32 [16, 2, 12, 256, 256], P('loop', 'bcast'), may hold values from -0.09375 to 0.09375
- x_list: int32 [16, 2, 12, 2], P('loop', 'bcast'), may hold values from 0 to 4, as said below
- c_list: int32 [16, 2, 10, 2], P('loop', 'bcast'), may hold values from 0 to 3, as said below
- owner: int32 [16, 4], P('loop'), may hold values from 0 to 1, as said below
Outputs:
- product: float32 [16, 2, 10, 256, 256], P('loop', 'bcast')
Inputs may be any that keep to these rules, and one draw needn't show every extreme that they name: `s_list`: positions within one list are distinct. `x_list`: positions within one list are distinct; entries with first value 4 are empty and stand after the occupied ones; some device's list has no empty entry. `c_list`: positions within one list are distinct. owner[l, s] = (s + q_l) mod 2 for a whole number q_l of each block-row group.
All inputs are finite; a program needn't handle non-finite values.
Results may differ from a plain program's by a relative error of at most 0.0003.
Values sent between devices are 32-bit elements; how exact they have to be, the bound alone decides.
No kernel may reach another device: no remote copies, remote signals or barrier semaphores. Data moves between devices by JAX's collectives and lax.ppermute only.
A program may use at most 192 MiB of HBM per device.

v0:
```python
import jax
import jax.numpy as jnp
from jax import lax
from jax.sharding import PartitionSpec as P

RB = 3
KB = 4
CB = 4
STEPS = 4


HIGHEST = lax.Precision.HIGHEST


def shifted(shard, axis, by):
    length = lax.axis_size(axis)
    return lax.ppermute(shard, axis, [(i, (i + by) % length) for i in range(length)])


def spread(block, axis, owner):
    block = jnp.where(lax.axis_index(axis) == owner, block, jnp.zeros_like(block))
    return lax.psum(block, axis)


def densify(blocks, places, row_count, col_count):
    whole = places.astype(jnp.int32)
    chosen = (whole[:, 0][:, None, None] == jnp.arange(row_count)[None, :, None]) & (
        whole[:, 1][:, None, None] == jnp.arange(col_count)[None, None, :]
    )
    return jnp.einsum("irc,iab->rcab", chosen.astype(jnp.float32), blocks, precision=HIGHEST)


def block_terms(left, right, pairs):
    full_slab = jnp.einsum("rkab,kcbd->rcad", left, right, precision=HIGHEST)
    return full_slab[pairs[:, 0], pairs[:, 1]]


def per_device(s_blocks, s_list, x_blocks, x_list, c_list, owner):
    width = lax.axis_size("bcast")
    pairs = c_list[0, 0]
    resident = (x_blocks[0, 0], x_list[0, 0].astype(jnp.float32))
    current = resident
    total = jnp.zeros((pairs.shape[0], x_blocks.shape[3], x_blocks.shape[4]), jnp.float32)
    for step in range(STEPS):
        if step > 0:
            current = shifted((current[0], current[1]), "loop", -1)
        root = owner[0, step]
        slot = step // width
        left_blocks, left_places = (
            spread(s_blocks[0, 0, slot], "bcast", root),
            spread(s_list[0, 0, slot].astype(jnp.float32), "bcast", root),
        )
        left = densify(left_blocks, left_places, RB, KB)
        right = densify(current[0], current[1], KB, CB)
        total = total + block_terms(left, right, pairs)
    return total[None, None]


def solution(mesh):
    return jax.shard_map(
        per_device,
        mesh=mesh,
        in_specs=(
            P("loop", "bcast", None, None, None, None),
            P("loop", "bcast", None, None, None),
            P("loop", "bcast", None, None, None),
            P("loop", "bcast", None, None),
            P("loop", "bcast", None, None),
            P("loop", None),
        ),
        out_specs=P("loop", "bcast", None, None, None),
        check_vma=False,
    )
```

profile of v0, /device:TPU:0, one launch (start us, length us, event | category | flops | bytes accessed | tf_op | source)
XLA Modules:
  0.0 394.9 jit_solution(14435559528424766709)
XLA Ops:
  6.5 1.5 fusion.79
  10.5 6.8 %select_bitcast_fusion.2 = (f32[10,256,256]{2,1,0:T(8,128)}, f32[10,256,256]{2,1,0:T(8,128)}, f32[10,256,256]{2,1,0:T(8,128)}, f32[10,256,256]{2,1,0:T(8,128)}) fusion(f32[1,1,2,10,256,256]{5,4,3,2,1,0:T(8,128)} %param.6, pred[]{:T(512)S(6)} %eq.342, pred[]{:T(512)S(6)} %eq.372, pred[]{:T(512)S(6)} %eq.357, pred[]{:T(512)S(6)} %eq.327), kind=kLoop, calls=%fused_computation.39 | loop fusion | flops 2621440 | bytes 15728644 | tf_op jit(solution)/shard_map/jit(_where)/select_n | solution.py:21
  17.3 1.9 copy-done.4
  19.2 5.4 %collective-permute-start.1 = (f32[12,256,256]{2,1,0:T(8,128)S(1)}, f32[12,256,256]{2,1,0:T(8,128)}, u32[]{:S(2)}, u32[]{:S(2)}) collective-permute-start(f32[12,256,256]{2,1,0:T(8,128)S(1)} %bitcast.139), channel_id=1, source_target_pairs={{0,30},{2,0},{4,2},{6,4},{8,6},{10,8},{12,10},{14,12},{16,14},{18,... | collective-permute-start | bytes 9437192 | tf_op jit(solution)/shard_map/ppermute | solution.py:17
  24.6 0.7 collective-permute-start
  25.3 5.0 %all-reduce = (f32[10,2]{0,1:T(2,128)S(1)}, f32[10,2]{0,1:T(2,128)S(1)}, f32[10,2]{0,1:T(2,128)S(1)}, f32[10,2]{0,1:T(2,128)S(1)}) all-reduce(f32[10,2]{0,1:T(2,128)S(1)} %get-tuple-element.18, f32[10,2]{0,1:T(2,128)S(1)} %get-tuple-element.19, f32[10,2]{0,1:T(2,128)S(1)} %get-tuple-element.20, ...), channel_id=1, replica_groups=mesh['loop'=16,'bcast'=2] {'bcast'}, use_global_device_ids=true, to_apply=%region_6.7 | all-reduce | flops 80 | bytes 640 | tf_op jit(solution)/shard_map/psum | solution.py:22
  30.4 29.0 %collective-permute-done.1 = f32[12,256,256]{2,1,0:T(8,128)} collective-permute-done((f32[12,256,256]{2,1,0:T(8,128)S(1)}, f32[12,256,256]{2,1,0:T(8,128)}, u32[]{:S(2)}, u32[]{:S(2)}) %collective-permute-start.1) | collective-permute-done | bytes 3145760 | tf_op jit(solution)/shard_map/ppermute | solution.py:17
  59.4 4.7 %collective-permute-start.3 = (f32[12,256,256]{2,1,0:T(8,128)}, f32[12,256,256]{2,1,0:T(8,128)S(1)}, u32[]{:S(2)}, u32[]{:S(2)}) collective-permute-start(f32[12,256,256]{2,1,0:T(8,128)} %collective-permute-done.1), channel_id=1, source_target_pairs={{0,30},{2,0},{4,2},{6,4},{8,6},{10,8},{12,10},{14,12},{16,14},{18,... | collective-permute-start | bytes 9437192 | tf_op jit(solution)/shard_map/ppermute | solution.py:17
  64.1 0.1 iota_compare_fusion
  64.2 0.1 iota_compare_fusion.1
  64.3 0.1 iota_compare_fusion.4
  64.3 0.1 iota_compare_fusion.5
  64.4 0.1 iota_compare_fusion.8
  64.8 0.1 and_bitcast_fusion.4
  64.9 0.1 and_bitcast_fusion.5
  64.9 0.1 and_bitcast_fusion.6
  65.0 0.1 and_bitcast_fusion.3
  65.1 34.1 %collective-permute-done.3 = f32[12,256,256]{2,1,0:T(8,128)S(1)} collective-permute-done((f32[12,256,256]{2,1,0:T(8,128)}, f32[12,256,256]{2,1,0:T(8,128)S(1)}, u32[]{:S(2)}, u32[]{:S(2)}) %collective-permute-start.3) | collective-permute-done | bytes 3145760 | tf_op jit(solution)/shard_map/ppermute | solution.py:17
  99.2 4.5 %collective-permute-start.5 = (f32[12,256,256]{2,1,0:T(8,128)S(1)}, f32[12,256,256]{2,1,0:T(8,128)S(1)}, u32[]{:S(2)}, u32[]{:S(2)}) collective-permute-start(f32[12,256,256]{2,1,0:T(8,128)S(1)} %collective-permute-done.3), channel_id=1, source_target_pairs={{0,30},{2,0},{4,2},{6,4},{8,6},{10,8},{12,10},{14,12},{16,14},{18,... | collective-permute-start | bytes 9437192 | tf_op jit(solution)/shard_map/ppermute | solution.py:17
  103.7 0.1 and_bitcast_fusion.7
  103.8 6.2 %fusion.32 = f32[4,4,256,256,1]{3,1,2,0,4:T(4,128)} fusion(f32[12,256,256,1]{2,1,0,3:T(8,128)S(1)} %bitcast.140, pred[12,4,4,1]{2,1,0,3:T(4,128)(4,1)S(1)} %and_bitcast_fusion.3), kind=kOutput, calls=%fused_computation.41 | convolution fusion | flops 150994944 | bytes 7340224 | tf_op jit(solution)/shard_map/irc,iab->rcab/dot_general | solution.py:30
  110.1 0.1 iota_compare_fusion.10
  110.2 0.1 and_bitcast_fusion.2
  110.3 28.3 %collective-permute-done.2 = f32[12,2]{0,1:T(2,128)S(1)} collective-permute-done((f32[12,2]{0,1:T(2,128)S(1)}, f32[12,2]{0,1:T(2,128)S(1)}, u32[]{:S(2)}, u32[]{:S(2)}) %collective-permute-start.2) | collective-permute-done | bytes 128 | tf_op jit(solution)/shard_map/ppermute | solution.py:17
  138.5 4.8 %collective-permute-start.4 = (f32[12,2]{0,1:T(2,128)S(1)}, f32[12,2]{0,1:T(2,128)S(1)}, u32[]{:S(2)}, u32[]{:S(2)}) collective-permute-start(f32[12,2]{0,1:T(2,128)S(1)} %collective-permute-done.2), channel_id=1, source_target_pairs={{0,30},{2,0},{4,2},{6,4},{8,6},{10,8},{12,10},{14,12},{16,14},{18,... | collective-permute-start | bytes 296 | tf_op jit(solution)/shard_map/ppermute | solution.py:17
  143.3 0.1 iota_compare_fusion.6
  143.4 0.1 and_bitcast_fusion.1
  143.5 1.1 collective-permute-done.4
  144.6 0.1 iota_compare_fusion.2
  144.7 0.1 and_bitcast_fusion
  144.8 8.3 %fusion.35 = f32[4,4,256,256,1]{3,1,2,0,4:T(4,128)} fusion(f32[12,256,256,1]{2,1,0,3:T(8,128)} %bitcast.23, pred[12,4,4,1]{2,1,0,3:T(4,128)(4,1)S(1)} %and_bitcast_fusion.2), kind=kOutput, calls=%fused_computation.42 | convolution fusion | flops 150994944 | bytes 7340224 | tf_op jit(solution)/shard_map/irc,iab->rcab/dot_general | solution.py:30
  153.1 6.2 %fusion.38 = f32[4,4,256,256,1]{3,1,2,0,4:T(4,128)} fusion(f32[12,256,256,1]{2,1,0,3:T(8,128)S(1)} %bitcast.141, pred[12,4,4,1]{2,1,0,3:T(4,128)(4,1)S(1)} %and_bitcast_fusion.1), kind=kOutput, calls=%fused_computation.43 | convolution fusion | flops 150994944 | bytes 7340224 | tf_op jit(solution)/shard_map/irc,iab->rcab/dot_general | solution.py:30
  159.3 6.1 %fusion.41 = f32[4,4,256,256,1]{3,1,2,0,4:T(4,128)} fusion(f32[12,256,256,1]{2,1,0,3:T(8,128)S(1)} %bitcast.142, pred[12,4,4,1]{2,1,0,3:T(4,128)(4,1)S(1)} %and_bitcast_fusion), kind=kOutput, calls=%fused_computation.44 | convolution fusion | flops 150994944 | bytes 7340224 | tf_op jit(solution)/shard_map/irc,iab->rcab/dot_general | solution.py:30
  165.4 99.5 %all-reduce.4.cloned.1.call-done = (f32[10,256,256]{2,1,0:T(8,128)}, f32[10,256,256]{2,1,0:T(8,128)}, f32[10,256,256]{2,1,0:T(8,128)}, f32[10,256,256]{2,1,0:T(8,128)}) async-done(((f32[10,256,256]{2,1,0:T(8,128)}, f32[10,256,256]{2,1,0:T(8,128)}, f32[10,256,256]{2,1,0:T(8,128)}, f32[10,256,256]{2,1,0:T(8,128)}), (f32[10,256,256]{2,1,0:T(8,128)}, f32[10,256,256]{2,1,0:T(8,128)}, f32[10,256,256]{2,1,0:T(8,128)}, ...) | async-done | bytes 10485776 | tf_op jit(solution)/shard_map/psum | solution.py:22
  265.0 6.3 %fusion.8 = f32[3,4,256,256]{3,1,2,0:T(4,128)S(1)} fusion(f32[10,256,256,1]{2,1,0,3:T(8,128)} %bitcast.138, pred[10,3,4,1]{2,1,0,3:T(4,128)(4,1)S(1)} %and_bitcast_fusion.4), kind=kOutput, calls=%fused_computation.12 | convolution fusion | flops 94371840 | bytes 5767288 | tf_op jit(solution)/shard_map/irc,iab->rcab/dot_general | solution.py:30
  271.3 20.4 %fusion.59 = f32[3,4,256,256]{2,3,0,1:T(8,128)S(1)} fusion(f32[3,4,256,256]{3,1,2,0:T(4,128)S(1)} %fusion.8, f32[4,4,256,256,1]{3,1,2,0,4:T(4,128)S(1)} %copy-done.3), kind=kOutput, calls=%fused_computation.48 | convolution fusion | flops 9663676416 | bytes 10485760 | tf_op jit(solution)/shard_map/rkab,kcbd->rcad/dot_general | solution.py:34
  291.7 2.3 gather_fusion.3
  294.0 6.2 %fusion.12 = f32[3,4,256,256]{3,1,2,0:T(4,128)S(1)} fusion(f32[10,256,256,1]{2,1,0,3:T(8,128)} %bitcast.137, pred[10,3,4,1]{2,1,0,3:T(4,128)(4,1)S(1)} %and_bitcast_fusion.5), kind=kOutput, calls=%fused_computation.16 | convolution fusion | flops 94371840 | bytes 5767288 | tf_op jit(solution)/shard_map/irc,iab->rcab/dot_general | solution.py:30
  300.3 20.2 %fusion.54 = f32[3,4,256,256]{2,3,0,1:T(8,128)S(1)} fusion(f32[3,4,256,256]{3,1,2,0:T(4,128)S(1)} %fusion.12, f32[4,4,256,256,1]{3,1,2,0,4:T(4,128)S(1)} %copy-done.2), kind=kOutput, calls=%fused_computation.47 | convolution fusion | flops 9663676416 | bytes 10485760 | tf_op jit(solution)/shard_map/rkab,kcbd->rcad/dot_general | solution.py:34
  320.5 2.4 gather_fusion.2
  322.9 6.5 %fusion.16 = f32[3,4,256,256]{3,1,2,0:T(4,128)S(1)} fusion(f32[10,256,256,1]{2,1,0,3:T(8,128)} %bitcast.136, pred[10,3,4,1]{2,1,0,3:T(4,128)(4,1)S(1)} %and_bitcast_fusion.6), kind=kOutput, calls=%fused_computation.20 | convolution fusion | flops 94371840 | bytes 5767288 | tf_op jit(solution)/shard_map/irc,iab->rcab/dot_general | solution.py:30
  329.4 20.2 %fusion.49 = f32[3,4,256,256]{2,3,0,1:T(8,128)S(1)} fusion(f32[3,4,256,256]{3,1,2,0:T(4,128)S(1)} %fusion.16, f32[4,4,256,256,1]{3,1,2,0,4:T(4,128)S(1)} %copy-done.1), kind=kOutput, calls=%fused_computation.46 | convolution fusion | flops 9663676416 | bytes 10485760 | tf_op jit(solution)/shard_map/rkab,kcbd->rcad/dot_general | solution.py:34
  349.6 2.3 gather_fusion.1
  351.9 6.3 %fusion.20 = f32[3,4,256,256]{3,1,2,0:T(4,128)S(1)} fusion(f32[10,256,256,1]{2,1,0,3:T(8,128)} %bitcast.135, pred[10,3,4,1]{2,1,0,3:T(4,128)(4,1)S(1)} %and_bitcast_fusion.7), kind=kOutput, calls=%fused_computation.24 | convolution fusion | flops 94371840 | bytes 5767288 | tf_op jit(solution)/shard_map/irc,iab->rcab/dot_general | solution.py:30
  358.2 20.3 %fusion.44 = f32[3,4,256,256]{2,3,0,1:T(8,128)S(1)} fusion(f32[3,4,256,256]{3,1,2,0:T(4,128)S(1)} %fusion.20, f32[4,4,256,256,1]{3,1,2,0,4:T(4,128)S(1)} %copy-done), kind=kOutput, calls=%fused_computation.45 | convolution fusion | flops 9663676416 | bytes 10485760 | tf_op jit(solution)/shard_map/rkab,kcbd->rcad/dot_general | solution.py:34
  378.5 2.3 gather_fusion
  380.8 4.9 %add_bitcast_fusion = f32[1,1,10,256,256]{3,4,2,1,0:T(8,128)S(1)} fusion(f32[10,256,256]{1,2,0:T(8,128)} %gather_fusion.3, f32[10,256,256]{1,2,0:T(8,128)} %gather_fusion.2, f32[10,256,256]{1,2,0:T(8,128)} %gather_fusion, f32[10,256,256]{1,2,0:T(8,128)} %gather_fusion.1), kind=kLoop, calls=%fused_computation.36 | loop fusion | flops 1966080 | bytes 13107200 | tf_op jit(solution)/shard_map/add | solution.py:55
  385.7 2.1 copy.7
  (42 shorter events, 0.5 us)
Async XLA Ops:
  6.5 258.4 %all-reduce.4.cloned.1.call-start = ((), (), s32[]{:S(2)}) async-start(), calls=%async_computation | async-start | bytes 20971520 | tf_op jit(solution)/shard_map/psum | solution.py:22
  17.3 1.9 copy-start.4
  17.3 7.3 %copy-start.6 = (s32[1,1,12,2]{2,3,1,0:T(2,128)S(1)}, s32[1,1,12,2]{2,3,1,0:T(2,128)}, u32[]{:S(2)}) copy-start(s32[1,1,12,2]{2,3,1,0:T(2,128)} %param.9) | copy-start | bytes 292
  17.3 8.0 %copy-start.5 = (s32[1,1,2,10,2]{3,4,2,1,0:T(2,128)S(1)}, s32[1,1,2,10,2]{3,4,2,1,0:T(2,128)}, u32[]{:S(2)}) copy-start(s32[1,1,2,10,2]{3,4,2,1,0:T(2,128)} %param.7) | copy-start | bytes 484
  19.2 40.2 %collective-permute-start.1 = (f32[12,256,256]{2,1,0:T(8,128)S(1)}, f32[12,256,256]{2,1,0:T(8,128)}, u32[]{:S(2)}, u32[]{:S(2)}) collective-permute-start(f32[12,256,256]{2,1,0:T(8,128)S(1)} %bitcast.139), channel_id=1, source_target_pairs={{0,30},{2,0},{4,2},{6,4},{8,6},{10,8},{12,10},{14,12},{16,14},{18,... | collective-permute-start | bytes 9437192 | tf_op jit(solution)/shard_map/ppermute | solution.py:17
  24.6 85.4 %collective-permute-start = (f32[12,2]{0,1:T(2,128)S(1)}, f32[12,2]{0,1:T(2,128)S(1)}, u32[]{:S(2)}, u32[]{:S(2)}) collective-permute-start(f32[12,2]{0,1:T(2,128)S(1)} %get-tuple-element.28), channel_id=1, source_target_pairs={{0,30},{2,0},{4,2},{6,4},{8,6},{10,8},{12,10},{14,12},{16,14},{18,... | collective-permute-start | bytes 296 | tf_op jit(solution)/shard_map/ppermute | solution.py:17
  59.4 39.8 %collective-permute-start.3 = (f32[12,256,256]{2,1,0:T(8,128)}, f32[12,256,256]{2,1,0:T(8,128)S(1)}, u32[]{:S(2)}, u32[]{:S(2)}) collective-permute-start(f32[12,256,256]{2,1,0:T(8,128)} %collective-permute-done.1), channel_id=1, source_target_pairs={{0,30},{2,0},{4,2},{6,4},{8,6},{10,8},{12,10},{14,12},{16,14},{18,... | collective-permute-start | bytes 9437192 | tf_op jit(solution)/shard_map/ppermute | solution.py:17
  99.2 60.1 %collective-permute-start.5 = (f32[12,256,256]{2,1,0:T(8,128)S(1)}, f32[12,256,256]{2,1,0:T(8,128)S(1)}, u32[]{:S(2)}, u32[]{:S(2)}) collective-permute-start(f32[12,256,256]{2,1,0:T(8,128)S(1)} %collective-permute-done.3), channel_id=1, source_target_pairs={{0,30},{2,0},{4,2},{6,4},{8,6},{10,8},{12,10},{14,12},{16,14},{18,... | collective-permute-start | bytes 9437192 | tf_op jit(solution)/shard_map/ppermute | solution.py:17
  103.8 6.2 %copy-start.7 = (s32[1,1,10,2]{2,3,1,0:T(2,128)S(1)}, s32[1,1,10,2]{2,3,1,0:T(2,128)}, u32[]{:S(2)}) copy-start(s32[1,1,10,2]{2,3,1,0:T(2,128)} %param.10) | copy-start | bytes 244
  110.0 28.5 %collective-permute-start.2 = (f32[12,2]{0,1:T(2,128)S(1)}, f32[12,2]{0,1:T(2,128)S(1)}, u32[]{:S(2)}, u32[]{:S(2)}) collective-permute-start(f32[12,2]{0,1:T(2,128)S(1)} %collective-permute-done), channel_id=1, source_target_pairs={{0,30},{2,0},{4,2},{6,4},{8,6},{10,8},{12,10},{14,12},{16,14},{18,... | collective-permute-start | bytes 296 | tf_op jit(solution)/shard_map/ppermute | solution.py:17
  138.5 6.1 %collective-permute-start.4 = (f32[12,2]{0,1:T(2,128)S(1)}, f32[12,2]{0,1:T(2,128)S(1)}, u32[]{:S(2)}, u32[]{:S(2)}) collective-permute-start(f32[12,2]{0,1:T(2,128)S(1)} %collective-permute-done.2), channel_id=1, source_target_pairs={{0,30},{2,0},{4,2},{6,4},{8,6},{10,8},{12,10},{14,12},{16,14},{18,... | collective-permute-start | bytes 296 | tf_op jit(solution)/shard_map/ppermute | solution.py:17
  265.0 6.3 %copy-start.3 = (f32[4,4,256,256,1]{3,1,2,0,4:T(4,128)S(1)}, f32[4,4,256,256,1]{3,1,2,0,4:T(4,128)}, u32[]{:S(2)}) copy-start(f32[4,4,256,256,1]{3,1,2,0,4:T(4,128)} %fusion.41) | copy-start | bytes 12582916
  294.0 6.3 %copy-start.2 = (f32[4,4,256,256,1]{3,1,2,0,4:T(4,128)S(1)}, f32[4,4,256,256,1]{3,1,2,0,4:T(4,128)}, u32[]{:S(2)}) copy-start(f32[4,4,256,256,1]{3,1,2,0,4:T(4,128)} %fusion.38) | copy-start | bytes 12582916
  322.9 6.5 %copy-start.1 = (f32[4,4,256,256,1]{3,1,2,0,4:T(4,128)S(1)}, f32[4,4,256,256,1]{3,1,2,0,4:T(4,128)}, u32[]{:S(2)}) copy-start(f32[4,4,256,256,1]{3,1,2,0,4:T(4,128)} %fusion.35) | copy-start | bytes 12582916
  351.9 6.3 %copy-start = (f32[4,4,256,256,1]{3,1,2,0,4:T(4,128)S(1)}, f32[4,4,256,256,1]{3,1,2,0,4:T(4,128)}, u32[]{:S(2)}) copy-start(f32[4,4,256,256,1]{3,1,2,0,4:T(4,128)} %fusion.32) | copy-start | bytes 12582916
Sparse Core Ops, SparseCore 0:
  17.4 247.4 all-reduce.3
where the time goes:
time: 399 us; the launch traced here: 395 us
  waiting for transfers between devices  192 us (48%)
  matrix products  133 us (33%)
  starting transfers between devices  20.1 us (5%)
  between operations  16.4 us (4%)
  local copies, waits for them, and re-layouts  14.9 us (4%)
  other arithmetic  13.2 us (3%)
  blocking collectives  5 us (1%)
    psum x1, waiting for transfers between devices, spread(): return lax.psum(block, axis)  99.5 us
    ppermute x6, waiting for transfers between devices, shifted(): lax.ppermute(shard, axis, [(i, (i + by) % length) for i in range(length)])  92.5 us
    dot_general x4, matrix products, block_terms(): full_slab = jnp.einsum('rkab,kcbd->rcad', left, right, precision=HIGHEST)  81 us
    dot_general x8, matrix products, densify(): jnp.einsum('irc,iab->rcab', chosen.astype(jnp.float32), blocks, precision...  52.2 us
    ppermute x6, starting transfers between devices, shifted(): lax.ppermute(shard, axis, [(i, (i + by) % length) for i in range(length)])  20.1 us
    gather x4, local copies, waits for them, and re-layouts, block_terms(): return full_slab[pairs[:, 0], pairs[:, 1]]  9.38 us
  transfers between devices with their start and end apart: 7, of which 5 were waited for; matrix products, arithmetic and copies ran while one was open for 7% of the time, Pallas kernels for 0%

commit v1 on v0

v1 whole, which is shorter than its diff:
```python
import functools

import jax
import jax.numpy as jnp
from jax import lax
from jax.experimental import pallas as pl
from jax.experimental.pallas import tpu as pltpu
from jax.sharding import PartitionSpec as P

RB = 3
KB = 4
CB = 4
STEPS = 4

X_AT = 0
OWN_FLAG_AT = X_AT + STEPS * KB * CB
GROUP_STEP_AT = OWN_FLAG_AT + STEPS
OUT_AT = GROUP_STEP_AT + STEPS


def positions(places, row_count, col_count):
    cells = jnp.arange(row_count * col_count)
    rows, cols = cells // col_count, cells % col_count
    there = (places[..., None, :, 0] == rows[:, None]) & (places[..., None, :, 1] == cols[:, None])
    return jnp.max(jnp.where(there, jnp.arange(places.shape[-2]), -1), axis=-1)


def halves(values):
    high = values.astype(jnp.bfloat16)
    return high, (values - high.astype(jnp.float32)).astype(jnp.bfloat16)


def dot(left, right):
    return jnp.dot(left, right, preferred_element_type=jnp.float32)


def product_terms(left_blocks, right_high, right_low):
    left_high, left_low = halves(jnp.concatenate(left_blocks, axis=0))
    return dot(left_high, right_high) + dot(left_high, right_low) + dot(left_low, right_high)


def group_kernel(group, own_at, first, n_own, meta, *refs):
    refs = list(refs)
    x_refs = [refs.pop(0) for _ in range(CB)]
    s_refs = [refs.pop(0) for _ in range(RB if n_own else 0)]
    if not first:
        acc_in = refs.pop(0)
        refs.pop(0)
    acc_ref, r_ref = refs
    k = pl.program_id(0)
    step = meta[GROUP_STEP_AT + group]

    @pl.when(k == 0)
    def _():
        acc_ref[...] = jnp.zeros_like(acc_ref) if first else acc_in[...]

    bs = x_refs[0].shape[-1]
    for c in range(CB):
        there = meta[X_AT + (step * KB + k) * CB + c] >= 0
        high, low = halves(jnp.where(there, x_refs[c][0], 0.0))
        r_ref[0, 0, :, c * bs : (c + 1) * bs] = high
        r_ref[0, 1, :, c * bs : (c + 1) * bs] = low

    if n_own:

        @pl.when(meta[OWN_FLAG_AT + step] > 0)
        def _():
            blocks = []
            for r in range(RB):
                there = meta[own_at + (step // 2) * RB * KB + r * KB + k] >= 0
                blocks.append(jnp.where(there, s_refs[r][0, 0], 0.0))
            terms = product_terms(blocks, r_ref[0, 0], r_ref[0, 1])
            acc_ref[...] += terms.reshape(acc_ref.shape)


def take_group(group, own_at, meta, x, s_own, carried):
    slots, bs = x.shape[0], x.shape[-1]
    first = carried is None
    n_own = 0 if s_own is None else s_own.shape[0]

    def x_index(c):
        def at(k, meta):
            return (jnp.maximum(meta[X_AT + (meta[GROUP_STEP_AT + group] * KB + k) * CB + c], 0), 0, 0)

        return at

    def s_index(r):
        def at(k, meta):
            slot = meta[GROUP_STEP_AT + group] // 2
            return (slot, jnp.maximum(meta[own_at + slot * RB * KB + r * KB + k], 0), 0, 0)

        return at

    acc_spec = pl.BlockSpec((RB, bs, CB * bs), lambda k, meta: (0, 0, 0))
    r_spec = pl.BlockSpec((1, 2, bs, CB * bs), lambda k, meta: (meta[GROUP_STEP_AT + group], 0, k, 0))
    in_specs = [pl.BlockSpec((1, bs, bs), x_index(c)) for c in range(CB)]
    operands = [x] * CB
    if n_own:
        in_specs += [pl.BlockSpec((1, 1, bs, bs), s_index(r)) for r in range(RB)]
        operands += [s_own] * RB
    aliases = {}
    if not first:
        aliases = {1 + len(operands): 0, 2 + len(operands): 1}
        in_specs += [acc_spec, pl.BlockSpec(memory_space=pl.ANY)]
        operands += list(carried)
    return pl.pallas_call(
        functools.partial(group_kernel, group, own_at, first, n_own),
        grid_spec=pltpu.PrefetchScalarGridSpec(
            num_scalar_prefetch=1, grid=(KB,), in_specs=in_specs, out_specs=[acc_spec, r_spec]
        ),
        out_shape=[
            jax.ShapeDtypeStruct((RB, bs, CB * bs), jnp.float32),
            jax.ShapeDtypeStruct((STEPS, 2, KB * bs, CB * bs), jnp.bfloat16),
        ],
        input_output_aliases=aliases,
        compiler_params=pltpu.CompilerParams(vmem_limit_bytes=32 * 2**20),
        cost_estimate=pl.CostEstimate(flops=3 * 2 * RB * KB * CB * bs**3, bytes_accessed=16 * 2**20, transcendentals=0),
        name="take_group",
    )(meta, *operands)


def finish_kernel(piece_at, step_at, n_out, meta, *refs):
    s_refs, (acc_in, r_ref, out_ref, acc_ref) = refs[:RB], refs[RB:]
    j, k = pl.program_id(0), pl.program_id(1)

    @pl.when((j == 0) & (k == 0))
    def _():
        acc_ref[...] = acc_in[...]

    blocks = []
    for r in range(RB):
        there = meta[piece_at + j * RB * KB + r * KB + k] >= 0
        blocks.append(jnp.where(there, s_refs[r][0, 0], 0.0))
    terms = product_terms(blocks, r_ref[0, 0], r_ref[0, 1])
    acc_ref[...] += terms.reshape(acc_ref.shape)
    bs = out_ref.shape[-1]

    @pl.when((j == pl.num_programs(0) - 1) & (k == pl.num_programs(1) - 1))
    def _():
        for m in range(n_out):
            row = meta[OUT_AT + 2 * m]
            col = pl.multiple_of(meta[OUT_AT + 2 * m + 1] * bs, bs)
            out_ref[m] = acc_ref[row, :, pl.ds(col, bs)]


def finish(piece_at, step_at, meta, pieces, acc, right, n_out):
    n_pieces, bs = pieces.shape[0], pieces.shape[-1]

    def s_index(r):
        def at(j, k, meta):
            return (j, jnp.maximum(meta[piece_at + j * RB * KB + r * KB + k], 0), 0, 0)

        return at

    return pl.pallas_call(
        functools.partial(finish_kernel, piece_at, step_at, n_out),
        grid_spec=pltpu.PrefetchScalarGridSpec(
            num_scalar_prefetch=1,
            grid=(n_pieces, KB),
            in_specs=[pl.BlockSpec((1, 1, bs, bs), s_index(r)) for r in range(RB)]
            + [
                pl.BlockSpec((RB, bs, CB * bs), lambda j, k, meta: (0, 0, 0)),
                pl.BlockSpec((1, 2, bs, CB * bs), lambda j, k, meta: (meta[step_at + j], 0, k, 0)),
            ],
            out_specs=pl.BlockSpec((n_out, bs, bs), lambda j, k, meta: (0, 0, 0)),
            scratch_shapes=[pltpu.VMEM((RB, bs, CB * bs), jnp.float32)],
        ),
        out_shape=jax.ShapeDtypeStruct((n_out, bs, bs), jnp.float32),
        compiler_params=pltpu.CompilerParams(vmem_limit_bytes=40 * 2**20),
        cost_estimate=pl.CostEstimate(
            flops=3 * 2 * n_pieces * RB * KB * CB * bs**3, bytes_accessed=18 * 2**20, transcendentals=0
        ),
        name="finish",
    )(meta, *([pieces] * RB), acc, right)


def per_device(s_blocks, s_list, x_blocks, x_list, c_list, owner):
    length, width = lax.axis_size("loop"), lax.axis_size("bcast")
    line, column = lax.axis_index("loop"), lax.axis_index("bcast")
    s_own, x_own, pairs, owner = s_blocks[0, 0], x_blocks[0, 0], c_list[0, 0], owner[0]
    depth, n_s, bs = s_own.shape[0], s_own.shape[1], s_own.shape[-1]
    n_x, n_out = x_own.shape[0], pairs.shape[0]

    swapped = width == 2
    if swapped:
        pieces = lax.ppermute(s_own, "bcast", [(0, 1), (1, 0)])
    else:
        held = lax.all_gather(s_own, "bcast")
        pieces = jnp.stack([held[owner[s], s // width] for s in range(STEPS)])

    near = [(g, (g - 1) % length if g % 2 == 0 else (g - 3) % length) for g in range(length)]
    far = [(g, (g - 3) % length if g % 2 == 0 else (g - 1) % length) for g in range(length)]
    groups = [x_own, lax.ppermute(x_own, "loop", near), lax.ppermute(x_own, "loop", far)]
    groups.append(lax.ppermute(groups[1], "loop", [(g, g ^ 1) for g in range(length)]))
    odd = line % 2
    group_step = jnp.stack([0 * odd, 3 - 2 * odd, 1 + 2 * odd, 0 * odd + 2])

    lists = jnp.concatenate([x_list.reshape(-1), s_list.reshape(-1)])
    lists = lax.all_gather(lists, ("loop", "bcast")).reshape(length, width, -1)
    mine = jnp.take(lists, (line + jnp.arange(STEPS)) % length, axis=0)
    x_places = jnp.take(mine, column, axis=1)[:, : 2 * n_x].reshape(STEPS, n_x, 2)
    s_places = mine[0, :, 2 * n_x :].reshape(width, depth, n_s, 2)
    steps = jnp.arange(STEPS)
    if swapped:
        own_flag = (owner == column).astype(jnp.int32)
        starts = width * jnp.arange(depth)
        piece_steps = starts + own_flag[::width]
        tables = [positions(s_places[column], RB, KB), positions(s_places[1 - column], RB, KB)]
    else:
        own_flag = jnp.zeros_like(steps)
        piece_steps = steps
        tables = [jnp.zeros((0,), jnp.int32), positions(s_places[owner, steps // width], RB, KB)]
    own_at = OUT_AT + 2 * n_out
    piece_at = own_at + tables[0].size
    step_at = piece_at + tables[1].size
    meta = jnp.concatenate(
        [
            part.reshape(-1).astype(jnp.int32)
            for part in (positions(x_places, KB, CB), own_flag, group_step, pairs, *tables, piece_steps)
        ]
    )

    carried = None
    for group in (0, 1, 3, 2):
        carried = take_group(group, own_at, meta, groups[group], s_own if swapped else None, carried)
    out = finish(piece_at, step_at, meta, pieces, *carried, n_out)
    return out[None, None]


def solution(mesh):
    return jax.shard_map(
        per_device,
        mesh=mesh,
        in_specs=(
            P("loop", "bcast", None, None, None, None),
            P("loop", "bcast", None, None, None),
            P("loop", "bcast", None, None, None),
            P("loop", "bcast", None, None),
            P("loop", "bcast", None, None),
            P("loop", None),
        ),
        out_specs=P("loop", "bcast", None, None, None),
        check_vma=False,
    )
```

time: 399 us -> 207 us (0.52)
  waiting for transfers between devices: 192 us -> 0.01 us
  blocking collectives: 5 us -> 144 us
  matrix products: 133 us -> 0 us
  Pallas kernels: 0 us -> 43.7 us
  between operations: 16.4 us -> 0.1 us
  starting transfers between devices: 20.1 us -> 7.46 us
  other arithmetic: 13.2 us -> 1.2 us
  local copies, waits for them, and re-layouts: 14.9 us -> 9.5 us
    unnamed x0 -> x1, blocking collectives: none -> 144 us
    dot_general x12 -> x0, matrix products: 133 us -> none  [the longest x4 81 us: block_terms(): full_slab = jnp.einsum('rkab,kcbd->rcad', left, right, precision=HIGHEST)]
    psum x1 -> x0, waiting for transfers between devices: 99.5 us -> none  [spread(): return lax.psum(block, axis)]
    ppermute x6 -> x4, waiting for transfers between devices: 92.5 us -> 0.01 us  [the longest x1 0.01 us: per_device(): lax.ppermute(x_own, 'loop', near)]
    pallas_call x0 -> x5, Pallas kernels: none -> 43.7 us  [the longest x4 27.9 us: take_group(): pl.pallas_call(functools.partial(group_kernel, group, own_at, first, n_ow...]
    ppermute x6 -> x4, starting transfers between devices: 20.1 us -> 7.46 us  [the longest x1 5.42 us: per_device(): lax.ppermute(x_own, 'loop', near)]
    gather x4 -> x1, local copies, waits for them, and re-layouts: 9.38 us -> 0.57 us  [per_device(): mine = jnp.take(lists, (line + jnp.arange(STEPS)) % length, axis=0)]
    select_n x2 -> x5, other arithmetic: 6.76 us -> 0.1 us  [the longest x2 0.09 us: per_device(): mine = jnp.take(lists, (line + jnp.arange(STEPS)) % length, axis=0)]
  transfers between devices with their start and end apart: 7 -> 4, of which waited for: 5 -> 0; matrix products, arithmetic and copies ran while one was open for 7% -> 3% of each run, Pallas kernels for 0% -> 14%
where the time goes in v1:
time: 207 us; the launch traced here: 206 us
  blocking collectives  144 us (70%)
  Pallas kernels  43.7 us (21%)
  local copies, waits for them, and re-layouts  9.5 us (5%)
  starting transfers between devices  7.46 us (4%)
    unnamed x1, blocking collectives  144 us
    pallas_call x4, Pallas kernels, take_group(): pl.pallas_call(functools.partial(group_kernel, group, own_at, first, n_ow...  27.9 us
    pallas_call x1, Pallas kernels, finish(): pl.pallas_call(functools.partial(finish_kernel, piece_at, step_at, n_out)...  15.8 us
    unnamed x10, local copies, waits for them, and re-layouts  6.94 us
    ppermute x1, starting transfers between devices, per_device(): lax.ppermute(x_own, 'loop', near)  5.42 us
  transfers between devices with their start and end apart: 4, of which 0 were waited for; matrix products, arithmetic and copies ran while one was open for 3% of the time, Pallas kernels for 14%

profile of v1, /device:TPU:0, one launch (start us, length us, event | category | flops | bytes accessed | tf_op | source)
XLA Modules:
  0.0 206.4 jit_solution(17929201484565107315)
XLA Ops:
  0.0 5.4 %collective-permute-start.2 = (f32[12,256,256]{2,1,0:T(8,128)}, f32[12,256,256]{2,1,0:T(8,128)}, u32[]{:S(2)}, u32[]{:S(2)}) collective-permute-start(f32[12,256,256]{2,1,0:T(8,128)} %bitcast.33), channel_id=1, source_target_pairs={{0,30},{2,28},{4,2},{6,0},{8,6},{10,4},{12,10},{14,8},{16,14},{18,... | collective-permute-start | bytes 9437192 | tf_op jit(solution)/shard_map/ppermute | solution.py:193
  5.4 1.5 collective-permute-start
  6.9 0.5 collective-permute-start.1
  7.4 0.8 copy.30
  8.2 0.1 reshape.131
  8.3 0.8 copy.29
  9.0 0.1 reshape.130
  9.1 0.2 add_dynamic-update-slice_fusion
  9.3 144.4 %all-reduce = s32[2048]{0:T(1024)S(1)} all-reduce(s32[2048]{0:T(1024)S(1)} %add_dynamic-update-slice_fusion), channel_id=2, replica_groups=mesh['loop'=16,'bcast'=2] {'loop','bcast'}, use_global_device_ids=true, to_apply=%add | all-reduce | flops 2048 | bytes 16384
  153.8 0.1 reshape.132
  153.8 0.0 collective-permute-done.2.refs_0_.refs_1_.refs_2_.refs_3_
  153.9 0.1 collective-permute-start.3
  153.9 0.6 gather_fusion
  154.5 0.1 broadcast_select_fusion
  154.6 0.1 slice.49
  154.7 0.1 reshape_squeeze.7
  154.8 0.1 copy.37
  154.9 0.1 copy.38
  155.0 0.1 copy.39
  155.1 0.1 copy.40
  155.2 0.1 copy.41
  155.3 0.1 copy.42
  155.4 0.1 fusion
  155.5 0.1 reshape.135
  155.6 0.1 reshape.136
  155.7 0.1 copy.31
  155.8 0.1 copy.32
  155.9 0.1 copy.33
  156.0 0.1 copy.34
  156.1 0.1 copy.35
  156.2 0.1 select_reduce_fusion
  156.3 0.1 reshape.134
  156.4 0.7 fusion.2
  157.0 0.1 slice.35
  157.1 0.8 copy.36
  157.9 0.1 reshape_squeeze.6
  158.0 0.1 concatenate.7.meta
  158.1 0.0 copy-start
  158.1 2.5 %copy-done = f32[1,1,2,10,256,256]{5,4,3,2,1,0:T(8,128)S(1)} copy-done((f32[1,1,2,10,256,256]{5,4,3,2,1,0:T(8,128)S(1)}, f32[1,1,2,10,256,256]{5,4,3,2,1,0:T(8,128)}, u32[]{:S(2)}) %copy-start) | copy-done | bytes 5242904
  160.6 1.9 copy-done.2
  162.5 3.5 %take_group.4 = (f32[3,256,1024]{2,1,0:T(8,128)S(1)}, bf16[4,2,1024,1024]{3,2,1,0:T(8,128)(2,1)}) custom-call(s32[142]{0:T(256)S(1)} %concatenate.7.meta, f32[12,256,256]{2,1,0:T(8,128)S(1)} %bitcast.35, f32[12,256,256]{2,1,0:T(8,128)S(1)} %bitcast.36, f32[12,256,256]{2,1,0:T(8,128)S(1)} %bitcast.37, f32[12,256,256]{2,1,0:T(8,128)S(1)} %bitcast.38, ...), custom_call_target="tpu_custom_call" | custom-call | flops 4831838208 | bytes 16777216 | tf_op jit(solution)/shard_map/take_group/pallas_call | solution.py:106
  165.9 0.2 copy-done.1
  166.1 10.0 %take_group.5 = (f32[3,256,1024]{2,1,0:T(8,128)S(1)}, bf16[4,2,1024,1024]{3,2,1,0:T(8,128)(2,1)}) custom-call(s32[142]{0:T(256)S(1)} %concatenate.7.meta, f32[12,256,256]{2,1,0:T(8,128)} %collective-permute-done.2.refs_0_.refs_1_.refs_2_.refs_3_, ...), custom_call_target="tpu_custom_call", output_to_operand_aliasing={{0}: (8, {}), {1}: (9, {})} | custom-call | flops 4831838208 | bytes 16777216 | tf_op jit(solution)/shard_map/take_group/pallas_call | solution.py:106
  176.2 0.0 collective-permute-done.3.refs_0_.refs_1_.refs_2_.refs_3_
  176.2 5.6 %take_group.6 = (f32[3,256,1024]{2,1,0:T(8,128)S(1)}, bf16[4,2,1024,1024]{3,2,1,0:T(8,128)(2,1)}) custom-call(s32[142]{0:T(256)S(1)} %concatenate.7.meta, f32[12,256,256]{2,1,0:T(8,128)} %collective-permute-done.3.refs_0_.refs_1_.refs_2_.refs_3_, ...), custom_call_target="tpu_custom_call", output_to_operand_aliasing={{0}: (8, {}), {1}: (9, {})} | custom-call | flops 4831838208 | bytes 16777216 | tf_op jit(solution)/shard_map/take_group/pallas_call | solution.py:106
  181.8 8.8 %take_group.7 = (f32[3,256,1024]{2,1,0:T(8,128)S(1)}, bf16[4,2,1024,1024]{3,2,1,0:T(8,128)(2,1)}) custom-call(s32[142]{0:T(256)S(1)} %concatenate.7.meta, f32[12,256,256]{2,1,0:T(8,128)S(1)} %collective-permute-done.1.refs_0_.refs_1_.refs_2_.refs_3_, ...), custom_call_target="tpu_custom_call", output_to_operand_aliasing={{0}: (8, {}), {1}: (9, {})} | custom-call | flops 4831838208 | bytes 16777216 | tf_op jit(solution)/shard_map/take_group/pallas_call | solution.py:106
  190.6 0.0 collective-permute-done.refs_0_.refs_1_.refs_2_
  190.6 15.8 %finish.1 = f32[10,256,256]{2,1,0:T(8,128)} custom-call(s32[142]{0:T(256)S(1)} %concatenate.7.meta, f32[2,10,256,256]{3,2,1,0:T(8,128)} %collective-permute-done.refs_0_.refs_1_.refs_2_, f32[2,10,256,256]{3,2,1,0:T(8,128)} %collective-permute-done.refs_0_.refs_1_.refs_2_, f32[2,10,256,256]{3,2,1,0:T(8,128)} %collective-permute-done.refs_0_.refs_1_.refs_2_, ...), custom_call_target="tpu_custom_call" | custom-call | flops 9663676416 | bytes 18874368 | tf_op jit(solution)/shard_map/finish/pallas_call | solution.py:155
  (15 shorter events, 0.1 us)
Async XLA Ops:
  0.0 153.8 %collective-permute-start.2 = (f32[12,256,256]{2,1,0:T(8,128)}, f32[12,256,256]{2,1,0:T(8,128)}, u32[]{:S(2)}, u32[]{:S(2)}) collective-permute-start(f32[12,256,256]{2,1,0:T(8,128)} %bitcast.33), channel_id=1, source_target_pairs={{0,30},{2,28},{4,2},{6,0},{8,6},{10,4},{12,10},{14,8},{16,14},{18,... | collective-permute-start | bytes 9437192 | tf_op jit(solution)/shard_map/ppermute | solution.py:193
  5.4 185.2 %collective-permute-start = (f32[2,10,256,256]{3,2,1,0:T(8,128)}, f32[2,10,256,256]{3,2,1,0:T(8,128)}, u32[]{:S(2)}, u32[]{:S(2)}) collective-permute-start(f32[2,10,256,256]{3,2,1,0:T(8,128)} %bitcast.20), channel_id=1, source_target_pairs={{0,1},{1,0},{2,3},{3,2},{4,5},{5,4},{6,7},{7,6},{8,9},{9,8},{10,11... | collective-permute-start | bytes 15728648 | tf_op jit(solution)/shard_map/ppermute | solution.py:186
  6.9 174.9 %collective-permute-start.1 = (f32[12,256,256]{2,1,0:T(8,128)}, f32[12,256,256]{2,1,0:T(8,128)S(1)}, u32[]{:S(2)}, u32[]{:S(2)}) collective-permute-start(f32[12,256,256]{2,1,0:T(8,128)} %bitcast.34), channel_id=1, source_target_pairs={{0,26},{2,0},{4,30},{6,4},{8,2},{10,8},{12,6},{14,12},{16,10},{18,... | collective-permute-start | bytes 9437192 | tf_op jit(solution)/shard_map/ppermute | solution.py:193
  153.9 22.3 %collective-permute-start.3 = (f32[12,256,256]{2,1,0:T(8,128)}, f32[12,256,256]{2,1,0:T(8,128)}, u32[]{:S(2)}, u32[]{:S(2)}) collective-permute-start(f32[12,256,256]{2,1,0:T(8,128)} %collective-permute-done.2.refs_0_.refs_1_.refs_2_.refs_3_), channel_id=1, source_target_pairs={{0,2},{2,0},{4,6},{6,4},{8,10},{10,8},{12,14},{14,12},{16,18},{18,... | collective-permute-start | bytes 9437192 | tf_op jit(solution)/shard_map/ppermute | solution.py:194
  158.1 2.5 %copy-start = (f32[1,1,2,10,256,256]{5,4,3,2,1,0:T(8,128)S(1)}, f32[1,1,2,10,256,256]{5,4,3,2,1,0:T(8,128)}, u32[]{:S(2)}) copy-start(f32[1,1,2,10,256,256]{5,4,3,2,1,0:T(8,128)} %param.6) | copy-start | bytes 15728644
  160.6 1.9 copy-start.2
  162.4 3.7 %copy-start.1 = (f32[1,1,2,10,256,256]{5,4,3,2,1,0:T(8,128)S(1)}, f32[1,1,2,10,256,256]{5,4,3,2,1,0:T(8,128)}, u32[]{:S(2)}) copy-start(f32[1,1,2,10,256,256]{5,4,3,2,1,0:T(8,128)} %param.6) | copy-start | bytes 15728644

commit v2 on v0

v2 whole, which is shorter than its diff:
```python
import functools

import jax
import jax.numpy as jnp
from jax import lax
from jax.experimental import pallas as pl
from jax.experimental.pallas import tpu as pltpu
from jax.sharding import PartitionSpec as P

RB = 3
KB = 4
CB = 4
STEPS = 4
UNROLL = 4
LIST_ROWS = 8


def pack_kernel(cuts, list_at, n_after, *refs):
    source, refs = refs[0], refs[1:]
    if list_at is not None:
        listed, refs = refs[0], refs[1:]
    target, sems = refs[n_after:]
    copies = [
        pltpu.make_async_copy(source.at[pl.ds(a, n)], target.at[pl.ds(b, n)], sems.at[i])
        for i, (a, b, n) in enumerate(cuts)
    ]
    if list_at is not None:
        copies.append(pltpu.make_async_copy(listed, target.at[pl.ds(list_at, LIST_ROWS)], sems.at[len(cuts)]))
    for copy in copies:
        copy.start()
    for copy in copies:
        copy.wait()


def pack(source, first, count, listed=None, after=()):
    columns = source.shape[1]
    part = count // 4
    cuts = [(first + i * part, i * part, part) for i in range(4)]
    rows = count + (0 if listed is None else LIST_ROWS)
    operands = [source] + ([] if listed is None else [listed]) + list(after)
    return pl.pallas_call(
        functools.partial(pack_kernel, cuts, None if listed is None else count, len(after)),
        in_specs=[pl.BlockSpec(memory_space=pl.ANY)] * len(operands),
        out_specs=pl.BlockSpec(memory_space=pl.ANY),
        out_shape=jax.ShapeDtypeStruct((rows, columns), source.dtype),
        scratch_shapes=[pltpu.SemaphoreType.DMA((5,))],
        cost_estimate=pl.CostEstimate(flops=0, bytes_accessed=8 * count * columns, transcendentals=0),
        name="pack",
    )(*operands)


def as_rows(places, columns):
    flat = places.reshape(-1).astype(jnp.float32)
    return jnp.pad(flat, (0, LIST_ROWS * columns - flat.size)).reshape(LIST_ROWS, columns)


def from_rows(packed, at, size):
    return packed[at : at + LIST_ROWS].reshape(-1)[:size].astype(jnp.int32)


def halves(values):
    high = values.astype(jnp.bfloat16)
    return high, (values - high.astype(jnp.float32)).astype(jnp.bfloat16)


def dot(left, right):
    return jnp.dot(left, right, preferred_element_type=jnp.float32)


def multiply_kernel(n_out, bs, plan, n_arrays, first, last, meta, *refs):
    arrays, refs = refs[:n_arrays], refs[n_arrays:]
    if not first:
        refs = refs[1:]
    if last:
        acc, out, r_map, o_map, todo, sems = refs
    else:
        acc, r_map, o_map, todo = refs
    if first:
        acc[...] = jnp.zeros_like(acc)
    for cell in range(RB * CB):
        o_map[cell] = -1
    for m in range(n_out):
        o_map[meta[2 * m] * CB + meta[2 * m + 1]] = m

    for left_at, first_block, n_left, list_at, uses in plan:
        left = arrays[left_at]
        for right_at, n_right, flag_at, right_list_at in uses:
            right = arrays[right_at]

            @pl.when(meta[flag_at] > 0)
            def _():
                for cell in range(KB * CB):
                    r_map[cell] = -1
                for j in range(n_right):
                    k, c = meta[right_list_at + 2 * j], meta[right_list_at + 2 * j + 1]
                    r_map[k * CB + c] = j

                def collect(i, count):
                    row, k = meta[list_at + 2 * i], meta[list_at + 2 * i + 1]
                    for c in range(CB):
                        j, m = r_map[k * CB + c], o_map[row * CB + c]
                        todo[count] = (i * 64 + jnp.maximum(j, 0)) * 64 + jnp.maximum(m, 0)
                        count = count + ((j >= 0) & (m >= 0)).astype(jnp.int32)
                    return count

                count = lax.fori_loop(0, n_left, collect, jnp.int32(0))
                for u in range(UNROLL):
                    todo[count + u] = n_out

                def several(q, carry):
                    for u in range(UNROLL):
                        code = todo[q * UNROLL + u]
                        i, j, m = code // 4096, (code // 64) % 64, code % 64
                        left_high, left_low = halves(left[pl.ds(pl.multiple_of((first_block + i) * bs, bs), bs), :])
                        right_high, right_low = halves(right[pl.ds(pl.multiple_of(j * bs, bs), bs), :])
                        acc[m] += (
                            dot(left_high, right_high) + dot(left_high, right_low) + dot(left_low, right_high)
                        )
                    return carry

                lax.fori_loop(0, (count + UNROLL - 1) // UNROLL, several, 0)

    if last:
        copies = [pltpu.make_async_copy(acc.at[m], out.at[m], sems.at[m]) for m in range(n_out)]
        for copy in copies:
            copy.start()
        for copy in copies:
            copy.wait()


def multiply(acc, pairs, parts, last=False, blocks=1):
    n_out = pairs.shape[0]
    arrays, scalars, plan = [], [pairs.reshape(-1)], []
    at = scalars[0].size

    def place(array):
        for index, other in enumerate(arrays):
            if other is array:
                return index
        arrays.append(array)
        return len(arrays) - 1

    def table(values):
        nonlocal at
        scalars.append(values.reshape(-1).astype(jnp.int32))
        at += values.size
        return at - values.size

    for left, first_block, left_list, uses in parts:
        entry = (place(left), first_block, left_list.size // 2, table(left_list))
        plan.append(entry + ([(place(r), r_list.size // 2, table(flag), table(r_list)) for r, r_list, flag in uses],))
    meta = jnp.concatenate(scalars)
    bs = arrays[0].shape[-1]
    first = acc is None
    vmem = pl.BlockSpec(memory_space=pltpu.VMEM)
    acc_shape = jax.ShapeDtypeStruct((n_out + 1, bs, bs), jnp.float32)
    most = max(n for _, _, n, _, _ in plan)
    scratch = [pltpu.SMEM(((KB + 1) * CB,), jnp.int32), pltpu.SMEM((RB * CB,), jnp.int32)]
    scratch.append(pltpu.SMEM((most * CB + UNROLL,), jnp.int32))
    if last:
        scratch.append(pltpu.SemaphoreType.DMA((n_out,)))
    out_shape, out_specs = [acc_shape], [vmem]
    if last:
        out_shape.append(jax.ShapeDtypeStruct((n_out, bs, bs), jnp.float32))
        out_specs.append(pl.BlockSpec(memory_space=pl.ANY))
    results = pl.pallas_call(
        functools.partial(multiply_kernel, n_out, bs, plan, len(arrays), first, last),
        in_specs=[pl.BlockSpec(memory_space=pltpu.SMEM)] + [vmem] * (len(arrays) + (not first)),
        out_specs=out_specs,
        out_shape=out_shape,
        scratch_shapes=scratch,
        input_output_aliases={} if first else {1 + len(arrays): 0},
        compiler_params=pltpu.CompilerParams(vmem_limit_bytes=32 * 2**20),
        cost_estimate=pl.CostEstimate(
            flops=blocks * 10 * 3 * 2 * bs**3, bytes_accessed=4 * 2**20, transcendentals=0
        ),
        name="multiply",
    )(meta, *arrays, *([] if first else [acc]))
    return results[-1]


def per_device(s_blocks, s_list, x_blocks, x_list, c_list, owner):
    length, width = lax.axis_size("loop"), lax.axis_size("bcast")
    line, column = lax.axis_index("loop"), lax.axis_index("bcast")
    pairs, owner = c_list[0, 0], owner[0]
    depth, n_s, bs = s_blocks.shape[2], s_blocks.shape[3], s_blocks.shape[-1]
    n_x = x_blocks.shape[2]
    x_rows = n_x * bs
    s_own = s_blocks.reshape(depth * n_s * bs, bs)
    s_own_list, x_own_list = s_list[0, 0], x_list[0, 0]
    swapped = width == 2

    cuts = [0, 3, n_s, depth * n_s - 3, depth * n_s]
    if swapped:
        partner = [(0, 1), (1, 0)]
        s_rows = as_rows(s_own_list, bs)
        sent = [pack(s_own, cuts[0] * bs, (cuts[1] - cuts[0]) * bs)]
        sent.append(pack(s_own, cuts[1] * bs, (cuts[2] - cuts[1]) * bs, s_rows, (sent[0],)))
        came = [lax.ppermute(chunk, "bcast", partner) for chunk in sent]
        for q in (2, 3):
            chunk = pack(s_own, cuts[q] * bs, (cuts[q + 1] - cuts[q]) * bs, None, (came[q - 2],))
            came.append(lax.ppermute(chunk, "bcast", partner))
        their_list = from_rows(came[1], (cuts[2] - cuts[1]) * bs, s_own_list.size).reshape(depth, n_s, 2)
        x_packed = pack(x_blocks.reshape(x_rows, bs), 0, x_rows, as_rows(x_own_list, bs), (sent[0],))
    else:
        held = lax.all_gather(s_own, "bcast")
        held_lists = lax.all_gather(s_own_list, "bcast")
        x_packed = pack(x_blocks.reshape(x_rows, bs), 0, x_rows, as_rows(x_own_list, bs))

    inside = [(g, g ^ 1) for g in range(length)]
    near = [(g, (g - 1) % length if g % 2 == 0 else (g - 3) % length) for g in range(length)]
    far = [(g, (g - 3) % length) for g in range(0, length, 2)]
    beside = lax.ppermute(x_packed, "loop", inside)
    close = lax.ppermute(x_packed, "loop", near)
    away = lax.ppermute(x_packed, "loop", far)
    handed = lax.ppermute(close, "loop", inside)
    odd = line % 2
    even = 1 - odd

    def group(packed):
        return packed, from_rows(packed, x_rows, x_own_list.size)

    own = (x_blocks.reshape(x_rows, bs), x_own_list)
    beside, close, away, handed = group(beside), group(close), group(away), group(handed)
    choices = [
        [(own, 1)],
        [(beside, even), (close, odd)],
        [(handed, 1)],
        [(close, even), (away, odd)],
    ]

    def uses(held_steps, late):
        found = []
        for step, held in held_steps:
            for (rows, places), applies in choices[step]:
                if late is None or (rows is away[0]) == late:
                    found.append((rows, places, jnp.asarray(held * applies, jnp.int32).reshape(1)))
        return found

    if not swapped:
        acc = None
        for step in range(STEPS):
            piece = lax.dynamic_index_in_dim(held, owner[step], 0, False)
            places = lax.dynamic_index_in_dim(held_lists, owner[step], 0, False)[step // width]
            part = (piece, step // width * n_s, places, uses([(step, 1)], None))
            acc = multiply(acc, pairs, [part], last=step == STEPS - 1, blocks=n_s)
        return acc[None, None]

    mine = (owner == column).astype(jnp.int32)
    own_parts, their_steps = [], []
    for slot in range(depth):
        steps = [2 * slot, 2 * slot + 1]
        own_parts.append((slot, [(s, mine[s]) for s in steps]))
        their_steps.append([(s, 1 - mine[s]) for s in steps])

    def chunk_part(q, late):
        slot = cuts[q] // n_s
        lo = cuts[q] - slot * n_s
        return (came[q], 0, their_list[slot, lo : lo + cuts[q + 1] - cuts[q]], uses(their_steps[slot], late))

    def own_part(slot, late):
        return (s_own, slot * n_s, s_own_list[slot], uses(own_parts[slot][1], late))

    acc = multiply(None, pairs, [own_part(0, False)], blocks=n_s)
    acc = multiply(acc, pairs, [chunk_part(0, False), chunk_part(1, False)], blocks=n_s)
    acc = multiply(acc, pairs, [own_part(1, False)], blocks=n_s)
    acc = multiply(acc, pairs, [chunk_part(2, False)], blocks=n_s)
    acc = multiply(acc, pairs, [own_part(1, True), chunk_part(2, True)], blocks=n_s)
    out = multiply(acc, pairs, [chunk_part(3, None)], last=True, blocks=3)
    return out[None, None]


def solution(mesh):
    return jax.shard_map(
        per_device,
        mesh=mesh,
        in_specs=(
            P("loop", "bcast", None, None, None, None),
            P("loop", "bcast", None, None, None),
            P("loop", "bcast", None, None, None),
            P("loop", "bcast", None, None),
            P("loop", "bcast", None, None),
            P("loop", None),
        ),
        out_specs=P("loop", "bcast", None, None, None),
        check_vma=False,
    )
```

time: 399 us -> 382 us (0.957)
  Pallas kernels: 0 us -> 293 us
  waiting for transfers between devices: 192 us -> 47.8 us
  matrix products: 133 us -> 0 us
  other arithmetic: 13.2 us -> 0.03 us
  between operations: 16.4 us -> 5.47 us
  local copies, waits for them, and re-layouts: 14.9 us -> 21.6 us
  starting transfers between devices: 20.1 us -> 13.4 us
  blocking collectives: 5 us -> 0 us
    pallas_call x0 -> x11, Pallas kernels: none -> 293 us  [the longest x5 260 us: pack(): pl.pallas_call(functools.partial(pack_kernel, cuts, None if listed is Non...]
    dot_general x12 -> x0, matrix products: 133 us -> none  [the longest x4 81 us: block_terms(): full_slab = jnp.einsum('rkab,kcbd->rcad', left, right, precision=HIGHEST)]
    psum x1 -> x0, waiting for transfers between devices: 99.5 us -> none  [spread(): return lax.psum(block, axis)]
    ppermute x6 -> x8, waiting for transfers between devices: 92.5 us -> 47.8 us  [the longest x2 47.8 us: per_device(): came = [lax.ppermute(chunk, 'bcast', partner) for chunk in sent]]
    unnamed x16 -> x40, local copies, waits for them, and re-layouts: 1.88 us -> 16.9 us
    gather x4 -> x0, local copies, waits for them, and re-layouts: 9.38 us -> none  [block_terms(): return full_slab[pairs[:, 0], pairs[:, 1]]]
    select_n x2 -> x0, other arithmetic: 6.76 us -> none  [spread(): jnp.where(lax.axis_index(axis) == owner, block, jnp.zeros_like(block))]
    ppermute x6 -> x8, starting transfers between devices: 20.1 us -> 13.4 us  [the longest x1 5.47 us: per_device(): close = lax.ppermute(x_packed, 'loop', near)]
  transfers between devices with their start and end apart: 7 -> 8, of which waited for: 5 -> 1; matrix products, arithmetic and copies ran while one was open for 7% -> 2% of each run, Pallas kernels for 0% -> 43%
where the time goes in v2:
time: 382 us; the launch traced here: 381 us
  Pallas kernels  293 us (77%)
  waiting for transfers between devices  47.8 us (13%)
  local copies, waits for them, and re-layouts  21.6 us (6%)
  starting transfers between devices  13.4 us (4%)
  between operations  5.47 us (1%)
    pallas_call x5, Pallas kernels, pack(): pl.pallas_call(functools.partial(pack_kernel, cuts, None if listed is Non...  260 us
    ppermute x2, waiting for transfers between devices, per_device(): came = [lax.ppermute(chunk, 'bcast', partner) for chunk in sent]  47.8 us
    pallas_call x6, Pallas kernels, multiply(): pl.pallas_call(functools.partial(multiply_kernel, n_out, bs, plan, len(ar...  32.6 us
    unnamed x40, local copies, waits for them, and re-layouts  16.9 us
  transfers between devices with their start and end apart: 8, of which 1 were waited for; matrix products, arithmetic and copies ran while one was open for 2% of the time, Pallas kernels for 43%

profile of v2, /device:TPU:0, one launch (start us, length us, event | category | flops | bytes accessed | tf_op | source)
XLA Modules:
  0.0 381.3 jit_solution(3026523877238887779)
XLA Ops:
  0.0 25.0 %pack.5.refs_2_ = f32[768,256]{1,0:T(8,128)} custom-call(f32[5120,256]{1,0:T(8,128)} %bitcast.30), custom_call_target="tpu_custom_call" | custom-call | bytes 1572864 | tf_op jit(solution)/shard_map/pack/pallas_call | solution.py:41
  25.0 0.1 copy.19
  25.1 0.1 reshape_squeeze.18
  25.2 0.6 reshape.87.refs_1_
  25.8 96.7 %pack.7 = f32[3080,256]{1,0:T(8,128)} custom-call(f32[3072,256]{1,0:T(8,128)} %bitcast.39, f32[8,256]{1,0:T(8,128)} %reshape.87.refs_1_, f32[768,256]{1,0:T(8,128)} %pack.5.refs_2_), custom_call_target="tpu_custom_call" | custom-call | bytes 6291456 | tf_op jit(solution)/shard_map/pack/pallas_call | solution.py:41
  122.5 5.5 %collective-permute-start.1 = (f32[3080,256]{1,0:T(8,128)}, f32[3080,256]{1,0:T(8,128)S(1)}, u32[]{:S(2)}, u32[]{:S(2)}) collective-permute-start(f32[3080,256]{1,0:T(8,128)} %pack.7), channel_id=1, source_target_pairs={{0,30},{2,28},{4,2},{6,0},{8,6},{10,4},{12,10},{14,8},{16,14},{18,... | collective-permute-start | bytes 9461768 | tf_op jit(solution)/shard_map/ppermute | solution.py:214
  128.0 0.7 collective-permute-start.7
  128.6 0.1 copy.18
  128.7 0.1 convert_element_type.37
  128.8 0.6 reshape.84.refs_1_
  129.4 57.0 %pack.6 = f32[1800,256]{1,0:T(8,128)} custom-call(f32[5120,256]{1,0:T(8,128)} %bitcast.31, f32[8,256]{1,0:T(8,128)} %reshape.84.refs_1_, f32[768,256]{1,0:T(8,128)} %pack.5.refs_2_), custom_call_target="tpu_custom_call" | custom-call | bytes 3670016 | tf_op jit(solution)/shard_map/pack/pallas_call | solution.py:41
  186.4 1.6 collective-permute-start
  188.0 0.5 collective-permute-start.5
  188.5 3.0 collective-permute-start.3
  191.6 0.7 fusion.3
  196.2 0.1 copy.17
  196.2 0.1 reshape_squeeze.16
  196.3 0.1 copy.21
  196.4 0.1 reshape_squeeze.42
  196.5 0.1 copy.20
  198.0 47.8 %collective-permute-done.5.refs_1_.refs_0_ = f32[768,256]{1,0:T(8,128)} collective-permute-done((f32[768,256]{1,0:T(8,128)}, f32[768,256]{1,0:T(8,128)}, u32[]{:S(2)}, u32[]{:S(2)}) %collective-permute-start.5) | collective-permute-done | bytes 786464 | tf_op jit(solution)/shard_map/ppermute | solution.py:199
  245.8 56.7 %pack.9 = f32[1792,256]{1,0:T(8,128)} custom-call(f32[5120,256]{1,0:T(8,128)} %bitcast.32, f32[768,256]{1,0:T(8,128)} %collective-permute-done.5.refs_1_.refs_0_), custom_call_target="tpu_custom_call" | custom-call | bytes 3670016 | tf_op jit(solution)/shard_map/pack/pallas_call | solution.py:41
  302.5 1.6 collective-permute-start.6
  304.1 0.7 slice_bitcast_fusion.4
  304.8 0.1 convert_element_type.39
  305.0 0.1 reshape_squeeze.40
  305.2 25.0 %pack.8 = f32[768,256]{1,0:T(8,128)} custom-call(f32[5120,256]{1,0:T(8,128)} %bitcast.33, f32[1800,256]{1,0:T(8,128)} %collective-permute-done.refs_1_.refs_4_), custom_call_target="tpu_custom_call" | custom-call | bytes 1572864 | tf_op jit(solution)/shard_map/pack/pallas_call | solution.py:41
  330.2 0.6 collective-permute-start.4
  330.8 0.7 slice_bitcast_fusion
  331.6 0.7 concatenate.23.meta
  332.3 0.1 concatenate.22.meta
  332.4 2.5 copy-done
  334.9 1.9 copy-done.2
  336.7 6.0 %multiply.6.refs_5_ = f32[11,256,256]{2,1,0:T(8,128)S(1)} custom-call(s32[115]{0:T(128)S(1)} %concatenate.23.meta, f32[5120,256]{1,0:T(8,128)S(1)} %bitcast.34, f32[3072,256]{1,0:T(8,128)S(1)} %bitcast.40, f32[3080,256]{1,0:T(8,128)} %collective-permute-done.7.refs_2_, f32[3080,256]{1,0:T(8,128)S(1)} %collective-permute-done.1.refs_3_.refs_2_), custom_call_target="tpu_custom_call" | custom-call | flops 10066329600 | bytes 4194304 | tf_op jit(solution)/shard_map/multiply/pallas_call | solution.py:166
  342.8 7.9 %multiply.7.refs_3_ = f32[11,256,256]{2,1,0:T(8,128)S(1)} custom-call(s32[190]{0:T(256)S(1)} %concatenate.22.meta, f32[768,256]{1,0:T(8,128)} %collective-permute-done.5.refs_1_.refs_0_, f32[3072,256]{1,0:T(8,128)S(1)} %bitcast.41, f32[3080,256]{1,0:T(8,128)} %collective-permute-done.7.refs_2_, ...), custom_call_target="tpu_custom_call", output_to_operand_aliasing={{}: (6, {})} | custom-call | flops 10066329600 | bytes 4194304 | tf_op jit(solution)/shard_map/multiply/pallas_call | solution.py:166
  350.7 1.6 copy-done.4
  352.3 0.7 slice_bitcast_fusion.1
  353.0 0.1 concatenate.19.meta
  353.1 0.7 slice_bitcast_fusion.3
  353.8 0.7 concatenate.21.meta
  354.7 2.5 copy-done.1
  357.2 1.8 copy-done.5
  359.0 5.1 %multiply.8.refs_3_ = f32[11,256,256]{2,1,0:T(8,128)S(1)} custom-call(s32[90]{0:T(128)S(1)} %concatenate.21.meta, f32[5120,256]{1,0:T(8,128)S(1)} %bitcast.35, f32[3080,256]{1,0:T(8,128)} %collective-permute-done.2.refs_1_, f32[3080,256]{1,0:T(8,128)S(1)} %collective-permute-done.1.refs_3_.refs_2_, ...), custom_call_target="tpu_custom_call", output_to_operand_aliasing={{}: (4, {})} | custom-call | flops 10066329600 | bytes 4194304 | tf_op jit(solution)/shard_map/multiply/pallas_call | solution.py:166
  364.1 1.6 copy-done.6
  365.7 2.0 copy-done.7
  367.6 5.6 %multiply.9.refs_3_ = f32[11,256,256]{2,1,0:T(8,128)S(1)} custom-call(s32[84]{0:T(128)S(1)} %concatenate.20.meta, f32[1792,256]{1,0:T(8,128)} %collective-permute-done.6.refs_0_.refs_2_, f32[3080,256]{1,0:T(8,128)} %collective-permute-done.2.refs_1_, f32[3080,256]{1,0:T(8,128)S(1)} %collective-permute-done.1.refs_3_.refs_2_, ...), custom_call_target="tpu_custom_call", output_to_operand_aliasing={{}: (4, {})} | custom-call | flops 10066329600 | bytes 4194304 | tf_op jit(solution)/shard_map/multiply/pallas_call | solution.py:166
  373.3 2.5 multiply.10.refs_4_
  375.8 5.5 %multiply.11 = (f32[11,256,256]{2,1,0:T(8,128)S(1)}, f32[10,256,256]{2,1,0:T(8,128)}) custom-call(s32[101]{0:T(128)S(1)} %concatenate.18.meta, f32[768,256]{1,0:T(8,128)} %collective-permute-done.4.refs_0_, f32[3080,256]{1,0:T(8,128)} %collective-permute-done.2.refs_1_, ...), custom_call_target="tpu_custom_call", output_to_operand_aliasing={{0}: (5, {})} | custom-call | flops 3019898880 | bytes 4194304 | tf_op jit(solution)/shard_map/multiply/pallas_call | solution.py:166
  (55 shorter events, 0.6 us)
Async XLA Ops:
  0.0 25.0 %copy-start.9 = (s32[1,1,12,2]{2,3,1,0:T(2,128)S(1)}, s32[1,1,12,2]{2,3,1,0:T(2,128)}, u32[]{:S(2)}) copy-start(s32[1,1,12,2]{2,3,1,0:T(2,128)} %param.9) | copy-start | bytes 292
  25.8 102.8 %copy-start.8 = (s32[1,1,2,10,2]{3,4,2,1,0:T(2,128)S(1)}, s32[1,1,2,10,2]{3,4,2,1,0:T(2,128)}, u32[]{:S(2)}) copy-start(s32[1,1,2,10,2]{3,4,2,1,0:T(2,128)} %param.7) | copy-start | bytes 484
  122.5 208.3 %collective-permute-start.1 = (f32[3080,256]{1,0:T(8,128)}, f32[3080,256]{1,0:T(8,128)S(1)}, u32[]{:S(2)}, u32[]{:S(2)}) collective-permute-start(f32[3080,256]{1,0:T(8,128)} %pack.7), channel_id=1, source_target_pairs={{0,30},{2,28},{4,2},{6,0},{8,6},{10,4},{12,10},{14,8},{16,14},{18,... | collective-permute-start | bytes 9461768 | tf_op jit(solution)/shard_map/ppermute | solution.py:214
  128.0 202.9 %collective-permute-start.7 = (f32[3080,256]{1,0:T(8,128)}, f32[3080,256]{1,0:T(8,128)}, u32[]{:S(2)}, u32[]{:S(2)}) collective-permute-start(f32[3080,256]{1,0:T(8,128)} %pack.7), channel_id=1, source_target_pairs={{0,2},{2,0},{4,6},{6,4},{8,10},{10,8},{12,14},{14,12},{16,18},{18,... | collective-permute-start | bytes 9461768 | tf_op jit(solution)/shard_map/ppermute | solution.py:213
  129.4 62.1 %copy-start.11 = (s32[1,4]{1,0:T(1,128)S(1)}, s32[1,4]{1,0:T(1,128)}, u32[]{:S(2)}) copy-start(s32[1,4]{1,0:T(1,128)} %param.11) | copy-start | bytes 52
  129.4 66.7 %copy-start.10 = (s32[1,1,10,2]{2,3,1,0:T(2,128)S(1)}, s32[1,1,10,2]{2,3,1,0:T(2,128)}, u32[]{:S(2)}) copy-start(s32[1,1,10,2]{2,3,1,0:T(2,128)} %param.10) | copy-start | bytes 244
  186.4 117.7 %collective-permute-start = (f32[1800,256]{1,0:T(8,128)}, f32[1800,256]{1,0:T(8,128)}, u32[]{:S(2)}, u32[]{:S(2)}) collective-permute-start(f32[1800,256]{1,0:T(8,128)} %pack.6), channel_id=1, source_target_pairs={{0,1},{1,0},{2,3},{3,2},{4,5},{5,4},{6,7},{7,6},{8,9},{9,8},{10,11... | collective-permute-start | bytes 5529608 | tf_op jit(solution)/shard_map/ppermute | solution.py:199
  188.0 57.7 %collective-permute-start.5 = (f32[768,256]{1,0:T(8,128)}, f32[768,256]{1,0:T(8,128)}, u32[]{:S(2)}, u32[]{:S(2)}) collective-permute-start(f32[768,256]{1,0:T(8,128)} %pack.5.refs_2_), channel_id=1, source_target_pairs={{0,1},{1,0},{2,3},{3,2},{4,5},{5,4},{6,7},{7,6},{8,9},{9,8},{10,11... | collective-permute-start | bytes 2359304 | tf_op jit(solution)/shard_map/ppermute | solution.py:199
  188.5 163.8 %collective-permute-start.3 = (f32[3080,256]{1,0:T(8,128)}, f32[3080,256]{1,0:T(8,128)}, u32[]{:S(2)}, u32[]{:S(2)}) collective-permute-start(f32[3080,256]{1,0:T(8,128)} %pack.7), channel_id=1, source_target_pairs={{0,26},{4,30},{8,2},{12,6},{16,10},{20,14},{24,18},{28,22},{1,27},... | collective-permute-start | bytes 9461768 | tf_op jit(solution)/shard_map/ppermute | solution.py:215
  302.5 63.2 %collective-permute-start.6 = (f32[1792,256]{1,0:T(8,128)}, f32[1792,256]{1,0:T(8,128)}, u32[]{:S(2)}, u32[]{:S(2)}) collective-permute-start(f32[1792,256]{1,0:T(8,128)} %pack.9), channel_id=1, source_target_pairs={{0,1},{1,0},{2,3},{3,2},{4,5},{5,4},{6,7},{7,6},{8,9},{9,8},{10,11... | collective-permute-start | bytes 5505032 | tf_op jit(solution)/shard_map/ppermute | solution.py:202
  330.2 45.6 %collective-permute-start.4 = (f32[768,256]{1,0:T(8,128)}, f32[768,256]{1,0:T(8,128)}, u32[]{:S(2)}, u32[]{:S(2)}) collective-permute-start(f32[768,256]{1,0:T(8,128)} %pack.8), channel_id=1, source_target_pairs={{0,1},{1,0},{2,3},{3,2},{4,5},{5,4},{6,7},{7,6},{8,9},{9,8},{10,11... | collective-permute-start | bytes 2359304 | tf_op jit(solution)/shard_map/ppermute | solution.py:202
  330.8 22.3 %collective-permute-start.2 = (f32[3080,256]{1,0:T(8,128)S(1)}, f32[3080,256]{1,0:T(8,128)}, u32[]{:S(2)}, u32[]{:S(2)}) collective-permute-start(f32[3080,256]{1,0:T(8,128)S(1)} %collective-permute-done.1.refs_3_.refs_2_), channel_id=1, source_target_pairs={{0,2},{2,0},{4,6},{6,4},{8,10},{10,8},{12,14},{14,12},{16,18},{18,... | collective-permute-start | bytes 9461768 | tf_op jit(solution)/shard_map/ppermute | solution.py:216
  332.4 2.5 copy-start
  334.8 1.9 copy-start.2
  336.7 6.0 %copy-start.3 = (f32[1,1,12,256,256]{4,3,2,1,0:T(8,128)S(1)}, f32[1,1,12,256,256]{4,3,2,1,0:T(8,128)}, u32[]{:S(2)}) copy-start(f32[1,1,12,256,256]{4,3,2,1,0:T(8,128)} %param.8) | copy-start | bytes 9437188
  350.7 1.6 copy-start.4
  354.7 2.5 copy-start.1
  357.2 1.8 copy-start.5
  359.0 14.3 %slice-start = ((s8[5242880]{0:T(1024)(128)(4,1)}), s8[1048576]{0:T(1024)(128)(4,1)S(1)}, s32[]{:S(2)}) async-start(s8[5242880]{0:T(1024)(128)(4,1)} %bitcast.36), calls=%async_computation | async-start | bytes 2097152
  364.1 1.6 copy-start.6
  365.7 7.6 %slice-start.1 = ((s8[5242880]{0:T(1024)(128)(4,1)}), s8[4194304]{0:T(1024)(128)(4,1)S(1)}, s32[]{:S(2)}) async-start(s8[5242880]{0:T(1024)(128)(4,1)} %bitcast.36), calls=%async_computation.1 | async-start | bytes 8388608
  365.7 2.0 copy-start.7

commit v3 on v2

v3 whole, which is shorter than its diff:
```python
import functools

import jax
import jax.numpy as jnp
from jax import lax
from jax.experimental import pallas as pl
from jax.experimental.pallas import tpu as pltpu
from jax.sharding import PartitionSpec as P

RB = 3
KB = 4
CB = 4
STEPS = 4
UNROLL = 4
LIST_ROWS = 8
X_PARTS = 2
VMEM_LIMIT = 24 * 2**20
PACK_LIMIT = 56 * 2**20


def pack_kernel(cuts, *refs):
    target, sems = refs[-2:]
    copies = [
        pltpu.make_async_copy(refs[which].at[pl.ds(a, n)], target.at[pl.ds(b, n)], sems.at[i])
        for i, (which, a, b, n) in enumerate(cuts)
    ]
    for copy in copies:
        copy.start()
    for copy in copies:
        copy.wait()


def pack(source, first, count, listed=None, after=()):
    columns = source.shape[1]
    part = count // 4
    cuts = [(0, first + i * part, i * part, part) for i in range(4)]
    operands = [source]
    if listed is not None:
        cuts.append((1, 0, count, LIST_ROWS))
        operands.append(listed)
    operands += after
    rows = sum(n for _, _, _, n in cuts)
    return pl.pallas_call(
        functools.partial(pack_kernel, cuts),
        in_specs=[pl.BlockSpec(memory_space=pl.ANY)] * len(operands),
        out_specs=pl.BlockSpec(memory_space=pltpu.VMEM),
        out_shape=jax.ShapeDtypeStruct((rows, columns), source.dtype),
        scratch_shapes=[pltpu.SemaphoreType.DMA((len(cuts),))],
        compiler_params=pltpu.CompilerParams(vmem_limit_bytes=PACK_LIMIT),
        cost_estimate=pl.CostEstimate(flops=0, bytes_accessed=8 * count * columns, transcendentals=0),
        name="pack",
    )(*operands)


def as_rows(places, columns):
    flat = places.reshape(-1).astype(jnp.float32)
    return jnp.pad(flat, (0, LIST_ROWS * columns - flat.size)).reshape(LIST_ROWS, columns)


def from_rows(packed, at, size):
    return packed[at : at + LIST_ROWS].reshape(-1)[:size].astype(jnp.int32)


def halves(values):
    high = values.astype(jnp.bfloat16)
    return high, (values - high.astype(jnp.float32)).astype(jnp.bfloat16)


def dot(left, right):
    return jnp.dot(left, right, preferred_element_type=jnp.float32)


def multiply_kernel(n_out, bs, plan, n_tables, n_arrays, first, last, *refs):
    tables, refs = refs[:n_tables], refs[n_tables:]
    meta = tables[0]
    arrays, refs = refs[:n_arrays], refs[n_arrays:]
    if not first:
        refs = refs[1:]
    if last:
        acc, out, r_map, o_map, todo, sems = refs
    else:
        acc, r_map, o_map, todo = refs
    if first:
        acc[...] = jnp.zeros_like(acc)
    for cell in range(RB * CB):
        o_map[cell] = -1
    for m in range(n_out):
        o_map[meta[2 * m] * CB + meta[2 * m + 1]] = m

    for left_at, first_block, n_left, table_at, list_at, uses in plan:
        entries = tables[table_at]
        left = arrays[left_at]
        for right_at, n_right, flag_at, right_list_at in uses:
            right = arrays[right_at]

            @pl.when(meta[flag_at] > 0)
            def _():
                for cell in range(KB * CB):
                    r_map[cell] = -1
                for j in range(n_right):
                    k, c = meta[right_list_at + 2 * j], meta[right_list_at + 2 * j + 1]
                    r_map[k * CB + c] = j

                def collect(i, count):
                    row, k = entries[list_at + 2 * i], entries[list_at + 2 * i + 1]
                    for c in range(CB):
                        j, m = r_map[k * CB + c], o_map[row * CB + c]
                        todo[count] = (i * 64 + jnp.maximum(j, 0)) * 64 + jnp.maximum(m, 0)
                        count = count + ((j >= 0) & (m >= 0)).astype(jnp.int32)
                    return count

                count = lax.fori_loop(0, n_left, collect, jnp.int32(0))
                for u in range(UNROLL):
                    todo[count + u] = n_out

                def several(q, carry):
                    for u in range(UNROLL):
                        code = todo[q * UNROLL + u]
                        i, j, m = code // 4096, (code // 64) % 64, code % 64
                        left_high, left_low = halves(left[pl.ds(pl.multiple_of((first_block + i) * bs, bs), bs), :])
                        right_high, right_low = halves(right[pl.ds(pl.multiple_of(j * bs, bs), bs), :])
                        acc[m] += (
                            dot(left_high, right_high) + dot(left_high, right_low) + dot(left_low, right_high)
                        )
                    return carry

                lax.fori_loop(0, (count + UNROLL - 1) // UNROLL, several, 0)

    if last:
        copies = [pltpu.make_async_copy(acc.at[m], out.at[m], sems.at[m]) for m in range(n_out)]
        for copy in copies:
            copy.start()
        for copy in copies:
            copy.wait()


def multiply(acc, pairs, parts, last=False, late_list=None):
    n_out = pairs.shape[0]
    arrays, scalars, plan = [], [pairs.reshape(-1)], []
    at = scalars[0].size

    def place(array):
        for index, other in enumerate(arrays):
            if other is array:
                return index
        arrays.append(array)
        return len(arrays) - 1

    def table(values):
        nonlocal at
        scalars.append(values.reshape(-1).astype(jnp.int32))
        at += values.size
        return at - values.size

    for left, first_block, left_list, uses in parts:
        if isinstance(left_list, tuple):
            entry = (place(left), first_block, left_list[1], 1, left_list[0])
        else:
            entry = (place(left), first_block, left_list.size // 2, 0, table(left_list))
        plan.append(entry + ([(place(r), r_list.size // 2, table(flag), table(r_list)) for r, r_list, flag in uses],))
    tables = [jnp.concatenate(scalars)] + ([] if late_list is None else [late_list])
    bs = arrays[0].shape[-1]
    first = acc is None
    vmem = pl.BlockSpec(memory_space=pltpu.VMEM)
    acc_shape = jax.ShapeDtypeStruct((n_out + 1, bs, bs), jnp.float32)
    most = max(n for _, _, n, _, _, _ in plan)
    scratch = [pltpu.SMEM(((KB + 1) * CB,), jnp.int32), pltpu.SMEM((RB * CB,), jnp.int32)]
    scratch.append(pltpu.SMEM((most * CB + UNROLL,), jnp.int32))
    if last:
        scratch.append(pltpu.SemaphoreType.DMA((n_out,)))
    out_shape, out_specs = [acc_shape], [vmem]
    if last:
        out_shape.append(jax.ShapeDtypeStruct((n_out, bs, bs), jnp.float32))
        out_specs.append(pl.BlockSpec(memory_space=pl.ANY))
    results = pl.pallas_call(
        functools.partial(multiply_kernel, n_out, bs, plan, len(tables), len(arrays), first, last),
        in_specs=[pl.BlockSpec(memory_space=pltpu.SMEM)] * len(tables) + [vmem] * (len(arrays) + (not first)),
        out_specs=out_specs,
        out_shape=out_shape,
        scratch_shapes=scratch,
        input_output_aliases={} if first else {len(tables) + len(arrays): 0},
        compiler_params=pltpu.CompilerParams(vmem_limit_bytes=VMEM_LIMIT),
        cost_estimate=pl.CostEstimate(
            flops=5 * 10**9, bytes_accessed=4 * 2**20, transcendentals=0
        ),
        name="multiply",
    )(*tables, *arrays, *([] if first else [acc]))
    return results[-1]


def per_device(s_blocks, s_list, x_blocks, x_list, c_list, owner):
    length, width = lax.axis_size("loop"), lax.axis_size("bcast")
    line, column = lax.axis_index("loop"), lax.axis_index("bcast")
    pairs, owner = c_list[0, 0], owner[0]
    depth, n_s, bs = s_blocks.shape[2], s_blocks.shape[3], s_blocks.shape[-1]
    n_x = x_blocks.shape[2]
    s_own = s_blocks.reshape(depth * n_s * bs, bs)
    s_own_list, x_own_list = s_list[0, 0], x_list[0, 0]
    swapped = width == 2

    if swapped:
        partner = [(0, 1), (1, 0)]
        came = lax.ppermute(s_own, "bcast", partner)
        their_list = lax.ppermute(s_own_list.reshape(-1), "bcast", partner)
    else:
        held = lax.all_gather(s_own, "bcast")
        held_lists = lax.all_gather(s_own_list, "bcast")

    inside = [(g, g ^ 1) for g in range(length)]
    near = [(g, (g - 1) % length if g % 2 == 0 else (g - 3) % length) for g in range(length)]
    far = [(g, (g - 3) % length if g % 2 == 0 else (g - 1) % length) for g in range(length)]
    x_own = x_blocks.reshape(n_x * bs, bs)
    share = n_x // X_PARTS
    x_parts = []
    for p in range(X_PARTS):
        rows = as_rows(x_own_list[p * share : (p + 1) * share], bs)
        x_parts.append(jnp.concatenate([x_own[p * share * bs : (p + 1) * share * bs], rows]))

    def moved(parts, pairs):
        return [lax.ppermute(part, "loop", pairs) for part in parts]

    def listed(parts):
        return [(part, from_rows(part, share * bs, 2 * share)) for part in parts]

    close_parts = moved(x_parts, near)
    groups = {
        "own": [(x_own, x_own_list)],
        "close": listed(close_parts),
        "handed": listed(moved(close_parts, inside)),
    }
    odd = line % 2
    even = 1 - odd
    choices = [
        [("own", 1)],
        [("away", even), ("close", odd)],
        [("handed", 1)],
        [("close", even), ("away", odd)],
    ]

    def uses(held_steps, names):
        found = []
        for step, held in held_steps:
            for name, applies in choices[step]:
                if name in names:
                    flag = jnp.asarray(held * applies, jnp.int32).reshape(1)
                    found += [(rows, places, flag) for rows, places in groups[name]]
        return found

    if not swapped:
        groups["away"] = listed(moved(x_parts, far))
        acc = None
        for step in range(STEPS):
            piece = lax.dynamic_index_in_dim(held, owner[step], 0, False)
            places = lax.dynamic_index_in_dim(held_lists, owner[step], 0, False)[step // width]
            part = (piece, step // width * n_s, places, uses([(step, 1)], groups))
            acc = multiply(acc, pairs, [part], last=step == STEPS - 1)
        return acc[None, None]

    mine = (owner == column).astype(jnp.int32)

    def own_part(slot, *names):
        steps = [(s, mine[s]) for s in (2 * slot, 2 * slot + 1)]
        return (s_own, slot * n_s, s_own_list[slot], uses(steps, names))

    def their_part(slot, *names):
        steps = [(s, 1 - mine[s]) for s in (2 * slot, 2 * slot + 1)]
        return (came, slot * n_s, (slot * 2 * n_s, n_s), uses(steps, names))

    packed = pack(x_own, 0, n_x * bs, as_rows(x_own_list, bs), (close_parts[0],))
    packed = lax.ppermute(packed, "loop", far)
    groups["away"] = [(packed, from_rows(packed, n_x * bs, x_own_list.size))]
    acc = multiply(None, pairs, [own_part(0, "own", "close"), own_part(1, "close", "handed")])
    acc = multiply(acc, pairs, [own_part(0, "away"), own_part(1, "away")])
    their_parts = [their_part(0, "own", "close", "away"), their_part(1, "close", "handed", "away")]
    out = multiply(acc, pairs, their_parts, last=True, late_list=their_list)
    return out[None, None]


def solution(mesh):
    return jax.shard_map(
        per_device,
        mesh=mesh,
        in_specs=(
            P("loop", "bcast", None, None, None, None),
            P("loop", "bcast", None, None, None),
            P("loop", "bcast", None, None, None),
            P("loop", "bcast", None, None),
            P("loop", "bcast", None, None),
            P("loop", None),
        ),
        out_specs=P("loop", "bcast", None, None, None),
        check_vma=False,
    )
```

time: 382 us -> 144 us (0.38)
  Pallas kernels: 293 us -> 31.5 us
  waiting for transfers between devices: 47.8 us -> 70.2 us
    pallas_call x11 -> x4, Pallas kernels: 293 us -> 31.5 us  [the longest x3 27.7 us: multiply(): pl.pallas_call(functools.partial(multiply_kernel, n_out, bs, plan, len(ta...]
    ppermute x8 -> x7, waiting for transfers between devices: 47.8 us -> 70.2 us  [the longest x4 57.3 us: moved(): return [lax.ppermute(part, 'loop', pairs) for part in parts]]
    ppermute x8 -> x7, starting transfers between devices: 13.4 us -> 11 us  [the longest x4 6.39 us: moved(): return [lax.ppermute(part, 'loop', pairs) for part in parts]]
    unnamed x40 -> x35, local copies, waits for them, and re-layouts: 16.9 us -> 15.7 us
  transfers between devices with their start and end apart: 8 -> 7, of which waited for: 1 -> 4; matrix products, arithmetic and copies ran while one was open for 2% -> 6% of each run, Pallas kernels for 43% -> 12%
where the time goes in v3:
time: 144 us; the launch traced here: 143 us
  waiting for transfers between devices  70.2 us (49%)
  Pallas kernels  31.5 us (22%)
  local copies, waits for them, and re-layouts  22.3 us (15%)
  starting transfers between devices  11 us (8%)
  between operations  5.36 us (4%)
  other arithmetic  2.21 us (2%)
    ppermute x4, waiting for transfers between devices, moved(): return [lax.ppermute(part, 'loop', pairs) for part in parts]  57.3 us
    pallas_call x3, Pallas kernels, multiply(): pl.pallas_call(functools.partial(multiply_kernel, n_out, bs, plan, len(ta...  27.7 us
    unnamed x35, local copies, waits for them, and re-layouts  15.7 us
    ppermute x1, waiting for transfers between devices, per_device(): packed = lax.ppermute(packed, 'loop', far)  10.7 us
    ppermute x4, starting transfers between devices, moved(): return [lax.ppermute(part, 'loop', pairs) for part in parts]  6.39 us
    pallas_call x1, Pallas kernels, pack(): pl.pallas_call(functools.partial(pack_kernel, cuts), in_specs=[pl.BlockSp...  3.74 us
  transfers between devices with their start and end apart: 7, of which 4 were waited for; matrix products, arithmetic and copies ran while one was open for 6% of the time, Pallas kernels for 12%

profile of v3, /device:TPU:0, one launch (start us, length us, event | category | flops | bytes accessed | tf_op | source)
XLA Modules:
  0.0 142.5 jit_solution(4321416108100462436)
XLA Ops:
  0.0 0.8 slice_convert_fusion
  0.8 0.1 copy.18
  0.9 0.1 convert_element_type.42
  1.0 2.2 %fusion = (f32[1,1,6,256,256]{4,3,2,1,0:T(8,128)S(1)}, f32[1,1,6,256,256]{4,3,2,1,0:T(8,128)S(1)}) fusion(f32[1,1,12,256,256]{4,3,2,1,0:T(8,128)} %param.8), kind=kLoop, calls=%fused_computation.15 | loop fusion | bytes 6291456 | tf_op jit(solution)/shard_map/slice | solution.py:217
  3.3 0.1 pad_maximum_fusion
  3.4 5.5 %collective-permute-start = (f32[1544,256]{1,0:T(8,128)S(1)}, f32[1544,256]{1,0:T(8,128)}, u32[]{:S(2)}, u32[]{:S(2)}) collective-permute-start(f32[1544,256]{1,0:T(8,128)S(1)} %pad_maximum_fusion), channel_id=1, source_target_pairs={{0,30},{2,28},{4,2},{6,0},{8,6},{10,4},{12,10},{14,8},{16,14},{18,... | collective-permute-start | bytes 4743176 | tf_op jit(solution)/shard_map/ppermute | solution.py:220
  8.8 0.1 copy.19
  8.9 0.1 convert_element_type.46
  9.0 1.2 pad_maximum_fusion.1
  10.3 0.8 collective-permute-start.2
  11.1 1.5 %collective-permute-start.6 = (f32[5120,256]{1,0:T(8,128)}, f32[5120,256]{1,0:T(8,128)}, u32[]{:S(2)}, u32[]{:S(2)}) collective-permute-start(f32[5120,256]{1,0:T(8,128)} %bitcast.35), channel_id=1, source_target_pairs={{0,1},{1,0},{2,3},{3,2},{4,5},{5,4},{6,7},{7,6},{8,9},{9,8},{10,11... | collective-permute-start | bytes 15728648 | tf_op jit(solution)/shard_map/ppermute | solution.py:203
  12.6 0.1 copy.17
  12.7 0.1 reshape_squeeze.22
  12.8 0.6 reshape.87.refs_1_
  13.4 30.4 %collective-permute-done.refs_2_.refs_3_.refs_5_ = f32[1544,256]{1,0:T(8,128)} collective-permute-done((f32[1544,256]{1,0:T(8,128)S(1)}, f32[1544,256]{1,0:T(8,128)}, u32[]{:S(2)}, u32[]{:S(2)}) %collective-permute-start) | collective-permute-done | bytes 1581088 | tf_op jit(solution)/shard_map/ppermute | solution.py:220
  43.8 3.7 %pack.1 = f32[3080,256]{1,0:T(8,128)} custom-call(f32[3072,256]{1,0:T(8,128)} %bitcast.32, f32[8,256]{1,0:T(8,128)} %reshape.87.refs_1_, f32[1544,256]{1,0:T(8,128)} %collective-permute-done.refs_2_.refs_3_.refs_5_), custom_call_target="tpu_custom_call" | custom-call | bytes 6291456 | tf_op jit(solution)/shard_map/pack/pallas_call | solution.py:43
  47.6 1.5 %collective-permute-start.1 = (f32[3080,256]{1,0:T(8,128)}, f32[3080,256]{1,0:T(8,128)}, u32[]{:S(2)}, u32[]{:S(2)}) collective-permute-start(f32[3080,256]{1,0:T(8,128)} %pack.1), channel_id=1, source_target_pairs={{0,26},{2,0},{4,30},{6,4},{8,2},{10,8},{12,6},{14,12},{16,10},{18,... | collective-permute-start | bytes 9461768 | tf_op jit(solution)/shard_map/ppermute | solution.py:270
  49.0 0.1 copy.20
  49.1 0.1 reshape_squeeze.23
  49.2 1.6 %collective-permute-start.5 = (s32[40]{0:T(128)S(1)}, s32[40]{0:T(128)S(1)}, u32[]{:S(2)}, u32[]{:S(2)}) collective-permute-start(s32[40]{0:T(128)S(1)} %reshape_squeeze.23), channel_id=1, source_target_pairs={{0,1},{1,0},{2,3},{3,2},{4,5},{5,4},{6,7},{7,6},{8,9},{9,8},{10,11... | collective-permute-start | bytes 488 | tf_op jit(solution)/shard_map/ppermute | solution.py:204
  50.8 27.0 %collective-permute-done.2.refs_4_.refs_6_ = f32[1544,256]{1,0:T(8,128)} collective-permute-done((f32[1544,256]{1,0:T(8,128)}, f32[1544,256]{1,0:T(8,128)}, u32[]{:S(2)}, u32[]{:S(2)}) %collective-permute-start.2) | collective-permute-done | bytes 1581088 | tf_op jit(solution)/shard_map/ppermute | solution.py:220
  77.8 0.1 collective-permute-start.4
  77.9 0.7 fusion.2
  83.7 0.1 copy.22
  83.8 0.1 reshape_squeeze.25
  83.9 0.1 copy.21
  84.0 0.1 reshape_squeeze.24
  84.1 0.1 copy.16
  84.2 0.1 reshape_squeeze.10
  84.3 0.7 slice_bitcast_fusion.3
  85.0 0.7 slice_bitcast_fusion.2
  85.7 0.7 slice_bitcast_fusion.1
  86.4 0.7 slice_bitcast_fusion
  87.2 1.9 %concatenate.19.refs_0_ = s32[163]{0:T(256)S(1)} concatenate(s32[20]{0:T(128)S(1)} %reshape_squeeze.10, s32[20]{0:T(128)S(1)} %reshape_squeeze.24, s32[1]{0:T(128)} %bitcast, s32[24]{0:T(128)S(1)} %reshape_squeeze.22, s32[1]{0:T(128)} %bitcast.14, s32[12]{0:T(128)S(1)} %slice_convert_fusion.5, s32[1]{0:T(128)} %bitcast.14, s32[12]{0:T(128)S(1)} %slice_convert_fusion.4, ...), dimensions={0} | concatenate | bytes 1304 | tf_op jit(solution)/shard_map/concatenate | solution.py:161
  89.1 2.5 %copy-done.5 = f32[1,1,2,10,256,256]{5,4,3,2,1,0:T(8,128)S(1)} copy-done((f32[1,1,2,10,256,256]{5,4,3,2,1,0:T(8,128)S(1)}, f32[1,1,2,10,256,256]{5,4,3,2,1,0:T(8,128)}, u32[]{:S(2)}) %copy-start.5) | copy-done | bytes 5242904
  91.6 7.7 %multiply.3.refs_3_ = f32[11,256,256]{2,1,0:T(8,128)S(1)} custom-call(s32[163]{0:T(256)S(1)} %concatenate.19.refs_0_, f32[5120,256]{1,0:T(8,128)S(1)} %bitcast.36, f32[3072,256]{1,0:T(8,128)S(1)} %bitcast.33, f32[1544,256]{1,0:T(8,128)} %collective-permute-done.refs_2_.refs_3_.refs_5_, f32[1544,256]{1,0:T(8,128)} %collective-permute-done.2.refs_4_.refs_6_, ...), custom_call_target="tpu_custom_call" | custom-call | flops 5000000000 | bytes 4194304 | tf_op jit(solution)/shard_map/multiply/pallas_call | solution.py:175
  99.3 1.6 %copy-done.1 = f32[11,256,256]{2,1,0:T(8,128)} copy-done((f32[11,256,256]{2,1,0:T(8,128)}, f32[11,256,256]{2,1,0:T(8,128)S(1)}, u32[]{:S(2)}) %copy-start.1) | copy-done | bytes 2883608
  100.9 10.7 %collective-permute-done.1.refs_2_.refs_4_ = f32[3080,256]{1,0:T(8,128)} collective-permute-done((f32[3080,256]{1,0:T(8,128)}, f32[3080,256]{1,0:T(8,128)}, u32[]{:S(2)}, u32[]{:S(2)}) %collective-permute-start.1) | collective-permute-done | bytes 3153952 | tf_op jit(solution)/shard_map/ppermute | solution.py:270
  111.6 0.7 slice_bitcast_fusion.4
  112.3 0.1 concatenate.18.refs_0_
  112.4 1.8 %copy-done.2 = f32[11,256,256]{2,1,0:T(8,128)S(1)} copy-done((f32[11,256,256]{2,1,0:T(8,128)S(1)}, f32[11,256,256]{2,1,0:T(8,128)}, u32[]{:S(2)}) %copy-start.2) | copy-done | bytes 2883608
  114.2 2.5 %copy-done.6 = f32[1,1,2,10,256,256]{5,4,3,2,1,0:T(8,128)S(1)} copy-done((f32[1,1,2,10,256,256]{5,4,3,2,1,0:T(8,128)S(1)}, f32[1,1,2,10,256,256]{5,4,3,2,1,0:T(8,128)}, u32[]{:S(2)}) %copy-start.6) | copy-done | bytes 5242904
  116.7 5.6 %multiply.4.refs_9_ = f32[11,256,256]{2,1,0:T(8,128)S(1)} custom-call(s32[110]{0:T(128)S(1)} %concatenate.18.refs_0_, f32[5120,256]{1,0:T(8,128)S(1)} %bitcast.37, f32[3080,256]{1,0:T(8,128)} %collective-permute-done.1.refs_2_.refs_4_, f32[11,256,256]{2,1,0:T(8,128)S(1)} %copy-done.2), custom_call_target="tpu_custom_call", output_to_operand_aliasing={{}: (3, {})} | custom-call | flops 5000000000 | bytes 4194304 | tf_op jit(solution)/shard_map/multiply/pallas_call | solution.py:175
  122.3 1.6 %copy-done.3 = f32[11,256,256]{2,1,0:T(8,128)} copy-done((f32[11,256,256]{2,1,0:T(8,128)}, f32[11,256,256]{2,1,0:T(8,128)S(1)}, u32[]{:S(2)}) %copy-start.3) | copy-done | bytes 2883608
  123.9 0.1 concatenate.17.refs_0_
  124.0 2.2 %collective-permute-done.5.refs_1_ = s32[40]{0:T(128)S(1)} collective-permute-done((s32[40]{0:T(128)S(1)}, s32[40]{0:T(128)S(1)}, u32[]{:S(2)}, u32[]{:S(2)}) %collective-permute-start.5) | collective-permute-done | bytes 192 | tf_op jit(solution)/shard_map/ppermute | solution.py:204
  126.2 1.8 %copy-done.4 = f32[11,256,256]{2,1,0:T(8,128)S(1)} copy-done((f32[11,256,256]{2,1,0:T(8,128)S(1)}, f32[11,256,256]{2,1,0:T(8,128)}, u32[]{:S(2)}) %copy-start.4) | copy-done | bytes 2883608
  128.1 14.4 %multiply.5 = (f32[11,256,256]{2,1,0:T(8,128)S(1)}, f32[10,256,256]{2,1,0:T(8,128)}) custom-call(s32[173]{0:T(256)S(1)} %concatenate.17.refs_0_, s32[40]{0:T(128)S(1)} %collective-permute-done.5.refs_1_, f32[5120,256]{1,0:T(8,128)} %collective-permute-done.6.refs_2_, f32[3072,256]{1,0:T(8,128)S(1)} %bitcast.34, ...), custom_call_target="tpu_custom_call", output_to_operand_aliasing={{0}: (9, {})} | custom-call | flops 5000000000 | bytes 4194304 | tf_op jit(solution)/shard_map/multiply/pallas_call | solution.py:175
  (38 shorter events, 0.1 us)
Async XLA Ops:
  3.4 40.4 %collective-permute-start = (f32[1544,256]{1,0:T(8,128)S(1)}, f32[1544,256]{1,0:T(8,128)}, u32[]{:S(2)}, u32[]{:S(2)}) collective-permute-start(f32[1544,256]{1,0:T(8,128)S(1)} %pad_maximum_fusion), channel_id=1, source_target_pairs={{0,30},{2,28},{4,2},{6,0},{8,6},{10,4},{12,10},{14,8},{16,14},{18,... | collective-permute-start | bytes 4743176 | tf_op jit(solution)/shard_map/ppermute | solution.py:220
  9.0 3.6 %copy-start.7 = (s32[1,1,12,2]{2,3,1,0:T(2,128)S(1)}, s32[1,1,12,2]{2,3,1,0:T(2,128)}, u32[]{:S(2)}) copy-start(s32[1,1,12,2]{2,3,1,0:T(2,128)} %param.9) | copy-start | bytes 292
  10.3 67.5 %collective-permute-start.2 = (f32[1544,256]{1,0:T(8,128)}, f32[1544,256]{1,0:T(8,128)}, u32[]{:S(2)}, u32[]{:S(2)}) collective-permute-start(f32[1544,256]{1,0:T(8,128)} %pad_maximum_fusion.1), channel_id=1, source_target_pairs={{0,30},{2,28},{4,2},{6,0},{8,6},{10,4},{12,10},{14,8},{16,14},{18,... | collective-permute-start | bytes 4743176 | tf_op jit(solution)/shard_map/ppermute | solution.py:220
  11.1 115.1 %collective-permute-start.6 = (f32[5120,256]{1,0:T(8,128)}, f32[5120,256]{1,0:T(8,128)}, u32[]{:S(2)}, u32[]{:S(2)}) collective-permute-start(f32[5120,256]{1,0:T(8,128)} %bitcast.35), channel_id=1, source_target_pairs={{0,1},{1,0},{2,3},{3,2},{4,5},{5,4},{6,7},{7,6},{8,9},{9,8},{10,11... | collective-permute-start | bytes 15728648 | tf_op jit(solution)/shard_map/ppermute | solution.py:203
  43.8 5.2 %copy-start.8 = (s32[1,1,2,10,2]{3,4,2,1,0:T(2,128)S(1)}, s32[1,1,2,10,2]{3,4,2,1,0:T(2,128)}, u32[]{:S(2)}) copy-start(s32[1,1,2,10,2]{3,4,2,1,0:T(2,128)} %param.7) | copy-start | bytes 484
  43.8 34.1 %copy-start.10 = (s32[1,4]{1,0:T(1,128)S(1)}, s32[1,4]{1,0:T(1,128)}, u32[]{:S(2)}) copy-start(s32[1,4]{1,0:T(1,128)} %param.11) | copy-start | bytes 52
  43.8 40.3 %copy-start.9 = (s32[1,1,10,2]{2,3,1,0:T(2,128)S(1)}, s32[1,1,10,2]{2,3,1,0:T(2,128)}, u32[]{:S(2)}) copy-start(s32[1,1,10,2]{2,3,1,0:T(2,128)} %param.10) | copy-start | bytes 244
  43.8 45.3 %copy-start = (f32[1,1,12,256,256]{4,3,2,1,0:T(8,128)S(1)}, f32[1,1,12,256,256]{4,3,2,1,0:T(8,128)}, u32[]{:S(2)}) copy-start(f32[1,1,12,256,256]{4,3,2,1,0:T(8,128)} %param.8) | copy-start | bytes 9437188
  47.6 64.0 %collective-permute-start.1 = (f32[3080,256]{1,0:T(8,128)}, f32[3080,256]{1,0:T(8,128)}, u32[]{:S(2)}, u32[]{:S(2)}) collective-permute-start(f32[3080,256]{1,0:T(8,128)} %pack.1), channel_id=1, source_target_pairs={{0,26},{2,0},{4,30},{6,4},{8,2},{10,8},{12,6},{14,12},{16,10},{18,... | collective-permute-start | bytes 9461768 | tf_op jit(solution)/shard_map/ppermute | solution.py:270
  49.0 36.7 %collective-permute-start.3 = (f32[1544,256]{1,0:T(8,128)}, f32[1544,256]{1,0:T(8,128)}, u32[]{:S(2)}, u32[]{:S(2)}) collective-permute-start(f32[1544,256]{1,0:T(8,128)} %collective-permute-done.refs_2_.refs_3_.refs_5_), channel_id=1, source_target_pairs={{0,2},{2,0},{4,6},{6,4},{8,10},{10,8},{12,14},{14,12},{16,18},{18,... | collective-permute-start | bytes 4743176 | tf_op jit(solution)/shard_map/ppermute | solution.py:220
  49.2 77.0 %collective-permute-start.5 = (s32[40]{0:T(128)S(1)}, s32[40]{0:T(128)S(1)}, u32[]{:S(2)}, u32[]{:S(2)}) collective-permute-start(s32[40]{0:T(128)S(1)} %reshape_squeeze.23), channel_id=1, source_target_pairs={{0,1},{1,0},{2,3},{3,2},{4,5},{5,4},{6,7},{7,6},{8,9},{9,8},{10,11... | collective-permute-start | bytes 488 | tf_op jit(solution)/shard_map/ppermute | solution.py:204
  77.8 8.7 %collective-permute-start.4 = (f32[1544,256]{1,0:T(8,128)}, f32[1544,256]{1,0:T(8,128)}, u32[]{:S(2)}, u32[]{:S(2)}) collective-permute-start(f32[1544,256]{1,0:T(8,128)} %collective-permute-done.2.refs_4_.refs_6_), channel_id=1, source_target_pairs={{0,2},{2,0},{4,6},{6,4},{8,10},{10,8},{12,14},{14,12},{16,18},{18,... | collective-permute-start | bytes 4743176 | tf_op jit(solution)/shard_map/ppermute | solution.py:220
  89.1 2.5 %copy-start.5 = (f32[1,1,2,10,256,256]{5,4,3,2,1,0:T(8,128)S(1)}, f32[1,1,2,10,256,256]{5,4,3,2,1,0:T(8,128)}, u32[]{:S(2)}) copy-start(f32[1,1,2,10,256,256]{5,4,3,2,1,0:T(8,128)} %param.6) | copy-start | bytes 15728644
  99.3 1.6 %copy-start.1 = (f32[11,256,256]{2,1,0:T(8,128)}, f32[11,256,256]{2,1,0:T(8,128)S(1)}, u32[]{:S(2)}) copy-start(f32[11,256,256]{2,1,0:T(8,128)S(1)} %multiply.3.refs_3_) | copy-start | bytes 8650756
  112.4 1.8 %copy-start.2 = (f32[11,256,256]{2,1,0:T(8,128)S(1)}, f32[11,256,256]{2,1,0:T(8,128)}, u32[]{:S(2)}) copy-start(f32[11,256,256]{2,1,0:T(8,128)} %copy-done.1) | copy-start | bytes 8650756
  114.2 2.5 %copy-start.6 = (f32[1,1,2,10,256,256]{5,4,3,2,1,0:T(8,128)S(1)}, f32[1,1,2,10,256,256]{5,4,3,2,1,0:T(8,128)}, u32[]{:S(2)}) copy-start(f32[1,1,2,10,256,256]{5,4,3,2,1,0:T(8,128)} %param.6) | copy-start | bytes 15728644
  122.3 1.7 %copy-start.3 = (f32[11,256,256]{2,1,0:T(8,128)}, f32[11,256,256]{2,1,0:T(8,128)S(1)}, u32[]{:S(2)}) copy-start(f32[11,256,256]{2,1,0:T(8,128)S(1)} %multiply.4.refs_9_) | copy-start | bytes 8650756
  126.2 1.8 %copy-start.4 = (f32[11,256,256]{2,1,0:T(8,128)S(1)}, f32[11,256,256]{2,1,0:T(8,128)}, u32[]{:S(2)}) copy-start(f32[11,256,256]{2,1,0:T(8,128)} %copy-done.3) | copy-start | bytes 8650756

commit v4 on v0

v4 whole, which is shorter than its diff:
```python
import functools

import jax
import jax.numpy as jnp
from jax import lax
from jax.experimental import pallas as pl
from jax.experimental.pallas import tpu as pltpu
from jax.sharding import PartitionSpec as P

RB = 3
KB = 4
CB = 4
STEPS = 4
UNROLL = 4
LIST_ROWS = 8
X_PARTS = 3
VMEM = pl.BlockSpec(memory_space=pltpu.VMEM)
SMEM = pl.BlockSpec(memory_space=pltpu.SMEM)


def pack_kernel(share, places, x, *refs):
    *targets, sems = refs
    n_x, bs = places.shape[0], x.shape[-1]
    cuts = [(0, n_x)] + [(p * share, share) for p in range(n_x // share)]
    copies = [
        pltpu.make_async_copy(x.at[pl.ds(first * bs, n * bs)], target.at[pl.ds(0, n * bs)], sems.at[i])
        for i, (target, (first, n)) in enumerate(zip(targets, cuts))
    ]
    for copy in copies:
        copy.start()
    lane = lax.broadcasted_iota(jnp.int32, (LIST_ROWS, bs), 1)
    for target, (first, n) in zip(targets, cuts):
        rows = jnp.zeros((LIST_ROWS, bs), jnp.float32)
        for j in range(n):
            for d in range(2):
                rows = jnp.where(lane == 2 * j + d, places[first + j, d].astype(jnp.float32), rows)
        target[n * bs : n * bs + LIST_ROWS] = rows
    for copy in copies:
        copy.wait()


def pack(x, places, share):
    n_x, bs = places.shape[0], x.shape[-1]
    sizes = [n_x] + [share] * (n_x // share)
    return pl.pallas_call(
        functools.partial(pack_kernel, share),
        in_specs=[SMEM, pl.BlockSpec(memory_space=pl.ANY)],
        out_specs=[VMEM] * len(sizes),
        out_shape=[jax.ShapeDtypeStruct((n * bs + LIST_ROWS, bs), x.dtype) for n in sizes],
        scratch_shapes=[pltpu.SemaphoreType.DMA((len(sizes),))],
        compiler_params=pltpu.CompilerParams(vmem_limit_bytes=16 * 2**20),
        cost_estimate=pl.CostEstimate(flops=0, bytes_accessed=2**20, transcendentals=0),
        name="pack",
    )(places, x)


def halves(values):
    high = values.astype(jnp.bfloat16)
    return high, (values - high.astype(jnp.float32)).astype(jnp.bfloat16)


def dot(left, right):
    return jnp.dot(left, right, preferred_element_type=jnp.float32)


def block(rows, index, bs):
    return rows[pl.ds(pl.multiple_of(index * bs, bs), bs), :]


def fill_map(target, size, read, count, columns):
    for cell in range(size):
        target[cell] = -1
    for entry in range(count):
        target[read(entry, 0) * columns + read(entry, 1)] = entry


def add_products(acc, n_out, bs, maps, todo, left_place, n_left, left, first, right):
    r_map, o_map = maps

    def collect(i, count):
        row, k = left_place(i)
        for c in range(CB):
            j, m = r_map[k * CB + c], o_map[row * CB + c]
            todo[count] = (i * 64 + jnp.maximum(j, 0)) * 64 + jnp.maximum(m, 0)
            count = count + ((j >= 0) & (m >= 0)).astype(jnp.int32)
        return count

    count = lax.fori_loop(0, n_left, collect, jnp.int32(0))
    for u in range(UNROLL):
        todo[count + u] = n_out

    def several(q, carry):
        for u in range(UNROLL):
            code = todo[q * UNROLL + u]
            i, j, m = code // 4096, (code // 64) % 64, code % 64
            left_high, left_low = halves(block(left, first + i, bs))
            right_high, right_low = right(j)
            acc[m] += dot(left_high, right_high) + dot(left_high, right_low) + dot(left_low, right_high)
        return carry

    lax.fori_loop(0, (count + UNROLL - 1) // UNROLL, several, 0)


def own_kernel(slot, n_left, n_x, plan, n_arrays, chooses, owner, pairs, left_list, left, *refs):
    arrays, refs = refs[:n_arrays], refs[n_arrays:]
    before, refs = (refs[0], refs[1:]) if slot and chooses else (None, refs)
    acc, refs = refs[0], refs[1:]
    if chooses:
        chosen, chosen_list, refs = refs[0], refs[1], refs[2:]
    here_lists, there_lists, refs = refs[:X_PARTS], refs[X_PARTS : 2 * X_PARTS], refs[2 * X_PARTS :]
    left_rows, here_rows, there_rows, r_map, o_map, todo, sems = refs
    n_out, bs = pairs.shape[0], left.shape[-1]
    place, column = lax.axis_index("loop") % 4, lax.axis_index("bcast")

    own_copies = [pltpu.make_async_copy(left.at[pl.ds(slot * n_left * bs, n_left * bs)], left_rows, sems.at[0])]
    if before is not None:
        own_copies.append(pltpu.make_async_copy(before, acc, sems.at[1]))
    for copy in own_copies:
        copy.start()

    def fetch(at, parts, rows, lists):
        copies = []
        for p, array in enumerate(parts):
            n = n_x // len(parts)
            right = arrays[array]
            target = rows.at[pl.ds(p * n * bs, n * bs)]
            copies.append(pltpu.make_async_copy(right.at[pl.ds(0, n * bs)], target, sems.at[at + 2 * p]))
            listed = right.at[pl.ds(n * bs, LIST_ROWS)]
            copies.append(pltpu.make_async_copy(listed, lists[p], sems.at[at + 2 * p + 1]))
        return copies

    def place_in(lists, count):
        n = n_x // count
        return lambda j, d: lists[j // n][0, 2 * (j % n) + d].astype(jnp.int32)

    def each(then):
        for step, places, parts in plan:
            applies = functools.reduce(jnp.logical_or, [place == value for value in places])
            mine = owner[step] == column if chooses else True
            pl.when(applies & mine)(functools.partial(then, parts, True))
            if chooses:
                pl.when(applies & jnp.logical_not(mine))(functools.partial(then, parts, False))

    def start(parts, here):
        for copy in fetch(2, parts, here_rows, here_lists) if here else fetch(
            2 + 2 * X_PARTS, parts, there_rows, there_lists
        ):
            copy.start()

    def land(wanted, parts, here):
        if here != wanted:
            return
        if here:
            for copy in fetch(2, parts, here_rows, here_lists):
                copy.wait()
            fill_map(r_map, KB * CB, place_in(here_lists, len(parts)), n_x, CB)
            return
        for copy in fetch(2 + 2 * X_PARTS, parts, there_rows, there_lists):
            copy.wait()
        read = place_in(there_lists, len(parts))
        for j in range(n_x):
            for d in range(2):
                chosen_list[2 * j + d] = read(j, d)

    def left_place(i):
        return left_list[slot * n_left + i, 0], left_list[slot * n_left + i, 1]

    each(start)
    fill_map(o_map, RB * CB, lambda m, d: pairs[m, d], n_out, CB)
    if before is None:
        acc[...] = jnp.zeros_like(acc)
    each(functools.partial(land, True))
    for copy in own_copies:
        copy.wait()
    add_products(
        acc, n_out, bs, (r_map, o_map), todo, left_place, n_left, left_rows, 0, lambda j: halves(block(here_rows, j, bs))
    )
    if chooses:
        each(functools.partial(land, False))

        def split(j, carry):
            chosen[j, 0], chosen[j, 1] = halves(block(there_rows, j, bs))
            return carry

        lax.fori_loop(0, n_x, split, 0)


def own_products(owner, pairs, left, slot, left_list, n_left, choices, before, chooses):
    bs, n_out = left.shape[-1], pairs.shape[0]
    arrays, plan = [], []
    for step, places, parts in choices:
        at = []
        for part in parts:
            known = [i for i, other in enumerate(arrays) if other is part]
            if not known:
                known = [len(arrays)]
                arrays.append(part)
            at.append(known[0])
        plan.append((step, places, at))
    n_x = sum(part.shape[0] // bs for part in choices[0][2])
    anywhere = pl.BlockSpec(memory_space=pl.ANY)
    operands = [left, *arrays] + ([before] if slot and chooses else [])
    out_shape, out_specs = [jax.ShapeDtypeStruct((n_out + 1, bs, bs), jnp.float32)], [VMEM]
    if chooses:
        out_shape.append(jax.ShapeDtypeStruct((n_x, 2, bs, bs), jnp.bfloat16))
        out_shape.append(jax.ShapeDtypeStruct((2 * n_x,), jnp.int32))
        out_specs += [VMEM, SMEM]
    return pl.pallas_call(
        functools.partial(own_kernel, slot, n_left, n_x, plan, len(arrays), chooses),
        in_specs=[SMEM] * 3 + [anywhere] * len(operands),
        out_specs=out_specs,
        out_shape=out_shape,
        scratch_shapes=[pltpu.SMEM((LIST_ROWS, bs), jnp.float32)] * (2 * X_PARTS)
        + [
            pltpu.VMEM((n_left * bs, bs), jnp.float32),
            pltpu.VMEM((n_x * bs, bs), jnp.float32),
            pltpu.VMEM((n_x * bs, bs), jnp.float32),
            pltpu.SMEM(((KB + 1) * CB,), jnp.int32),
            pltpu.SMEM((RB * CB,), jnp.int32),
            pltpu.SMEM((n_left * CB + UNROLL,), jnp.int32),
            pltpu.SemaphoreType.DMA((2 + 4 * X_PARTS,)),
        ],
        compiler_params=pltpu.CompilerParams(vmem_limit_bytes=OWN_LIMIT),
        cost_estimate=pl.CostEstimate(flops=0, bytes_accessed=2**20, transcendentals=0),
        name="own_products",
    )(owner, pairs, left_list, *operands)


OWN_LIMIT = 32 * 2**20
LAST_LIMIT = 24 * 2**20


def last_kernel(depth, n_left, n_x, pairs, late, *refs):
    right_lists, refs = refs[:depth], refs[depth:]
    left, before, chosen, refs = refs[0], refs[1], refs[2 : depth + 2], refs[depth + 2 :]
    out, acc, left_rows, r_map, o_map, todo, sems = refs
    n_out, bs = pairs.shape[0], left.shape[-1]
    size = n_left * bs
    fetched = [
        pltpu.make_async_copy(left.at[pl.ds(slot * size, size)], left_rows.at[pl.ds(slot * size, size)], sems.at[slot])
        for slot in range(depth)
    ]
    for copy in fetched:
        copy.start()
    for m in range(n_out):
        acc[m] = before[m]
    fill_map(o_map, RB * CB, lambda m, d: pairs[m, d], n_out, CB)
    for slot in range(depth):
        fill_map(r_map, KB * CB, lambda j, d: right_lists[slot][2 * j + d], n_x, CB)
        fetched[slot].wait()
        add_products(
            acc, n_out, bs, (r_map, o_map), todo,
            lambda i: (late[2 * (slot * n_left + i)], late[2 * (slot * n_left + i) + 1]),
            n_left, left_rows, slot * n_left,
            lambda j: (chosen[slot][j, 0], chosen[slot][j, 1]),
        )
    copies = [pltpu.make_async_copy(acc.at[m], out.at[m], sems.at[depth + m]) for m in range(n_out)]
    for copy in copies:
        copy.start()
    for copy in copies:
        copy.wait()


def last_products(pairs, late, right_lists, left, n_left, before, chosen):
    bs = left.shape[-1]
    n_out, n_x, depth = pairs.shape[0], chosen[0].shape[0], len(chosen)
    anywhere = pl.BlockSpec(memory_space=pl.ANY)
    return pl.pallas_call(
        functools.partial(last_kernel, depth, n_left, n_x),
        in_specs=[SMEM] * (2 + depth) + [anywhere] + [VMEM] * (1 + depth),
        out_specs=anywhere,
        out_shape=jax.ShapeDtypeStruct((n_out, bs, bs), jnp.float32),
        scratch_shapes=[
            pltpu.VMEM((n_out + 1, bs, bs), jnp.float32),
            pltpu.VMEM((depth * n_left * bs, bs), jnp.float32),
            pltpu.SMEM(((KB + 1) * CB,), jnp.int32),
            pltpu.SMEM((RB * CB,), jnp.int32),
            pltpu.SMEM((n_left * CB + UNROLL,), jnp.int32),
            pltpu.SemaphoreType.DMA((depth + n_out,)),
        ],
        compiler_params=pltpu.CompilerParams(vmem_limit_bytes=LAST_LIMIT),
        cost_estimate=pl.CostEstimate(flops=0, bytes_accessed=2**20, transcendentals=0),
        name="last_products",
    )(pairs, late, *right_lists, left, before, *chosen)


def per_device(s_blocks, s_list, x_blocks, x_list, c_list, owner):
    length, width = lax.axis_size("loop"), lax.axis_size("bcast")
    pairs, owner = c_list[0, 0], owner[0]
    depth, n_s, bs = s_blocks.shape[2], s_blocks.shape[3], s_blocks.shape[-1]
    n_x = x_blocks.shape[2]
    s_own, x_own = s_blocks.reshape(depth * n_s * bs, bs), x_blocks.reshape(n_x * bs, bs)
    s_own_list, x_own_list = s_list.reshape(depth * n_s, 2), x_list[0, 0]

    swapped = width == 2
    if swapped:
        partner = [(0, 1), (1, 0)]
        came = lax.ppermute(s_own, "bcast", partner)
        their_list = lax.ppermute(s_own_list.reshape(-1), "bcast", partner)
    else:
        held = lax.all_gather(s_own, "bcast")
        held_lists = lax.all_gather(s_own_list, "bcast")

    share = n_x // X_PARTS
    everything, *parts = pack(x_own, x_own_list, share)

    def moved(packed, to):
        return [lax.ppermute(part, "loop", [(g, (g + to[g % 4]) % length) for g in range(length)]) for part in packed]

    first = moved(parts, (-1, 1, -1, -3))
    second = moved(first, (1, -1, -3, -1))
    third = [lax.ppermute(part, "loop", [(g, g - 1) for g in range(3, length, 4)]) for part in second]
    other = moved([everything], (-3, -1, -3, -1))

    choices = [
        (0, (0, 1, 2, 3), [everything]),
        (1, (1, 3), first),
        (1, (0, 2), other),
        (2, (0, 1, 2, 3), second),
        (3, (0,), first),
        (3, (2,), third),
        (3, (1, 3), other),
    ]

    if not swapped:
        total = 0
        for step in range(STEPS):
            piece = lax.dynamic_index_in_dim(held, owner[step], 0, False)
            places = lax.dynamic_index_in_dim(held_lists, owner[step], 0, False)
            fit = [choice for choice in choices if choice[0] == step]
            total = total + own_products(owner, pairs, piece, step // width, places, n_s, fit, None, False)[0]
        return total[None, None, : pairs.shape[0]]

    acc, chosen, right_lists = None, [], []
    for slot in range(depth):
        fit = [choice for choice in choices if choice[0] // width == slot]
        acc, split, places = own_products(owner, pairs, s_own, slot, s_own_list, n_s, fit, acc, True)
        chosen.append(split)
        right_lists.append(places)
    return last_products(pairs, their_list, right_lists, came, n_s, acc, chosen)[None, None]


def solution(mesh):
    return jax.shard_map(
        per_device,
        mesh=mesh,
        in_specs=(
            P("loop", "bcast", None, None, None, None),
            P("loop", "bcast", None, None, None),
            P("loop", "bcast", None, None, None),
            P("loop", "bcast", None, None),
            P("loop", "bcast", None, None),
            P("loop", None),
        ),
        out_specs=P("loop", "bcast", None, None, None),
        check_vma=False,
    )
```

time: 399 us -> 133 us (0.33)
  the two profiles are of different devices: /device:TPU:0 before, /device:TPU:27 now
where the time goes in v4:
time: 133 us; the launch traced here: 132 us
  starting transfers between devices  49.6 us (37%)
  waiting for transfers between devices  37.1 us (28%)
  Pallas kernels  30.1 us (23%)
  local copies, waits for them, and re-layouts  15.6 us (12%)
    ppermute x7, starting transfers between devices, moved(): lax.ppermute(part, 'loop', [(g, (g + to[g % 4]) % length) for g in range(...  40.6 us
    ppermute x7, waiting for transfers between devices, moved(): lax.ppermute(part, 'loop', [(g, (g + to[g % 4]) % length) for g in range(...  37.1 us
    pallas_call x2, Pallas kernels, own_products(): pl.pallas_call(functools.partial(own_kernel, slot, n_left, n_x, plan, len...  15.2 us
    unnamed x34, local copies, waits for them, and re-layouts  14.5 us
    pallas_call x1, Pallas kernels, last_products(): pl.pallas_call(functools.partial(last_kernel, depth, n_left, n_x), in_spe...  12 us
    ppermute x3, starting transfers between devices, per_device(): lax.ppermute(part, 'loop', [(g, g - 1) for g in range(3, length, 4)])  7.48 us
    pallas_call x1, Pallas kernels, pack(): pl.pallas_call(functools.partial(pack_kernel, share), in_specs=[SMEM, pl....  2.85 us
  transfers between devices with their start and end apart: 12, of which 3 were waited for; matrix products, arithmetic and copies ran while one was open for 1% of the time, Pallas kernels for 14%

profile of v4, /device:TPU:27, one launch (start us, length us, event | category | flops | bytes accessed | tf_op | source)
XLA Modules:
  0.0 132.5 jit_solution(10961710797527234401)
XLA Ops:
  0.0 1.2 collective-permute-start.11
  1.2 0.8 copy.17.places
  2.0 1.9 %copy-done.10 = f32[1,1,12,256,256]{4,3,2,1,0:T(8,128)S(1)} copy-done((f32[1,1,12,256,256]{4,3,2,1,0:T(8,128)S(1)}, f32[1,1,12,256,256]{4,3,2,1,0:T(8,128)}, u32[]{:S(2)}) %copy-start.10) | copy-done | bytes 3145752
  3.9 2.9 %pack.1 = (f32[3080,256]{1,0:T(8,128)}, f32[1032,256]{1,0:T(8,128)S(1)}, f32[1032,256]{1,0:T(8,128)S(1)}, f32[1032,256]{1,0:T(8,128)S(1)}) custom-call(s32[12,2]{1,0:T(8,128)S(1)} %copy.17.places, f32[3072,256]{1,0:T(8,128)S(1)} %bitcast.11), custom_call_target="tpu_custom_call" | custom-call | bytes 1048576 | tf_op jit(solution)/shard_map/pack/pallas_call | solution.py:45
  6.8 1.1 collective-permute-start.3
  7.9 0.5 collective-permute-start.1
  8.5 1.1 collective-permute-start.2
  9.5 0.0 collective-permute-start.4
  9.6 21.4 %collective-permute-done.3.refs_3_.refs_5_ = f32[1032,256]{1,0:T(8,128)S(1)} collective-permute-done((f32[1032,256]{1,0:T(8,128)S(1)}, f32[1032,256]{1,0:T(8,128)S(1)}, u32[]{:S(2)}, u32[]{:S(2)}) %collective-permute-start.3) | collective-permute-done | bytes 1056800 | tf_op jit(solution)/shard_map/ppermute | solution.py:308
  31.0 25.0 %collective-permute-start.7 = (f32[1032,256]{1,0:T(8,128)S(1)}, f32[1032,256]{1,0:T(8,128)}, u32[]{:S(2)}, u32[]{:S(2)}) collective-permute-start(f32[1032,256]{1,0:T(8,128)S(1)} %collective-permute-done.3.refs_3_.refs_5_), channel_id=1, source_target_pairs={{0,2},{2,0},{4,30},{6,4},{8,10},{10,8},{12,6},{14,12},{16,18},{18,... | collective-permute-start | bytes 3170312 | tf_op jit(solution)/shard_map/ppermute | solution.py:308
  56.1 1.0 copy-done.1
  57.0 0.0 collective-permute-done.1.refs_1_.refs_3_
  57.0 10.3 %collective-permute-start.5 = (f32[1032,256]{1,0:T(8,128)S(1)}, f32[1032,256]{1,0:T(8,128)}, u32[]{:S(2)}, u32[]{:S(2)}) collective-permute-start(f32[1032,256]{1,0:T(8,128)S(1)} %collective-permute-done.1.refs_1_.refs_3_), channel_id=1, source_target_pairs={{0,2},{2,0},{4,30},{6,4},{8,10},{10,8},{12,6},{14,12},{16,18},{18,... | collective-permute-start | bytes 3170312 | tf_op jit(solution)/shard_map/ppermute | solution.py:308
  67.4 1.0 copy-done.4
  68.4 8.0 %collective-permute-done.2.refs_2_.refs_4_ = f32[1032,256]{1,0:T(8,128)S(1)} collective-permute-done((f32[1032,256]{1,0:T(8,128)S(1)}, f32[1032,256]{1,0:T(8,128)S(1)}, u32[]{:S(2)}, u32[]{:S(2)}) %collective-permute-start.2) | collective-permute-done | bytes 1056800 | tf_op jit(solution)/shard_map/ppermute | solution.py:308
  76.3 2.4 %collective-permute-start.6 = (f32[1032,256]{1,0:T(8,128)S(1)}, f32[1032,256]{1,0:T(8,128)}, u32[]{:S(2)}, u32[]{:S(2)}) collective-permute-start(f32[1032,256]{1,0:T(8,128)S(1)} %collective-permute-done.2.refs_2_.refs_4_), channel_id=1, source_target_pairs={{0,2},{2,0},{4,30},{6,4},{8,10},{10,8},{12,6},{14,12},{16,18},{18,... | collective-permute-start | bytes 3170312 | tf_op jit(solution)/shard_map/ppermute | solution.py:308
  78.7 1.0 copy-done.7
  79.7 0.0 collective-permute-done.7.refs_2_
  79.7 2.9 %collective-permute-start.10 = (f32[1032,256]{1,0:T(8,128)}, f32[1032,256]{1,0:T(8,128)}, u32[]{:S(2)}, u32[]{:S(2)}) collective-permute-start(f32[1032,256]{1,0:T(8,128)} %collective-permute-done.7.refs_2_), channel_id=1, source_target_pairs={{6,4},{14,12},{22,20},{30,28},{7,5},{15,13},{23,21},{31,29}} | collective-permute-start | bytes 3170312 | tf_op jit(solution)/shard_map/ppermute | solution.py:312
  82.6 0.0 collective-permute-done.5.refs_0_
  82.6 2.3 %collective-permute-start.8 = (f32[1032,256]{1,0:T(8,128)}, f32[1032,256]{1,0:T(8,128)}, u32[]{:S(2)}, u32[]{:S(2)}) collective-permute-start(f32[1032,256]{1,0:T(8,128)} %collective-permute-done.5.refs_0_), channel_id=1, source_target_pairs={{6,4},{14,12},{22,20},{30,28},{7,5},{15,13},{23,21},{31,29}} | collective-permute-start | bytes 3170312 | tf_op jit(solution)/shard_map/ppermute | solution.py:312
  84.9 7.7 %collective-permute-done.6.refs_1_ = f32[1032,256]{1,0:T(8,128)} collective-permute-done((f32[1032,256]{1,0:T(8,128)S(1)}, f32[1032,256]{1,0:T(8,128)}, u32[]{:S(2)}, u32[]{:S(2)}) %collective-permute-start.6) | collective-permute-done | bytes 1056800 | tf_op jit(solution)/shard_map/ppermute | solution.py:308
  92.5 2.3 %collective-permute-start.9 = (f32[1032,256]{1,0:T(8,128)}, f32[1032,256]{1,0:T(8,128)}, u32[]{:S(2)}, u32[]{:S(2)}) collective-permute-start(f32[1032,256]{1,0:T(8,128)} %collective-permute-done.6.refs_1_), channel_id=1, source_target_pairs={{6,4},{14,12},{22,20},{30,28},{7,5},{15,13},{23,21},{31,29}} | collective-permute-start | bytes 3170312 | tf_op jit(solution)/shard_map/ppermute | solution.py:312
  94.8 0.0 copy-done.14
  94.8 0.1 copy.15
  94.9 0.0 copy-done.15
  94.9 0.1 copy.22.pairs
  95.0 0.1 reshape.9
  95.1 0.1 copy.19.left_list
  95.2 0.1 reshape_reshape.3
  95.3 0.0 collective-permute-done.4.refs_4_.refs_9_
  95.3 0.3 collective-permute-start
  95.6 0.0 copy-done.13
  95.6 2.5 %copy-done = f32[1,1,2,10,256,256]{5,4,3,2,1,0:T(8,128)S(1)} copy-done((f32[1,1,2,10,256,256]{5,4,3,2,1,0:T(8,128)S(1)}, f32[1,1,2,10,256,256]{5,4,3,2,1,0:T(8,128)}, u32[]{:S(2)}) %copy-start) | copy-done | bytes 5242904
  98.1 1.2 copy-done.2
  99.3 1.2 copy-done.5
  100.5 1.2 copy-done.8
  101.8 8.0 %own_products.2 = (f32[11,256,256]{2,1,0:T(8,128)S(1)}, bf16[12,2,256,256]{3,2,1,0:T(8,128)(2,1)S(1)}, s32[24]{0:T(128)S(1)}) custom-call(s32[4]{0:T(128)S(1)} %bitcast.12, s32[10,2]{1,0:T(8,128)S(1)} %copy.22.pairs, s32[20,2]{1,0:T(8,128)S(1)} %copy.19.left_list, f32[5120,256]{1,0:T(8,128)S(1)} %bitcast.10, f32[3080,256]{1,0:T(8,128)} %get-tuple-element.15.refs_0_, ...), custom_call_target="tpu_custom_call" | custom-call | bytes 1048576 | tf_op jit(solution)/shard_map/own_products/pallas_call | solution.py:208
  109.8 0.0 copy-start.11
  109.8 1.6 %copy-done.11 = f32[11,256,256]{2,1,0:T(8,128)} copy-done((f32[11,256,256]{2,1,0:T(8,128)}, f32[11,256,256]{2,1,0:T(8,128)S(1)}, u32[]{:S(2)}) %copy-start.11) | copy-done | bytes 2883608
  111.3 0.0 collective-permute-done.10.refs_8_
  111.3 0.0 collective-permute-done.8.refs_6_
  111.3 0.0 collective-permute-done.9.refs_7_
  111.4 1.8 %copy-done.12 = f32[11,256,256]{2,1,0:T(8,128)S(1)} copy-done((f32[11,256,256]{2,1,0:T(8,128)S(1)}, f32[11,256,256]{2,1,0:T(8,128)}, u32[]{:S(2)}) %copy-start.12) | copy-done | bytes 2883608
  113.2 7.2 %own_products.3 = (f32[11,256,256]{2,1,0:T(8,128)S(1)}, bf16[12,2,256,256]{3,2,1,0:T(8,128)(2,1)S(1)}, s32[24]{0:T(128)S(1)}) custom-call(s32[4]{0:T(128)S(1)} %bitcast.13, s32[10,2]{1,0:T(8,128)S(1)} %copy.22.pairs, s32[20,2]{1,0:T(8,128)S(1)} %copy.19.left_list, f32[5120,256]{1,0:T(8,128)} %bitcast.9, f32[1032,256]{1,0:T(8,128)} %collective-permute-done.5.refs_0_, ...), custom_call_target="tpu_custom_call" | custom-call | bytes 1048576 | tf_op jit(solution)/shard_map/own_products/pallas_call | solution.py:208
  120.5 0.0 collective-permute-done.late
  120.5 0.0 collective-permute-done.11.refs_2_
  120.5 12.0 %last_products.1 = f32[10,256,256]{2,1,0:T(8,128)} custom-call(s32[10,2]{1,0:T(8,128)S(1)} %copy.22.pairs, s32[40]{0:T(128)S(1)} %collective-permute-done.late, s32[24]{0:T(128)S(1)} %get-tuple-element.19.refs_0_, s32[24]{0:T(128)S(1)} %get-tuple-element.21.refs_1_, f32[5120,256]{1,0:T(8,128)} %collective-permute-done.11.refs_2_, ...), custom_call_target="tpu_custom_call" | custom-call | bytes 1048576 | tf_op jit(solution)/shard_map/last_products/pallas_call | solution.py:268
  (19 shorter events, 0.0 us)
Async XLA Ops:
  0.0 120.5 %collective-permute-start.11 = (f32[5120,256]{1,0:T(8,128)}, f32[5120,256]{1,0:T(8,128)}, u32[]{:S(2)}, u32[]{:S(2)}) collective-permute-start(f32[5120,256]{1,0:T(8,128)} %bitcast.8), channel_id=1, source_target_pairs={{0,1},{1,0},{2,3},{3,2},{4,5},{5,4},{6,7},{7,6},{8,9},{9,8},{10,11... | collective-permute-start | bytes 15728648 | tf_op jit(solution)/shard_map/ppermute | solution.py:298
  2.0 1.9 %copy-start.10 = (f32[1,1,12,256,256]{4,3,2,1,0:T(8,128)S(1)}, f32[1,1,12,256,256]{4,3,2,1,0:T(8,128)}, u32[]{:S(2)}) copy-start(f32[1,1,12,256,256]{4,3,2,1,0:T(8,128)} %param.8) | copy-start | bytes 9437188
  3.9 90.9 %copy-start.14 = (s32[1,1,2,10,2]{3,4,2,1,0:T(2,128)S(1)}, s32[1,1,2,10,2]{3,4,2,1,0:T(2,128)}, u32[]{:S(2)}) copy-start(s32[1,1,2,10,2]{3,4,2,1,0:T(2,128)} %param.7) | copy-start | bytes 484
  3.9 91.0 %copy-start.15 = (s32[1,1,10,2]{2,3,1,0:T(2,128)S(1)}, s32[1,1,10,2]{2,3,1,0:T(2,128)}, u32[]{:S(2)}) copy-start(s32[1,1,10,2]{2,3,1,0:T(2,128)} %param.10) | copy-start | bytes 244
  3.9 91.7 %copy-start.13 = (s32[1,4]{1,0:T(1,128)S(1)}, s32[1,4]{1,0:T(1,128)}, u32[]{:S(2)}) copy-start(s32[1,4]{1,0:T(1,128)} %param.11) | copy-start | bytes 52
  6.8 24.3 %collective-permute-start.3 = (f32[1032,256]{1,0:T(8,128)S(1)}, f32[1032,256]{1,0:T(8,128)S(1)}, u32[]{:S(2)}, u32[]{:S(2)}) collective-permute-start(f32[1032,256]{1,0:T(8,128)S(1)} %get-tuple-element.18), channel_id=1, source_target_pairs={{0,30},{2,4},{4,2},{6,0},{8,6},{10,12},{12,10},{14,8},{16,14},{18,... | collective-permute-start | bytes 3170312 | tf_op jit(solution)/shard_map/ppermute | solution.py:308
  7.9 49.1 %collective-permute-start.1 = (f32[1032,256]{1,0:T(8,128)S(1)}, f32[1032,256]{1,0:T(8,128)S(1)}, u32[]{:S(2)}, u32[]{:S(2)}) collective-permute-start(f32[1032,256]{1,0:T(8,128)S(1)} %get-tuple-element.16), channel_id=1, source_target_pairs={{0,30},{2,4},{4,2},{6,0},{8,6},{10,12},{12,10},{14,8},{16,14},{18,... | collective-permute-start | bytes 3170312 | tf_op jit(solution)/shard_map/ppermute | solution.py:308
  8.5 67.9 %collective-permute-start.2 = (f32[1032,256]{1,0:T(8,128)S(1)}, f32[1032,256]{1,0:T(8,128)S(1)}, u32[]{:S(2)}, u32[]{:S(2)}) collective-permute-start(f32[1032,256]{1,0:T(8,128)S(1)} %get-tuple-element.17), channel_id=1, source_target_pairs={{0,30},{2,4},{4,2},{6,0},{8,6},{10,12},{12,10},{14,8},{16,14},{18,... | collective-permute-start | bytes 3170312 | tf_op jit(solution)/shard_map/ppermute | solution.py:308
  9.5 85.7 %collective-permute-start.4 = (f32[3080,256]{1,0:T(8,128)}, f32[3080,256]{1,0:T(8,128)S(1)}, u32[]{:S(2)}, u32[]{:S(2)}) collective-permute-start(f32[3080,256]{1,0:T(8,128)} %get-tuple-element.15.refs_0_), channel_id=1, source_target_pairs={{0,26},{2,0},{4,30},{6,4},{8,2},{10,8},{12,6},{14,12},{16,10},{18,... | collective-permute-start | bytes 9461768 | tf_op jit(solution)/shard_map/ppermute | solution.py:308
  31.0 48.7 %collective-permute-start.7 = (f32[1032,256]{1,0:T(8,128)S(1)}, f32[1032,256]{1,0:T(8,128)}, u32[]{:S(2)}, u32[]{:S(2)}) collective-permute-start(f32[1032,256]{1,0:T(8,128)S(1)} %collective-permute-done.3.refs_3_.refs_5_), channel_id=1, source_target_pairs={{0,2},{2,0},{4,30},{6,4},{8,10},{10,8},{12,6},{14,12},{16,18},{18,... | collective-permute-start | bytes 3170312 | tf_op jit(solution)/shard_map/ppermute | solution.py:308
  56.1 1.0 copy-start.1
  57.0 25.5 %collective-permute-start.5 = (f32[1032,256]{1,0:T(8,128)S(1)}, f32[1032,256]{1,0:T(8,128)}, u32[]{:S(2)}, u32[]{:S(2)}) collective-permute-start(f32[1032,256]{1,0:T(8,128)S(1)} %collective-permute-done.1.refs_1_.refs_3_), channel_id=1, source_target_pairs={{0,2},{2,0},{4,30},{6,4},{8,10},{10,8},{12,6},{14,12},{16,18},{18,... | collective-permute-start | bytes 3170312 | tf_op jit(solution)/shard_map/ppermute | solution.py:308
  67.4 1.0 copy-start.4
  76.3 16.2 %collective-permute-start.6 = (f32[1032,256]{1,0:T(8,128)S(1)}, f32[1032,256]{1,0:T(8,128)}, u32[]{:S(2)}, u32[]{:S(2)}) collective-permute-start(f32[1032,256]{1,0:T(8,128)S(1)} %collective-permute-done.2.refs_2_.refs_4_), channel_id=1, source_target_pairs={{0,2},{2,0},{4,30},{6,4},{8,10},{10,8},{12,6},{14,12},{16,18},{18,... | collective-permute-start | bytes 3170312 | tf_op jit(solution)/shard_map/ppermute | solution.py:308
  78.7 1.0 copy-start.7
  79.7 31.7 %collective-permute-start.10 = (f32[1032,256]{1,0:T(8,128)}, f32[1032,256]{1,0:T(8,128)}, u32[]{:S(2)}, u32[]{:S(2)}) collective-permute-start(f32[1032,256]{1,0:T(8,128)} %collective-permute-done.7.refs_2_), channel_id=1, source_target_pairs={{6,4},{14,12},{22,20},{30,28},{7,5},{15,13},{23,21},{31,29}} | collective-permute-start | bytes 3170312 | tf_op jit(solution)/shard_map/ppermute | solution.py:312
  82.6 28.8 %collective-permute-start.8 = (f32[1032,256]{1,0:T(8,128)}, f32[1032,256]{1,0:T(8,128)}, u32[]{:S(2)}, u32[]{:S(2)}) collective-permute-start(f32[1032,256]{1,0:T(8,128)} %collective-permute-done.5.refs_0_), channel_id=1, source_target_pairs={{6,4},{14,12},{22,20},{30,28},{7,5},{15,13},{23,21},{31,29}} | collective-permute-start | bytes 3170312 | tf_op jit(solution)/shard_map/ppermute | solution.py:312
  92.5 18.8 %collective-permute-start.9 = (f32[1032,256]{1,0:T(8,128)}, f32[1032,256]{1,0:T(8,128)}, u32[]{:S(2)}, u32[]{:S(2)}) collective-permute-start(f32[1032,256]{1,0:T(8,128)} %collective-permute-done.6.refs_1_), channel_id=1, source_target_pairs={{6,4},{14,12},{22,20},{30,28},{7,5},{15,13},{23,21},{31,29}} | collective-permute-start | bytes 3170312 | tf_op jit(solution)/shard_map/ppermute | solution.py:312
  95.3 25.2 %collective-permute-start = (s32[40]{0:T(128)S(1)}, s32[40]{0:T(128)S(1)}, u32[]{:S(2)}, u32[]{:S(2)}) collective-permute-start(s32[40]{0:T(128)S(1)} %reshape_reshape.3), channel_id=1, source_target_pairs={{0,1},{1,0},{2,3},{3,2},{4,5},{5,4},{6,7},{7,6},{8,9},{9,8},{10,11... | collective-permute-start | bytes 488 | tf_op jit(solution)/shard_map/ppermute | solution.py:299
  95.6 2.5 %copy-start = (f32[1,1,2,10,256,256]{5,4,3,2,1,0:T(8,128)S(1)}, f32[1,1,2,10,256,256]{5,4,3,2,1,0:T(8,128)}, u32[]{:S(2)}) copy-start(f32[1,1,2,10,256,256]{5,4,3,2,1,0:T(8,128)} %param.6) | copy-start | bytes 15728644
  98.1 1.2 copy-start.2
  99.3 1.2 copy-start.5
  100.5 1.2 copy-start.8
  101.8 9.6 %copy-start.3 = (f32[1032,256]{1,0:T(8,128)S(1)}, f32[1032,256]{1,0:T(8,128)}, u32[]{:S(2)}) copy-start(f32[1032,256]{1,0:T(8,128)} %copy-done.1) | copy-start | bytes 3170308
  101.8 9.6 %copy-start.6 = (f32[1032,256]{1,0:T(8,128)S(1)}, f32[1032,256]{1,0:T(8,128)}, u32[]{:S(2)}) copy-start(f32[1032,256]{1,0:T(8,128)} %copy-done.4) | copy-start | bytes 3170308
  101.8 9.6 %copy-start.9 = (f32[1032,256]{1,0:T(8,128)S(1)}, f32[1032,256]{1,0:T(8,128)}, u32[]{:S(2)}) copy-start(f32[1032,256]{1,0:T(8,128)} %copy-done.7) | copy-start | bytes 3170308
  109.8 1.6 %copy-start.11 = (f32[11,256,256]{2,1,0:T(8,128)}, f32[11,256,256]{2,1,0:T(8,128)S(1)}, u32[]{:S(2)}) copy-start(f32[11,256,256]{2,1,0:T(8,128)S(1)} %get-tuple-element.20.refs_10_) | copy-start | bytes 8650756
  111.4 1.8 %copy-start.12 = (f32[11,256,256]{2,1,0:T(8,128)S(1)}, f32[11,256,256]{2,1,0:T(8,128)}, u32[]{:S(2)}) copy-start(f32[11,256,256]{2,1,0:T(8,128)} %copy-done.11) | copy-start | bytes 8650756

commit v5 on v4

v5 whole, which is shorter than its diff:
```python
import functools

import jax
import jax.numpy as jnp
from jax import lax
from jax.experimental import pallas as pl
from jax.experimental.pallas import tpu as pltpu
from jax.sharding import PartitionSpec as P

RB = 3
KB = 4
CB = 4
STEPS = 4
LIST_ROWS = 8
X_PARTS = 3
LAST = 0
VMEM = pl.BlockSpec(memory_space=pltpu.VMEM)
SMEM = pl.BlockSpec(memory_space=pltpu.SMEM)


def pack_kernel(share, places, x, *refs):
    *targets, sems = refs
    n_x, bs = places.shape[0], x.shape[-1]
    cuts = [(0, n_x)] + [(p * share, share) for p in range(n_x // share)]
    copies = [
        pltpu.make_async_copy(x.at[pl.ds(first * bs, n * bs)], target.at[pl.ds(0, n * bs)], sems.at[i])
        for i, (target, (first, n)) in enumerate(zip(targets, cuts))
    ]
    for copy in copies:
        copy.start()
    lane = lax.broadcasted_iota(jnp.int32, (LIST_ROWS, bs), 1)
    for target, (first, n) in zip(targets, cuts):
        rows = jnp.zeros((LIST_ROWS, bs), jnp.float32)
        for j in range(n):
            for d in range(2):
                rows = jnp.where(lane == 2 * j + d, places[first + j, d].astype(jnp.float32), rows)
        target[n * bs : n * bs + LIST_ROWS] = rows
    for copy in copies:
        copy.wait()


def pack(x, places, share):
    n_x, bs = places.shape[0], x.shape[-1]
    sizes = [n_x] + [share] * (n_x // share)
    return pl.pallas_call(
        functools.partial(pack_kernel, share),
        in_specs=[SMEM, pl.BlockSpec(memory_space=pl.ANY)],
        out_specs=[VMEM] * len(sizes),
        out_shape=[jax.ShapeDtypeStruct((n * bs + LIST_ROWS, bs), x.dtype) for n in sizes],
        scratch_shapes=[pltpu.SemaphoreType.DMA((len(sizes),))],
        compiler_params=pltpu.CompilerParams(vmem_limit_bytes=16 * 2**20),
        cost_estimate=pl.CostEstimate(flops=0, bytes_accessed=2**20, transcendentals=0),
        name="pack",
    )(places, x)


def halves(values):
    high = values.astype(jnp.bfloat16)
    return high, (values - high.astype(jnp.float32)).astype(jnp.bfloat16)


def dot(left, right):
    return jnp.dot(left, right, preferred_element_type=jnp.float32)


def block(rows, index, bs):
    return rows[pl.ds(pl.multiple_of(index * bs, bs), bs), :]


def fill_map(target, size, read, count, columns):
    for cell in range(size):
        target[cell] = -1
    for entry in range(count):
        target[read(entry, 0) * columns + read(entry, 1)] = entry


def add_products(acc, n_out, bs, maps, todo, left_place, n_left, left, right):
    r_map, o_map = maps
    unroll = todo.shape[0] - n_left * CB

    def collect(i, count):
        row, base = left_place(i)
        for c in range(CB):
            j, m = r_map[base + c], o_map[row * CB + c]
            todo[count] = (i * 64 + jnp.maximum(j, 0)) * 64 + jnp.maximum(m, 0)
            count = count + ((j >= 0) & (m >= 0)).astype(jnp.int32)
        return count

    count = lax.fori_loop(0, n_left, collect, jnp.int32(0))
    for u in range(unroll):
        todo[count + u] = n_out

    def several(q, carry):
        for u in range(unroll):
            code = todo[q * unroll + u]
            i, j, m = code // 4096, (code // 64) % 64, code % 64
            left_high, left_low = halves(block(left, i, bs))
            right_high, right_low = right(j)
            acc[m] += dot(left_high, right_high) + dot(left_high, right_low) + dot(left_low, right_high)
        return carry

    lax.fori_loop(0, (count + unroll - 1) // unroll, several, 0)


def own_kernel(slot, n_left, n_x, plan, n_arrays, chooses, last, owner, pairs, left_list, *refs):
    refs = list(refs)

    def take(count):
        taken, refs[:count] = refs[:count], []
        return taken

    adds = chooses and slot > 0
    (list_before,) = take(1) if adds else (None,)
    (left,), arrays = take(1), take(n_arrays)
    acc_before, chosen_before = take(2) if adds else (None, None)
    (acc_out,) = take(1)
    chosen_out, chosen_list = take(2) if chooses else (None, None)
    here_lists, there_lists = take(X_PARTS), take(X_PARTS)
    left_rows, here_rows, there_rows, r_map, o_map, todo, sems = take(7)
    acc, chosen = (acc_out, chosen_out) if last else take(2)
    n_out, bs = pairs.shape[0], left.shape[-1]
    place, column = lax.axis_index("loop") % 4, lax.axis_index("bcast")
    mark = slot * n_x if last and chooses else 0

    own_copies = [pltpu.make_async_copy(left.at[pl.ds(slot * n_left * bs, n_left * bs)], left_rows, sems.at[0])]
    if adds:
        own_copies.append(pltpu.make_async_copy(acc_before, acc, sems.at[1]))
        own_copies.append(pltpu.make_async_copy(chosen_before, chosen.at[pl.ds(0, mark)], sems.at[2]))
    for copy in own_copies:
        copy.start()

    def fetch(at, parts, rows, lists):
        copies = []
        for p, array in enumerate(parts):
            n = n_x // len(parts)
            right = arrays[array]
            target = rows.at[pl.ds(p * n * bs, n * bs)]
            copies.append(pltpu.make_async_copy(right.at[pl.ds(0, n * bs)], target, sems.at[at + 2 * p]))
            listed = right.at[pl.ds(n * bs, LIST_ROWS)]
            copies.append(pltpu.make_async_copy(listed, lists[p], sems.at[at + 2 * p + 1]))
        return copies

    def copies_of(parts, here):
        if here:
            return fetch(5, parts, here_rows, here_lists)
        return fetch(5 + 2 * X_PARTS, parts, there_rows, there_lists)

    def place_in(lists, count):
        n = n_x // count
        return lambda j, d: lists[j // n][0, 2 * (j % n) + d].astype(jnp.int32)

    def each(then):
        for step, places, parts in plan:
            applies = functools.reduce(jnp.logical_or, [place == value for value in places])
            mine = owner[step] == column if chooses else True
            pl.when(applies & mine)(functools.partial(then, parts, True))
            if chooses:
                pl.when(applies & jnp.logical_not(mine))(functools.partial(then, parts, False))

    def start(parts, here):
        for copy in copies_of(parts, here):
            copy.start()

    def land(wanted, parts, here):
        if here != wanted:
            return
        for copy in copies_of(parts, here):
            copy.wait()
        if here:
            fill_map(r_map, KB * CB, place_in(here_lists, len(parts)), n_x, CB)
            return
        read = place_in(there_lists, len(parts))
        for j in range(n_x):
            for d in range(2):
                chosen_list[2 * (slot * n_x + j) + d] = read(j, d)

    def left_place(i):
        return left_list[slot * n_left + i, 0], left_list[slot * n_left + i, 1] * CB

    each(start)
    fill_map(o_map, RB * CB, lambda m, d: pairs[m, d], n_out, CB)
    if adds:
        for q in range(2 * slot * n_x):
            chosen_list[q] = list_before[q]
    else:
        acc[...] = jnp.zeros_like(acc)
    each(functools.partial(land, True))
    for copy in own_copies:
        copy.wait()
    add_products(
        acc, n_out, bs, (r_map, o_map), todo, left_place, n_left, left_rows, lambda j: halves(block(here_rows, j, bs))
    )
    if not chooses:
        return
    out_copies = []
    if not last:
        out_copies.append(pltpu.make_async_copy(acc, acc_out, sems.at[3]))
        out_copies[0].start()
    each(functools.partial(land, False))

    def split(j, carry):
        chosen[mark + j, 0], chosen[mark + j, 1] = halves(block(there_rows, j, bs))
        return carry

    lax.fori_loop(0, n_x, split, 0)
    if not last:
        out_copies.append(pltpu.make_async_copy(chosen, chosen_out, sems.at[4]))
        out_copies[1].start()
    for copy in out_copies:
        copy.wait()


def own_products(owner, pairs, left, slot, left_list, n_left, choices, before, chooses, last):
    bs, n_out = left.shape[-1], pairs.shape[0]
    arrays, plan = [], []
    for step, places, parts in choices:
        at = []
        for part in parts:
            known = [i for i, other in enumerate(arrays) if other is part]
            if not known:
                known = [len(arrays)]
                arrays.append(part)
            at.append(known[0])
        plan.append((step, places, at))
    n_x = sum(part.shape[0] // bs for part in choices[0][2])
    anywhere = pl.BlockSpec(memory_space=pl.ANY)
    smem, operands = [owner, pairs, left_list], [pltpu.with_memory_space_constraint(left, pltpu.HBM), *arrays]
    if before is not None:
        smem.append(before[2])
        operands += before[:2]
    acc_shape, chosen_shape = (n_out + 1, bs, bs), ((slot + 1) * n_x, 2, bs, bs)
    kind = pltpu.VMEM if last else pltpu.HBM
    out_shape, out_specs = [kind(acc_shape, jnp.float32)], [pl.BlockSpec(memory_space=kind)]
    if chooses:
        out_shape += [kind(chosen_shape, jnp.bfloat16), jax.ShapeDtypeStruct((2 * (slot + 1) * n_x,), jnp.int32)]
        out_specs += [pl.BlockSpec(memory_space=kind), SMEM]
    scratch = [pltpu.SMEM((LIST_ROWS, bs), jnp.float32)] * (2 * X_PARTS) + [
        pltpu.VMEM((n_left * bs, bs), jnp.float32),
        pltpu.VMEM((n_x * bs, bs), jnp.float32),
        pltpu.VMEM((n_x * bs, bs), jnp.float32),
        pltpu.SMEM(((KB + 1) * CB,), jnp.int32),
        pltpu.SMEM((RB * CB,), jnp.int32),
        pltpu.SMEM((n_left * CB + 4,), jnp.int32),
        pltpu.SemaphoreType.DMA((5 + 4 * X_PARTS,)),
    ]
    if not last:
        scratch += [pltpu.VMEM(acc_shape, jnp.float32), pltpu.VMEM(chosen_shape, jnp.bfloat16)]
    return pl.pallas_call(
        functools.partial(own_kernel, slot, n_left, n_x, plan, len(arrays), chooses, last),
        in_specs=[SMEM] * len(smem) + [anywhere] * len(operands),
        out_specs=out_specs,
        out_shape=out_shape,
        scratch_shapes=scratch,
        compiler_params=pltpu.CompilerParams(vmem_limit_bytes=OWN_LIMIT),
        cost_estimate=pl.CostEstimate(flops=0, bytes_accessed=2**20, transcendentals=0),
        name="own_products",
    )(*smem, *operands)


OWN_LIMIT = 24 * 2**20
LAST_LIMIT = 24 * 2**20


def their_kernel(n_s, first, last, pairs, late, right_list, left, before, chosen, *refs):
    if last:
        out, acc, left_rows, r_map, o_map, todo, sems = refs
    else:
        acc, left_rows, r_map, o_map, todo, sems = refs
    n_out, bs = pairs.shape[0], left.shape[-1]
    n_left, n_right = left.shape[0] // bs, chosen.shape[0]
    depth = r_map.shape[0] // ((KB + 1) * CB)
    n_x = n_right // depth
    part = left.shape[0] // 4
    fetched = []
    for q in range(4):
        rows = pl.ds(q * part, part)
        fetched.append(pltpu.make_async_copy(left.at[rows], left_rows.at[rows], sems.at[q]))
    for copy in fetched:
        copy.start()
    for m in range(n_out):
        acc[m] = before[m]
    fill_map(o_map, RB * CB, lambda m, d: pairs[m, d], n_out, CB)
    for cell in range(r_map.shape[0]):
        r_map[cell] = -1
    for j in range(n_right):
        r_map[(j // n_x * (KB + 1) + right_list[2 * j]) * CB + right_list[2 * j + 1]] = j
    for copy in fetched:
        copy.wait()

    def left_place(i):
        return late[2 * (first + i)], ((first + i) // n_s * (KB + 1) + late[2 * (first + i) + 1]) * CB

    add_products(
        acc, n_out, bs, (r_map, o_map), todo, left_place, n_left, left_rows, lambda j: (chosen[j, 0], chosen[j, 1])
    )
    if last:
        copies = [pltpu.make_async_copy(acc.at[m], out.at[m], sems.at[4 + m]) for m in range(n_out)]
        for copy in copies:
            copy.start()
        for copy in copies:
            copy.wait()


def their_products(pairs, late, left, first, n_s, before, last):
    bs = left.shape[-1]
    acc, chosen, right_list = before
    n_out, n_left = pairs.shape[0], left.shape[0] // bs
    depth = late.size // (2 * n_s)
    anywhere = pl.BlockSpec(memory_space=pl.ANY)
    return pl.pallas_call(
        functools.partial(their_kernel, n_s, first, last),
        in_specs=[SMEM] * 3 + [anywhere] + [VMEM] * 2,
        out_specs=anywhere if last else VMEM,
        out_shape=jax.ShapeDtypeStruct((n_out, bs, bs) if last else acc.shape, jnp.float32),
        scratch_shapes=([pltpu.VMEM(acc.shape, acc.dtype)] if last else [])
        + [
            pltpu.VMEM(left.shape, left.dtype),
            pltpu.SMEM((depth * (KB + 1) * CB,), jnp.int32),
            pltpu.SMEM((RB * CB,), jnp.int32),
            pltpu.SMEM((n_left * CB + (8 if n_left > 8 else 4),), jnp.int32),
            pltpu.SemaphoreType.DMA((4 + n_out,)),
        ],
        compiler_params=pltpu.CompilerParams(vmem_limit_bytes=LAST_LIMIT),
        cost_estimate=pl.CostEstimate(flops=0, bytes_accessed=2**20, transcendentals=0),
        name="their_products",
    )(pairs, late, right_list, left, acc, chosen)


def per_device(s_blocks, s_list, x_blocks, x_list, c_list, owner):
    length, width = lax.axis_size("loop"), lax.axis_size("bcast")
    pairs, owner = c_list[0, 0], owner[0]
    depth, n_s, bs = s_blocks.shape[2], s_blocks.shape[3], s_blocks.shape[-1]
    n_x = x_blocks.shape[2]
    s_own, x_own = s_blocks.reshape(depth * n_s * bs, bs), x_blocks.reshape(n_x * bs, bs)
    s_own_list, x_own_list = s_list.reshape(depth * n_s, 2), x_list[0, 0]

    swapped = width == 2
    if swapped:
        partner = [(0, 1), (1, 0)]
        their_list = lax.ppermute(s_own_list.reshape(-1), "bcast", partner)
        cuts = (0, depth * n_s - LAST, depth * n_s)
        chunks = [s_own[lo * bs : hi * bs] for lo, hi in zip(cuts, cuts[1:])]
        if LAST:
            chunks[0], their_list = lax.optimization_barrier((chunks[0], their_list))
        came = [lax.ppermute(chunk, "bcast", partner) for chunk in chunks if chunk.size]
    else:
        held = lax.all_gather(s_own, "bcast")
        held_lists = lax.all_gather(s_own_list, "bcast")

    share = n_x // X_PARTS
    everything, *parts = pack(x_own, x_own_list, share)

    def moved(packed, to):
        return [lax.ppermute(part, "loop", [(g, (g + to[g % 4]) % length) for g in range(length)]) for part in packed]

    first = moved(parts, (-1, 1, -1, -3))
    second = moved(first, (1, -1, -3, -1))
    other = moved([everything], (-3, -1, -3, -1))

    choices = [(0, (0, 1, 2, 3), [everything]), (1, (1, 3), first), (1, (0, 2), other)]
    choices += [(2, (0, 1, 2, 3), second), (3, (0,), first), (3, (1, 3), other)]

    def last_choice():
        return (3, (2,), [lax.ppermute(part, "loop", [(g, g - 1) for g in range(3, length, 4)]) for part in second])

    if not swapped:
        choices.append(last_choice())
        total = 0
        for step in range(STEPS):
            piece = lax.dynamic_index_in_dim(held, owner[step], 0, False)
            places = lax.dynamic_index_in_dim(held_lists, owner[step], 0, False)
            fit = [choice for choice in choices if choice[0] == step]
            added = own_products(owner, pairs, piece, step // width, places, n_s, fit, None, False, True)
            total = total + added[0]
        return total[None, None, : pairs.shape[0]]

    sums = None
    for slot in range(depth):
        if slot == 1:
            second[-1], places = lax.optimization_barrier((second[-1], sums[2]))
            sums = (*sums[:2], places)
            choices.append(last_choice())
        fit = [choice for choice in choices if choice[0] // width == slot]
        sums = own_products(owner, pairs, s_own, slot, s_own_list, n_s, fit, sums, True, slot == depth - 1)
    for q, rows in enumerate(came):
        final = q == len(came) - 1
        added = their_products(pairs, their_list, rows, cuts[q], n_s, sums, final)
        sums = (added, *sums[1:])
    return sums[0][None, None]


def solution(mesh):
    return jax.shard_map(
        per_device,
        mesh=mesh,
        in_specs=(
            P("loop", "bcast", None, None, None, None),
            P("loop", "bcast", None, None, None),
            P("loop", "bcast", None, None, None),
            P("loop", "bcast", None, None),
            P("loop", "bcast", None, None),
            P("loop", None),
        ),
        out_specs=P("loop", "bcast", None, None, None),
        check_vma=False,
    )
```

time: 133 us -> 129 us (0.970)
  the two profiles are of different devices: /device:TPU:27 before, /device:TPU:0 now
where the time goes in v5:
time: 129 us; the launch traced here: 127 us
  waiting for transfers between devices  72.7 us (56%)
  Pallas kernels  30.7 us (24%)
  starting transfers between devices  16.3 us (13%)
  local copies, waits for them, and re-layouts  6.83 us (5%)
    ppermute x7, waiting for transfers between devices, moved(): lax.ppermute(part, 'loop', [(g, (g + to[g % 4]) % length) for g in range(...  67.5 us
    pallas_call x2, Pallas kernels, own_products(): pl.pallas_call(functools.partial(own_kernel, slot, n_left, n_x, plan, len...  17.5 us
    pallas_call x1, Pallas kernels, their_products(): pl.pallas_call(functools.partial(their_kernel, n_s, first, last), in_spec...  10.3 us
    ppermute x7, starting transfers between devices, moved(): lax.ppermute(part, 'loop', [(g, (g + to[g % 4]) % length) for g in range(...  6.49 us
    unnamed x14, local copies, waits for them, and re-layouts  5.7 us
    ppermute x1, waiting for transfers between devices, per_device(): their_list = lax.ppermute(s_own_list.reshape(-1), 'bcast', partner)  5.24 us
    ppermute x3, starting transfers between devices, last_choice(): lax.ppermute(part, 'loop', [(g, g - 1) for g in range(3, length, 4)])  4.97 us
    ppermute x1, starting transfers between devices, per_device(): lax.ppermute(chunk, 'bcast', partner)  2.97 us
  transfers between devices with their start and end apart: 12, of which 4 were waited for; matrix products, arithmetic and copies ran while one was open for 1% of the time, Pallas kernels for 16%

profile of v5, /device:TPU:0, one launch (start us, length us, event | category | flops | bytes accessed | tf_op | source)
XLA Modules:
  0.0 126.7 jit_solution(13219439089116541452)
XLA Ops:
  0.0 3.0 %collective-permute-start.11 = (f32[5120,256]{1,0:T(8,128)}, f32[5120,256]{1,0:T(8,128)}, u32[]{:S(2)}, u32[]{:S(2)}) collective-permute-start(f32[5120,256]{1,0:T(8,128)} %bitcast.11), channel_id=1, source_target_pairs={{0,1},{1,0},{2,3},{3,2},{4,5},{5,4},{6,7},{7,6},{8,9},{9,8},{10,11... | collective-permute-start | bytes 15728648 | tf_op jit(solution)/shard_map/ppermute | solution.py:345
  3.0 0.8 copy.17.places
  3.7 0.0 copy-start.1
  3.7 1.9 %copy-done.1 = f32[1,1,12,256,256]{4,3,2,1,0:T(8,128)S(1)} copy-done((f32[1,1,12,256,256]{4,3,2,1,0:T(8,128)S(1)}, f32[1,1,12,256,256]{4,3,2,1,0:T(8,128)}, u32[]{:S(2)}) %copy-start.1) | copy-done | bytes 3145752
  5.6 0.0 copy-start.5
  5.6 0.0 copy-start.4
  5.6 0.0 copy-start.3
  5.6 2.8 %pack.1 = (f32[3080,256]{1,0:T(8,128)}, f32[1032,256]{1,0:T(8,128)S(1)}, f32[1032,256]{1,0:T(8,128)S(1)}, f32[1032,256]{1,0:T(8,128)S(1)}) custom-call(s32[12,2]{1,0:T(8,128)S(1)} %copy.17.places, f32[3072,256]{1,0:T(8,128)S(1)} %bitcast.8), custom_call_target="tpu_custom_call" | custom-call | bytes 1048576 | tf_op jit(solution)/shard_map/pack/pallas_call | solution.py:45
  8.5 2.8 %collective-permute-start.5 = (f32[3080,256]{1,0:T(8,128)}, f32[3080,256]{1,0:T(8,128)S(1)}, u32[]{:S(2)}, u32[]{:S(2)}) collective-permute-start(f32[3080,256]{1,0:T(8,128)} %get-tuple-element.18.refs_1_), channel_id=1, source_target_pairs={{0,26},{2,0},{4,30},{6,4},{8,2},{10,8},{12,6},{14,12},{16,10},{18,... | collective-permute-start | bytes 9461768 | tf_op jit(solution)/shard_map/ppermute | solution.py:354
  11.3 1.9 %collective-permute-start.3 = (f32[1032,256]{1,0:T(8,128)S(1)}, f32[1032,256]{1,0:T(8,128)}, u32[]{:S(2)}, u32[]{:S(2)}) collective-permute-start(f32[1032,256]{1,0:T(8,128)S(1)} %get-tuple-element.19), channel_id=1, source_target_pairs={{0,30},{2,4},{4,2},{6,0},{8,6},{10,12},{12,10},{14,8},{16,14},{18,... | collective-permute-start | bytes 3170312 | tf_op jit(solution)/shard_map/ppermute | solution.py:354
  13.2 0.2 collective-permute-start.4
  13.4 1.4 %collective-permute-start.1 = (f32[1032,256]{1,0:T(8,128)S(1)}, f32[1032,256]{1,0:T(8,128)}, u32[]{:S(2)}, u32[]{:S(2)}) collective-permute-start(f32[1032,256]{1,0:T(8,128)S(1)} %get-tuple-element.17), channel_id=1, source_target_pairs={{0,30},{2,4},{4,2},{6,0},{8,6},{10,12},{12,10},{14,8},{16,14},{18,... | collective-permute-start | bytes 3170312 | tf_op jit(solution)/shard_map/ppermute | solution.py:354
  14.8 42.9 %collective-permute-done.3.refs_2_.refs_5_ = f32[1032,256]{1,0:T(8,128)} collective-permute-done((f32[1032,256]{1,0:T(8,128)S(1)}, f32[1032,256]{1,0:T(8,128)}, u32[]{:S(2)}, u32[]{:S(2)}) %collective-permute-start.3) | collective-permute-done | bytes 1056800 | tf_op jit(solution)/shard_map/ppermute | solution.py:354
  57.7 0.0 collective-permute-start.6
  57.7 11.3 %collective-permute-done.4.refs_3_.refs_6_ = f32[1032,256]{1,0:T(8,128)} collective-permute-done((f32[1032,256]{1,0:T(8,128)S(1)}, f32[1032,256]{1,0:T(8,128)}, u32[]{:S(2)}, u32[]{:S(2)}) %collective-permute-start.4) | collective-permute-done | bytes 1056800 | tf_op jit(solution)/shard_map/ppermute | solution.py:354
  69.0 0.0 collective-permute-start.7
  69.0 13.3 %collective-permute-done.1.refs_4_.refs_7_ = f32[1032,256]{1,0:T(8,128)} collective-permute-done((f32[1032,256]{1,0:T(8,128)S(1)}, f32[1032,256]{1,0:T(8,128)}, u32[]{:S(2)}, u32[]{:S(2)}) %collective-permute-start.1) | collective-permute-done | bytes 1056800 | tf_op jit(solution)/shard_map/ppermute | solution.py:354
  82.3 0.2 collective-permute-start.2
  82.4 0.0 copy-done.5
  82.4 0.1 copy.22.pairs
  82.5 0.0 copy-done.4
  82.5 0.1 reshape.9
  82.6 0.1 copy.21.left_list
  82.7 0.0 collective-permute-done.6.refs_2_
  82.7 1.6 %collective-permute-start.8 = (f32[1032,256]{1,0:T(8,128)}, f32[1032,256]{1,0:T(8,128)}, u32[]{:S(2)}, u32[]{:S(2)}) collective-permute-start(f32[1032,256]{1,0:T(8,128)} %collective-permute-done.6.refs_2_), channel_id=1, source_target_pairs={{6,4},{14,12},{22,20},{30,28},{7,5},{15,13},{23,21},{31,29}} | collective-permute-start | bytes 3170312 | tf_op jit(solution)/shard_map/ppermute | solution.py:364
  84.4 0.0 collective-permute-done.7.refs_3_
  84.4 1.7 %collective-permute-start.9 = (f32[1032,256]{1,0:T(8,128)}, f32[1032,256]{1,0:T(8,128)}, u32[]{:S(2)}, u32[]{:S(2)}) collective-permute-start(f32[1032,256]{1,0:T(8,128)} %collective-permute-done.7.refs_3_), channel_id=1, source_target_pairs={{6,4},{14,12},{22,20},{30,28},{7,5},{15,13},{23,21},{31,29}} | collective-permute-start | bytes 3170312 | tf_op jit(solution)/shard_map/ppermute | solution.py:364
  86.0 0.0 collective-permute-done.5.refs_5_.refs_8_
  86.0 0.0 copy-done.3
  86.0 7.9 %own_products.2 = (f32[11,256,256]{2,1,0:T(8,128)}, bf16[12,2,256,256]{3,2,1,0:T(8,128)(2,1)}, s32[24]{0:T(128)S(1)}) custom-call(s32[4]{0:T(128)S(1)} %bitcast.9, s32[10,2]{1,0:T(8,128)S(1)} %copy.22.pairs, s32[20,2]{1,0:T(8,128)S(1)} %copy.21.left_list, f32[5120,256]{1,0:T(8,128)} %bitcast.12, f32[3080,256]{1,0:T(8,128)} %get-tuple-element.18.refs_1_, ...), custom_call_target="tpu_custom_call" | custom-call | bytes 1048576 | tf_op jit(solution)/shard_map/own_products/pallas_call | solution.py:248
  93.9 0.0 collective-permute-done.2.refs_4_
  94.0 1.7 %collective-permute-start.10 = (f32[1032,256]{1,0:T(8,128)}, f32[1032,256]{1,0:T(8,128)}, u32[]{:S(2)}, u32[]{:S(2)}) collective-permute-start(f32[1032,256]{1,0:T(8,128)} %collective-permute-done.2.refs_4_), channel_id=1, source_target_pairs={{6,4},{14,12},{22,20},{30,28},{7,5},{15,13},{23,21},{31,29}} | collective-permute-start | bytes 3170312 | tf_op jit(solution)/shard_map/ppermute | solution.py:364
  95.6 0.1 copy.15
  95.7 0.1 reshape_reshape.3
  95.8 1.9 %collective-permute-start = (s32[40]{0:T(128)S(1)}, s32[40]{0:T(128)S(1)}, u32[]{:S(2)}, u32[]{:S(2)}) collective-permute-start(s32[40]{0:T(128)S(1)} %reshape_reshape.3), channel_id=1, source_target_pairs={{0,1},{1,0},{2,3},{3,2},{4,5},{5,4},{6,7},{7,6},{8,9},{9,8},{10,11... | collective-permute-start | bytes 488 | tf_op jit(solution)/shard_map/ppermute | solution.py:340
  97.7 0.0 collective-permute-done.8.refs_9_
  97.7 0.0 collective-permute-done.9.refs_10_
  97.7 0.0 collective-permute-done.10.refs_11_
  97.7 0.0 copy-start
  97.7 1.9 %copy-done = bf16[12,2,256,256]{3,2,1,0:T(8,128)(2,1)S(1)} copy-done((bf16[12,2,256,256]{3,2,1,0:T(8,128)(2,1)S(1)}, bf16[12,2,256,256]{3,2,1,0:T(8,128)(2,1)}, u32[]{:S(2)}) %copy-start) | copy-done | bytes 3145752
  99.6 0.0 copy-start.2
  99.6 1.8 %copy-done.2 = f32[11,256,256]{2,1,0:T(8,128)S(1)} copy-done((f32[11,256,256]{2,1,0:T(8,128)S(1)}, f32[11,256,256]{2,1,0:T(8,128)}, u32[]{:S(2)}) %copy-start.2) | copy-done | bytes 2883608
  101.4 9.6 %own_products.3 = (f32[11,256,256]{2,1,0:T(8,128)S(1)}, bf16[24,2,256,256]{3,2,1,0:T(8,128)(2,1)S(1)}, s32[48]{0:T(128)S(1)}) custom-call(s32[4]{0:T(128)S(1)} %bitcast.10, s32[10,2]{1,0:T(8,128)S(1)} %copy.22.pairs, s32[20,2]{1,0:T(8,128)S(1)} %copy.21.left_list, s32[24]{0:T(128)S(1)} %get-tuple-element.22.refs_0_, f32[5120,256]{1,0:T(8,128)} %bitcast.13, ...), custom_call_target="tpu_custom_call" | custom-call | bytes 1048576 | tf_op jit(solution)/shard_map/own_products/pallas_call | solution.py:248
  111.1 5.2 %collective-permute-done.late = s32[40]{0:T(128)S(1)} collective-permute-done((s32[40]{0:T(128)S(1)}, s32[40]{0:T(128)S(1)}, u32[]{:S(2)}, u32[]{:S(2)}) %collective-permute-start) | collective-permute-done | bytes 192 | tf_op jit(solution)/shard_map/ppermute | solution.py:340
  116.3 0.0 collective-permute-done.11.left
  116.3 10.3 %their_products.1 = f32[10,256,256]{2,1,0:T(8,128)} custom-call(s32[10,2]{1,0:T(8,128)S(1)} %copy.22.pairs, s32[40]{0:T(128)S(1)} %collective-permute-done.late, s32[48]{0:T(128)S(1)} %get-tuple-element.26.right_list, f32[5120,256]{1,0:T(8,128)} %collective-permute-done.11.left, f32[11,256,256]{2,1,0:T(8,128)S(1)} %get-tuple-element.27.before, ...), custom_call_target="tpu_custom_call" | custom-call | bytes 1048576 | tf_op jit(solution)/shard_map/their_products/pallas_call | solution.py:310
  (1 shorter events, 0.0 us)
Async XLA Ops:
  0.0 116.3 %collective-permute-start.11 = (f32[5120,256]{1,0:T(8,128)}, f32[5120,256]{1,0:T(8,128)}, u32[]{:S(2)}, u32[]{:S(2)}) collective-permute-start(f32[5120,256]{1,0:T(8,128)} %bitcast.11), channel_id=1, source_target_pairs={{0,1},{1,0},{2,3},{3,2},{4,5},{5,4},{6,7},{7,6},{8,9},{9,8},{10,11... | collective-permute-start | bytes 15728648 | tf_op jit(solution)/shard_map/ppermute | solution.py:345
  3.7 1.9 %copy-start.1 = (f32[1,1,12,256,256]{4,3,2,1,0:T(8,128)S(1)}, f32[1,1,12,256,256]{4,3,2,1,0:T(8,128)}, u32[]{:S(2)}) copy-start(f32[1,1,12,256,256]{4,3,2,1,0:T(8,128)} %param.8) | copy-start | bytes 9437188
  5.6 76.8 %copy-start.5 = (s32[1,1,10,2]{2,3,1,0:T(2,128)S(1)}, s32[1,1,10,2]{2,3,1,0:T(2,128)}, u32[]{:S(2)}) copy-start(s32[1,1,10,2]{2,3,1,0:T(2,128)} %param.10) | copy-start | bytes 244
  5.6 76.9 %copy-start.4 = (s32[1,1,2,10,2]{3,4,2,1,0:T(2,128)S(1)}, s32[1,1,2,10,2]{3,4,2,1,0:T(2,128)}, u32[]{:S(2)}) copy-start(s32[1,1,2,10,2]{3,4,2,1,0:T(2,128)} %param.7) | copy-start | bytes 484
  5.6 80.4 %copy-start.3 = (s32[1,4]{1,0:T(1,128)S(1)}, s32[1,4]{1,0:T(1,128)}, u32[]{:S(2)}) copy-start(s32[1,4]{1,0:T(1,128)} %param.11) | copy-start | bytes 52
  8.5 77.6 %collective-permute-start.5 = (f32[3080,256]{1,0:T(8,128)}, f32[3080,256]{1,0:T(8,128)S(1)}, u32[]{:S(2)}, u32[]{:S(2)}) collective-permute-start(f32[3080,256]{1,0:T(8,128)} %get-tuple-element.18.refs_1_), channel_id=1, source_target_pairs={{0,26},{2,0},{4,30},{6,4},{8,2},{10,8},{12,6},{14,12},{16,10},{18,... | collective-permute-start | bytes 9461768 | tf_op jit(solution)/shard_map/ppermute | solution.py:354
  11.3 46.4 %collective-permute-start.3 = (f32[1032,256]{1,0:T(8,128)S(1)}, f32[1032,256]{1,0:T(8,128)}, u32[]{:S(2)}, u32[]{:S(2)}) collective-permute-start(f32[1032,256]{1,0:T(8,128)S(1)} %get-tuple-element.19), channel_id=1, source_target_pairs={{0,30},{2,4},{4,2},{6,0},{8,6},{10,12},{12,10},{14,8},{16,14},{18,... | collective-permute-start | bytes 3170312 | tf_op jit(solution)/shard_map/ppermute | solution.py:354
  13.2 55.8 %collective-permute-start.4 = (f32[1032,256]{1,0:T(8,128)S(1)}, f32[1032,256]{1,0:T(8,128)}, u32[]{:S(2)}, u32[]{:S(2)}) collective-permute-start(f32[1032,256]{1,0:T(8,128)S(1)} %get-tuple-element.20), channel_id=1, source_target_pairs={{0,30},{2,4},{4,2},{6,0},{8,6},{10,12},{12,10},{14,8},{16,14},{18,... | collective-permute-start | bytes 3170312 | tf_op jit(solution)/shard_map/ppermute | solution.py:354
  13.4 68.9 %collective-permute-start.1 = (f32[1032,256]{1,0:T(8,128)S(1)}, f32[1032,256]{1,0:T(8,128)}, u32[]{:S(2)}, u32[]{:S(2)}) collective-permute-start(f32[1032,256]{1,0:T(8,128)S(1)} %get-tuple-element.17), channel_id=1, source_target_pairs={{0,30},{2,4},{4,2},{6,0},{8,6},{10,12},{12,10},{14,8},{16,14},{18,... | collective-permute-start | bytes 3170312 | tf_op jit(solution)/shard_map/ppermute | solution.py:354
  57.7 25.0 %collective-permute-start.6 = (f32[1032,256]{1,0:T(8,128)}, f32[1032,256]{1,0:T(8,128)}, u32[]{:S(2)}, u32[]{:S(2)}) collective-permute-start(f32[1032,256]{1,0:T(8,128)} %collective-permute-done.3.refs_2_.refs_5_), channel_id=1, source_target_pairs={{0,2},{2,0},{4,30},{6,4},{8,10},{10,8},{12,6},{14,12},{16,18},{18,... | collective-permute-start | bytes 3170312 | tf_op jit(solution)/shard_map/ppermute | solution.py:354
  69.0 15.3 %collective-permute-start.7 = (f32[1032,256]{1,0:T(8,128)}, f32[1032,256]{1,0:T(8,128)}, u32[]{:S(2)}, u32[]{:S(2)}) collective-permute-start(f32[1032,256]{1,0:T(8,128)} %collective-permute-done.4.refs_3_.refs_6_), channel_id=1, source_target_pairs={{0,2},{2,0},{4,30},{6,4},{8,10},{10,8},{12,6},{14,12},{16,18},{18,... | collective-permute-start | bytes 3170312 | tf_op jit(solution)/shard_map/ppermute | solution.py:354
  82.3 11.7 %collective-permute-start.2 = (f32[1032,256]{1,0:T(8,128)}, f32[1032,256]{1,0:T(8,128)}, u32[]{:S(2)}, u32[]{:S(2)}) collective-permute-start(f32[1032,256]{1,0:T(8,128)} %collective-permute-done.1.refs_4_.refs_7_), channel_id=1, source_target_pairs={{0,2},{2,0},{4,30},{6,4},{8,10},{10,8},{12,6},{14,12},{16,18},{18,... | collective-permute-start | bytes 3170312 | tf_op jit(solution)/shard_map/ppermute | solution.py:354
  82.7 15.0 %collective-permute-start.8 = (f32[1032,256]{1,0:T(8,128)}, f32[1032,256]{1,0:T(8,128)}, u32[]{:S(2)}, u32[]{:S(2)}) collective-permute-start(f32[1032,256]{1,0:T(8,128)} %collective-permute-done.6.refs_2_), channel_id=1, source_target_pairs={{6,4},{14,12},{22,20},{30,28},{7,5},{15,13},{23,21},{31,29}} | collective-permute-start | bytes 3170312 | tf_op jit(solution)/shard_map/ppermute | solution.py:364
  84.4 13.4 %collective-permute-start.9 = (f32[1032,256]{1,0:T(8,128)}, f32[1032,256]{1,0:T(8,128)}, u32[]{:S(2)}, u32[]{:S(2)}) collective-permute-start(f32[1032,256]{1,0:T(8,128)} %collective-permute-done.7.refs_3_), channel_id=1, source_target_pairs={{6,4},{14,12},{22,20},{30,28},{7,5},{15,13},{23,21},{31,29}} | collective-permute-start | bytes 3170312 | tf_op jit(solution)/shard_map/ppermute | solution.py:364
  94.0 3.8 %collective-permute-start.10 = (f32[1032,256]{1,0:T(8,128)}, f32[1032,256]{1,0:T(8,128)}, u32[]{:S(2)}, u32[]{:S(2)}) collective-permute-start(f32[1032,256]{1,0:T(8,128)} %collective-permute-done.2.refs_4_), channel_id=1, source_target_pairs={{6,4},{14,12},{22,20},{30,28},{7,5},{15,13},{23,21},{31,29}} | collective-permute-start | bytes 3170312 | tf_op jit(solution)/shard_map/ppermute | solution.py:364
  95.8 20.5 %collective-permute-start = (s32[40]{0:T(128)S(1)}, s32[40]{0:T(128)S(1)}, u32[]{:S(2)}, u32[]{:S(2)}) collective-permute-start(s32[40]{0:T(128)S(1)} %reshape_reshape.3), channel_id=1, source_target_pairs={{0,1},{1,0},{2,3},{3,2},{4,5},{5,4},{6,7},{7,6},{8,9},{9,8},{10,11... | collective-permute-start | bytes 488 | tf_op jit(solution)/shard_map/ppermute | solution.py:340
  97.7 1.9 %copy-start = (bf16[12,2,256,256]{3,2,1,0:T(8,128)(2,1)S(1)}, bf16[12,2,256,256]{3,2,1,0:T(8,128)(2,1)}, u32[]{:S(2)}) copy-start(bf16[12,2,256,256]{3,2,1,0:T(8,128)(2,1)} %get-tuple-element.25.refs_13_) | copy-start | bytes 9437188
  99.6 1.8 %copy-start.2 = (f32[11,256,256]{2,1,0:T(8,128)S(1)}, f32[11,256,256]{2,1,0:T(8,128)}, u32[]{:S(2)}) copy-start(f32[11,256,256]{2,1,0:T(8,128)} %get-tuple-element.24.refs_12_) | copy-start | bytes 8650756

commit v6 on v5

--- a/solution.py
+++ b/solution.py
@@ -12,16 +12,16 @@
 CB = 4
 STEPS = 4
 LIST_ROWS = 8
-X_PARTS = 3
-LAST = 0
+SHARES = (4, 8, 12)
+X_PARTS = len(SHARES)
+FETCH = 5
 VMEM = pl.BlockSpec(memory_space=pltpu.VMEM)
 SMEM = pl.BlockSpec(memory_space=pltpu.SMEM)
 
 
-def pack_kernel(share, places, x, *refs):
+def pack_kernel(cuts, places, x, *refs):
     *targets, sems = refs
-    n_x, bs = places.shape[0], x.shape[-1]
-    cuts = [(0, n_x)] + [(p * share, share) for p in range(n_x // share)]
+    bs = x.shape[-1]
     copies = [
         pltpu.make_async_copy(x.at[pl.ds(first * bs, n * bs)], target.at[pl.ds(0, n * bs)], sems.at[i])
         for i, (target, (first, n)) in enumerate(zip(targets, cuts))
@@ -39,19 +39,20 @@
         copy.wait()
 
 
-def pack(x, places, share):
+def pack(x, places):
     n_x, bs = places.shape[0], x.shape[-1]
-    sizes = [n_x] + [share] * (n_x // share)
+    ends = [0] + [n_x * share // 12 for share in SHARES]
+    cuts = [(0, n_x)] + [(lo, hi - lo) for lo, hi in zip(ends, ends[1:])]
     return pl.pallas_call(
-        functools.partial(pack_kernel, share),
+        functools.partial(pack_kernel, cuts),
         in_specs=[SMEM, pl.BlockSpec(memory_space=pl.ANY)],
-        out_specs=[VMEM] * len(sizes),
-        out_shape=[jax.ShapeDtypeStruct((n * bs + LIST_ROWS, bs), x.dtype) for n in sizes],
-        scratch_shapes=[pltpu.SemaphoreType.DMA((len(sizes),))],
+        out_specs=[VMEM] * len(cuts),
+        out_shape=[jax.ShapeDtypeStruct((n * bs + LIST_ROWS, bs), x.dtype) for _, n in cuts],
+        scratch_shapes=[pltpu.SemaphoreType.DMA((len(cuts),))],
         compiler_params=pltpu.CompilerParams(vmem_limit_bytes=16 * 2**20),
         cost_estimate=pl.CostEstimate(flops=0, bytes_accessed=2**20, transcendentals=0),
         name="pack",
-    )(places, x)
+    )(places, pltpu.with_memory_space_constraint(x, pltpu.HBM))
 
 
 def halves(values):
@@ -74,7 +75,7 @@
         target[read(entry, 0) * columns + read(entry, 1)] = entry
 
 
-def add_products(acc, n_out, bs, maps, todo, left_place, n_left, left, right):
+def add_products(acc, n_out, bs, maps, todo, left_place, n_left, left, right, arrivals=()):
     r_map, o_map = maps
     unroll = todo.shape[0] - n_left * CB
 
@@ -85,10 +86,6 @@
             todo[count] = (i * 64 + jnp.maximum(j, 0)) * 64 + jnp.maximum(m, 0)
             count = count + ((j >= 0) & (m >= 0)).astype(jnp.int32)
         return count
-
-    count = lax.fori_loop(0, n_left, collect, jnp.int32(0))
-    for u in range(unroll):
-        todo[count + u] = n_out
 
     def several(q, carry):
         for u in range(unroll):
@@ -99,7 +96,18 @@
             acc[m] += dot(left_high, right_high) + dot(left_high, right_low) + dot(left_low, right_high)
         return carry
 
-    lax.fori_loop(0, (count + unroll - 1) // unroll, several, 0)
+    ends, count, entry = [], jnp.int32(0), 0
+    for entries, _ in arrivals or [(n_left, None)]:
+        count = lax.fori_loop(entry, entry + entries, collect, count)
+        entry += entries
+        ends.append(count // unroll)
+    for u in range(unroll):
+        todo[count + u] = n_out
+    ends[-1] = (count + unroll - 1) // unroll
+    for at, end in enumerate(ends):
+        if arrivals:
+            arrivals[at][1]()
+        lax.fori_loop(ends[at - 1] if at else 0, end, several, 0)
 
 
 def own_kernel(slot, n_left, n_x, plan, n_arrays, chooses, last, owner, pairs, left_list, *refs):
@@ -130,11 +138,12 @@
         copy.start()
 
     def fetch(at, parts, rows, lists):
-        copies = []
+        copies, entry = [], 0
         for p, array in enumerate(parts):
-            n = n_x // len(parts)
             right = arrays[array]
-            target = rows.at[pl.ds(p * n * bs, n * bs)]
+            n = right.shape[0] // bs
+            target = rows.at[pl.ds(entry * bs, n * bs)]
+            entry += n
             copies.append(pltpu.make_async_copy(right.at[pl.ds(0, n * bs)], target, sems.at[at + 2 * p]))
             listed = right.at[pl.ds(n * bs, LIST_ROWS)]
             copies.append(pltpu.make_async_copy(listed, lists[p], sems.at[at + 2 * p + 1]))
@@ -142,12 +151,12 @@
 
     def copies_of(parts, here):
         if here:
-            return fetch(5, parts, here_rows, here_lists)
-        return fetch(5 + 2 * X_PARTS, parts, there_rows, there_lists)
-
-    def place_in(lists, count):
-        n = n_x // count
-        return lambda j, d: lists[j // n][0, 2 * (j % n) + d].astype(jnp.int32)
+            return fetch(6, parts, here_rows, here_lists)
+        return fetch(6 + 2 * X_PARTS, parts, there_rows, there_lists)
+
+    def place_in(lists, parts):
+        at = [(p, j) for p, array in enumerate(parts) for j in range(arrays[array].shape[0] // bs)]
+        return lambda j, d: lists[at[j][0]][0, 2 * at[j][1] + d].astype(jnp.int32)
 
     def each(then):
         for step, places, parts in plan:
@@ -167,9 +176,9 @@
         for copy in copies_of(parts, here):
             copy.wait()
         if here:
-            fill_map(r_map, KB * CB, place_in(here_lists, len(parts)), n_x, CB)
+            fill_map(r_map, KB * CB, place_in(here_lists, parts), n_x, CB)
             return
-        read = place_in(there_lists, len(parts))
+        read = place_in(there_lists, parts)
         for j in range(n_x):
             for d in range(2):
                 chosen_list[2 * (slot * n_x + j) + d] = read(j, d)
@@ -202,10 +211,12 @@
         chosen[mark + j, 0], chosen[mark + j, 1] = halves(block(there_rows, j, bs))
         return carry
 
-    lax.fori_loop(0, n_x, split, 0)
-    if not last:
-        out_copies.append(pltpu.make_async_copy(chosen, chosen_out, sems.at[4]))
-        out_copies[1].start()
+    for q, (lo, hi) in enumerate(((0, n_x // 2), (n_x // 2, n_x))):
+        lax.fori_loop(lo, hi, split, 0)
+        if not last:
+            rows = pl.ds(lo, hi - lo)
+            out_copies.append(pltpu.make_async_copy(chosen.at[rows], chosen_out.at[rows], sems.at[4 + q]))
+            out_copies[-1].start()
     for copy in out_copies:
         copy.wait()
 
@@ -224,10 +235,11 @@
         plan.append((step, places, at))
     n_x = sum(part.shape[0] // bs for part in choices[0][2])
     anywhere = pl.BlockSpec(memory_space=pl.ANY)
-    smem, operands = [owner, pairs, left_list], [pltpu.with_memory_space_constraint(left, pltpu.HBM), *arrays]
+    smem = [owner, pairs, left_list]
+    operands = [pltpu.with_memory_space_constraint(rows, pltpu.HBM) for rows in (left, *arrays)]
     if before is not None:
         smem.append(before[2])
-        operands += before[:2]
+        operands += [pltpu.with_memory_space_constraint(one, pltpu.HBM) for one in before[:2]]
     acc_shape, chosen_shape = (n_out + 1, bs, bs), ((slot + 1) * n_x, 2, bs, bs)
     kind = pltpu.VMEM if last else pltpu.HBM
     out_shape, out_specs = [kind(acc_shape, jnp.float32)], [pl.BlockSpec(memory_space=kind)]
@@ -241,7 +253,7 @@
         pltpu.SMEM(((KB + 1) * CB,), jnp.int32),
         pltpu.SMEM((RB * CB,), jnp.int32),
         pltpu.SMEM((n_left * CB + 4,), jnp.int32),
-        pltpu.SemaphoreType.DMA((5 + 4 * X_PARTS,)),
+        pltpu.SemaphoreType.DMA((6 + 4 * X_PARTS,)),
     ]
     if not last:
         scratch += [pltpu.VMEM(acc_shape, jnp.float32), pltpu.VMEM(chosen_shape, jnp.bfloat16)]
@@ -261,69 +273,60 @@
 LAST_LIMIT = 24 * 2**20
 
 
-def their_kernel(n_s, first, last, pairs, late, right_list, left, before, chosen, *refs):
-    if last:
-        out, acc, left_rows, r_map, o_map, todo, sems = refs
-    else:
-        acc, left_rows, r_map, o_map, todo, sems = refs
+def last_kernel(n_s, pairs, late, right_list, left, before, chosen, out, acc, left_rows, r_map, o_map, todo, sems):
     n_out, bs = pairs.shape[0], left.shape[-1]
-    n_left, n_right = left.shape[0] // bs, chosen.shape[0]
-    depth = r_map.shape[0] // ((KB + 1) * CB)
+    n_right = chosen.shape[0]
+    depth = left.shape[0] // (n_s * bs)
     n_x = n_right // depth
-    part = left.shape[0] // 4
-    fetched = []
-    for q in range(4):
-        rows = pl.ds(q * part, part)
-        fetched.append(pltpu.make_async_copy(left.at[rows], left_rows.at[rows], sems.at[q]))
-    for copy in fetched:
+    n_left = left.shape[0] // bs
+    arrivals = []
+    for q, (lo, hi) in enumerate(zip(range(0, n_left, FETCH), [*range(FETCH, n_left, FETCH), n_left])):
+        rows = pl.ds(lo * bs, (hi - lo) * bs)
+        copy = pltpu.make_async_copy(left.at[rows], left_rows.at[rows], sems.at[n_out + q])
         copy.start()
-    for m in range(n_out):
-        acc[m] = before[m]
+        arrivals.append((hi - lo, copy.wait))
     fill_map(o_map, RB * CB, lambda m, d: pairs[m, d], n_out, CB)
     for cell in range(r_map.shape[0]):
         r_map[cell] = -1
     for j in range(n_right):
         r_map[(j // n_x * (KB + 1) + right_list[2 * j]) * CB + right_list[2 * j + 1]] = j
-    for copy in fetched:
+    for m in range(n_out):
+        acc[m] = before[m]
+
+    def left_place(i):
+        return late[2 * i], (i // n_s * (KB + 1) + late[2 * i + 1]) * CB
+
+    add_products(
+        acc, n_out, bs, (r_map, o_map), todo, left_place, n_left, left_rows, lambda j: (chosen[j, 0], chosen[j, 1]), arrivals
+    )
+    copies = [pltpu.make_async_copy(acc.at[m], out.at[m], sems.at[m]) for m in range(n_out)]
+    for copy in copies:
+        copy.start()
+    for copy in copies:
         copy.wait()
 
-    def left_place(i):
-        return late[2 * (first + i)], ((first + i) // n_s * (KB + 1) + late[2 * (first + i) + 1]) * CB
-
-    add_products(
-        acc, n_out, bs, (r_map, o_map), todo, left_place, n_left, left_rows, lambda j: (chosen[j, 0], chosen[j, 1])
-    )
-    if last:
-        copies = [pltpu.make_async_copy(acc.at[m], out.at[m], sems.at[4 + m]) for m in range(n_out)]
-        for copy in copies:
-            copy.start()
-        for copy in copies:
-            copy.wait()
-
-
-def their_products(pairs, late, left, first, n_s, before, last):
+
+def last_products(pairs, late, left, n_s, acc, chosen, right_list):
     bs = left.shape[-1]
-    acc, chosen, right_list = before
-    n_out, n_left = pairs.shape[0], left.shape[0] // bs
-    depth = late.size // (2 * n_s)
+    n_out, depth = pairs.shape[0], left.shape[0] // (n_s * bs)
     anywhere = pl.BlockSpec(memory_space=pl.ANY)
     return pl.pallas_call(
-        functools.partial(their_kernel, n_s, first, last),
+        functools.partial(last_kernel, n_s),
         in_specs=[SMEM] * 3 + [anywhere] + [VMEM] * 2,
-        out_specs=anywhere if last else VMEM,
-        out_shape=jax.ShapeDtypeStruct((n_out, bs, bs) if last else acc.shape, jnp.float32),
-        scratch_shapes=([pltpu.VMEM(acc.shape, acc.dtype)] if last else [])
-        + [
+        out_specs=anywhere,
+        out_shape=jax.ShapeDtypeStruct((n_out, bs, bs), jnp.float32),
+        scratch_shapes=[
+            pltpu.VMEM(acc.shape, acc.dtype),
             pltpu.VMEM(left.shape, left.dtype),
             pltpu.SMEM((depth * (KB + 1) * CB,), jnp.int32),
             pltpu.SMEM((RB * CB,), jnp.int32),
-            pltpu.SMEM((n_left * CB + (8 if n_left > 8 else 4),), jnp.int32),
-            pltpu.SemaphoreType.DMA((4 + n_out,)),
+            pltpu.SMEM((depth * n_s * CB + 8,), jnp.int32),
+            pltpu.SemaphoreType.DMA((n_out + pl.cdiv(depth * n_s, FETCH),)),
         ],
         compiler_params=pltpu.CompilerParams(vmem_limit_bytes=LAST_LIMIT),
         cost_estimate=pl.CostEstimate(flops=0, bytes_accessed=2**20, transcendentals=0),
-        name="their_products",
-    )(pairs, late, right_list, left, acc, chosen)
+        name="last_products",
+    )(pairs, late, right_list, pltpu.with_memory_space_constraint(left, pltpu.HBM), acc, chosen)
 
 
 def per_device(s_blocks, s_list, x_blocks, x_list, c_list, owner):
@@ -337,18 +340,13 @@
     swapped = width == 2
     if swapped:
         partner = [(0, 1), (1, 0)]
+        came = lax.ppermute(s_own, "bcast", partner)
         their_list = lax.ppermute(s_own_list.reshape(-1), "bcast", partner)
-        cuts = (0, depth * n_s - LAST, depth * n_s)
-        chunks = [s_own[lo * bs : hi * bs] for lo, hi in zip(cuts, cuts[1:])]
-        if LAST:
-            chunks[0], their_list = lax.optimization_barrier((chunks[0], their_list))
-        came = [lax.ppermute(chunk, "bcast", partner) for chunk in chunks if chunk.size]
     else:
         held = lax.all_gather(s_own, "bcast")
         held_lists = lax.all_gather(s_own_list, "bcast")
 
-    share = n_x // X_PARTS
-    everything, *parts = pack(x_own, x_own_list, share)
+    everything, *parts = pack(x_own, x_own_list)
 
     def moved(packed, to):
         return [lax.ppermute(part, "loop", [(g, (g + to[g % 4]) % length) for g in range(length)]) for part in packed]
@@ -382,11 +380,7 @@
             choices.append(last_choice())
         fit = [choice for choice in choices if choice[0] // width == slot]
         sums = own_products(owner, pairs, s_own, slot, s_own_list, n_s, fit, sums, True, slot == depth - 1)
-    for q, rows in enumerate(came):
-        final = q == len(came) - 1
-        added = their_products(pairs, their_list, rows, cuts[q], n_s, sums, final)
-        sums = (added, *sums[1:])
-    return sums[0][None, None]
+    return last_products(pairs, their_list, came, n_s, *sums)[None, None]
 
 
 def solution(mesh):

time: 129 us -> 126 us (0.977); the launches traced: 127 us -> 127 us
  Pallas kernels: 30.7 us -> 36.6 us
  local copies, waits for them, and re-layouts: 6.83 us -> 2.22 us
  starting transfers between devices: 16.3 us -> 13.6 us
  waiting for transfers between devices: 72.7 us -> 74.7 us
    unnamed x14 -> x12, local copies, waits for them, and re-layouts: 5.7 us -> 1.09 us
    pallas_call x2, Pallas kernels: 17.5 us -> 22.1 us  [own_products(): pl.pallas_call(functools.partial(own_kernel, slot, n_left, n_x, plan, len...]
    ppermute x1, waiting for transfers between devices: 5.24 us -> 7.22 us  [per_device(): their_list = lax.ppermute(s_own_list.reshape(-1), 'bcast', partner)]
    ppermute x1, starting transfers between devices: 1.91 us -> 0.07 us  [per_device(): their_list = lax.ppermute(s_own_list.reshape(-1), 'bcast', partner)]
  transfers between devices with their start and end apart: 12 -> 12, of which waited for: 4 -> 4; matrix products, arithmetic and copies ran while one was open for 1% -> 1% of each run, Pallas kernels for 16% -> 20%
where the time goes in v6:
time: 126 us; the launch traced here: 127 us
  waiting for transfers between devices  74.7 us (59%)
  Pallas kernels  36.6 us (29%)
  starting transfers between devices  13.6 us (11%)
  local copies, waits for them, and re-layouts  2.22 us (2%)
    ppermute x7, waiting for transfers between devices, moved(): lax.ppermute(part, 'loop', [(g, (g + to[g % 4]) % length) for g in range(...  67.5 us
    pallas_call x2, Pallas kernels, own_products(): pl.pallas_call(functools.partial(own_kernel, slot, n_left, n_x, plan, len...  22.1 us
    pallas_call x1, Pallas kernels, last_products(): pl.pallas_call(functools.partial(last_kernel, n_s), in_specs=[SMEM] * 3 +...  10.9 us
    ppermute x1, waiting for transfers between devices, per_device(): their_list = lax.ppermute(s_own_list.reshape(-1), 'bcast', partner)  7.22 us
    ppermute x7, starting transfers between devices, moved(): lax.ppermute(part, 'loop', [(g, (g + to[g % 4]) % length) for g in range(...  6.49 us
    ppermute x3, starting transfers between devices, last_choice(): lax.ppermute(part, 'loop', [(g, g - 1) for g in range(3, length, 4)])  4.12 us
    pallas_call x1, Pallas kernels, pack(): pl.pallas_call(functools.partial(pack_kernel, cuts), in_specs=[SMEM, pl.B...  3.5 us
    ppermute x1, starting transfers between devices, per_device(): came = lax.ppermute(s_own, 'bcast', partner)  2.97 us
  transfers between devices with their start and end apart: 12, of which 4 were waited for; matrix products, arithmetic and copies ran while one was open for 1% of the time, Pallas kernels for 20%

profile of v6, /device:TPU:0, one launch (start us, length us, event | category | flops | bytes accessed | tf_op | source)
XLA Modules:
  0.0 127.3 jit_solution(5549097114619031586)
XLA Ops:
  0.0 3.0 %collective-permute-start.11 = (f32[5120,256]{1,0:T(8,128)}, f32[5120,256]{1,0:T(8,128)}, u32[]{:S(2)}, u32[]{:S(2)}) collective-permute-start(f32[5120,256]{1,0:T(8,128)} %bitcast.10), channel_id=1, source_target_pairs={{0,1},{1,0},{2,3},{3,2},{4,5},{5,4},{6,7},{7,6},{8,9},{9,8},{10,11... | collective-permute-start | bytes 15728648 | tf_op jit(solution)/shard_map/ppermute | solution.py:343
  3.0 0.8 copy.17.places
  3.7 0.0 copy-start.4
  3.7 0.0 copy-start.3
  3.7 0.0 copy-start.1
  3.7 3.5 %pack.1 = (f32[3080,256]{1,0:T(8,128)S(1)}, f32[1032,256]{1,0:T(8,128)S(1)}, f32[1032,256]{1,0:T(8,128)S(1)}, f32[1032,256]{1,0:T(8,128)S(1)}) custom-call(s32[12,2]{1,0:T(8,128)S(1)} %copy.17.places, f32[3072,256]{1,0:T(8,128)} %bitcast.13), custom_call_target="tpu_custom_call" | custom-call | bytes 1048576 | tf_op jit(solution)/shard_map/pack/pallas_call | solution.py:46
  7.2 0.0 copy-start
  7.3 2.8 %collective-permute-start.5 = (f32[3080,256]{1,0:T(8,128)S(1)}, f32[3080,256]{1,0:T(8,128)}, u32[]{:S(2)}, u32[]{:S(2)}) collective-permute-start(f32[3080,256]{1,0:T(8,128)S(1)} %get-tuple-element.18.refs_1_), channel_id=1, source_target_pairs={{0,26},{2,0},{4,30},{6,4},{8,2},{10,8},{12,6},{14,12},{16,10},{18,... | collective-permute-start | bytes 9461768 | tf_op jit(solution)/shard_map/ppermute | solution.py:352
  10.1 1.9 %collective-permute-start.3 = (f32[1032,256]{1,0:T(8,128)S(1)}, f32[1032,256]{1,0:T(8,128)}, u32[]{:S(2)}, u32[]{:S(2)}) collective-permute-start(f32[1032,256]{1,0:T(8,128)S(1)} %get-tuple-element.19), channel_id=1, source_target_pairs={{0,30},{2,4},{4,2},{6,0},{8,6},{10,12},{12,10},{14,8},{16,14},{18,... | collective-permute-start | bytes 3170312 | tf_op jit(solution)/shard_map/ppermute | solution.py:352
  12.0 0.2 collective-permute-start.4
  12.2 1.4 %collective-permute-start.1 = (f32[1032,256]{1,0:T(8,128)S(1)}, f32[1032,256]{1,0:T(8,128)}, u32[]{:S(2)}, u32[]{:S(2)}) collective-permute-start(f32[1032,256]{1,0:T(8,128)S(1)} %get-tuple-element.17), channel_id=1, source_target_pairs={{0,30},{2,4},{4,2},{6,0},{8,6},{10,12},{12,10},{14,8},{16,14},{18,... | collective-permute-start | bytes 3170312 | tf_op jit(solution)/shard_map/ppermute | solution.py:352
  13.6 42.7 %collective-permute-done.3.refs_2_.refs_5_ = f32[1032,256]{1,0:T(8,128)} collective-permute-done((f32[1032,256]{1,0:T(8,128)S(1)}, f32[1032,256]{1,0:T(8,128)}, u32[]{:S(2)}, u32[]{:S(2)}) %collective-permute-start.3) | collective-permute-done | bytes 1056800 | tf_op jit(solution)/shard_map/ppermute | solution.py:352
  56.3 0.0 collective-permute-start.6
  56.3 11.3 %collective-permute-done.4.refs_3_.refs_6_ = f32[1032,256]{1,0:T(8,128)} collective-permute-done((f32[1032,256]{1,0:T(8,128)S(1)}, f32[1032,256]{1,0:T(8,128)}, u32[]{:S(2)}, u32[]{:S(2)}) %collective-permute-start.4) | collective-permute-done | bytes 1056800 | tf_op jit(solution)/shard_map/ppermute | solution.py:352
  67.6 0.0 collective-permute-start.7
  67.6 13.5 %collective-permute-done.1.refs_4_.refs_7_ = f32[1032,256]{1,0:T(8,128)} collective-permute-done((f32[1032,256]{1,0:T(8,128)S(1)}, f32[1032,256]{1,0:T(8,128)}, u32[]{:S(2)}, u32[]{:S(2)}) %collective-permute-start.1) | collective-permute-done | bytes 1056800 | tf_op jit(solution)/shard_map/ppermute | solution.py:352
  81.1 0.2 collective-permute-start.2
  81.2 0.0 copy-done.4
  81.2 0.1 copy.22.pairs
  81.3 0.0 copy-done.3
  81.3 0.1 reshape.9
  81.4 0.1 copy.21.left_list
  81.5 0.0 collective-permute-done.6.refs_2_
  81.5 1.7 %collective-permute-start.8 = (f32[1032,256]{1,0:T(8,128)}, f32[1032,256]{1,0:T(8,128)}, u32[]{:S(2)}, u32[]{:S(2)}) collective-permute-start(f32[1032,256]{1,0:T(8,128)} %collective-permute-done.6.refs_2_), channel_id=1, source_target_pairs={{6,4},{14,12},{22,20},{30,28},{7,5},{15,13},{23,21},{31,29}} | collective-permute-start | bytes 3170312 | tf_op jit(solution)/shard_map/ppermute | solution.py:362
  83.2 0.0 collective-permute-done.7.refs_3_
  83.2 1.7 %collective-permute-start.9 = (f32[1032,256]{1,0:T(8,128)}, f32[1032,256]{1,0:T(8,128)}, u32[]{:S(2)}, u32[]{:S(2)}) collective-permute-start(f32[1032,256]{1,0:T(8,128)} %collective-permute-done.7.refs_3_), channel_id=1, source_target_pairs={{6,4},{14,12},{22,20},{30,28},{7,5},{15,13},{23,21},{31,29}} | collective-permute-start | bytes 3170312 | tf_op jit(solution)/shard_map/ppermute | solution.py:362
  84.9 0.0 collective-permute-done.5.refs_5_.refs_8_
  84.9 0.0 copy-done
  84.9 0.0 copy-done.1
  84.9 12.3 %own_products.2 = (f32[11,256,256]{2,1,0:T(8,128)}, bf16[12,2,256,256]{3,2,1,0:T(8,128)(2,1)}, s32[24]{0:T(128)S(1)}) custom-call(s32[4]{0:T(128)S(1)} %bitcast.8, s32[10,2]{1,0:T(8,128)S(1)} %copy.22.pairs, s32[20,2]{1,0:T(8,128)S(1)} %copy.21.left_list, f32[5120,256]{1,0:T(8,128)} %bitcast.11, f32[3080,256]{1,0:T(8,128)} %copy-done, ...), custom_call_target="tpu_custom_call" | custom-call | bytes 1048576 | tf_op jit(solution)/shard_map/own_products/pallas_call | solution.py:260
  97.2 0.0 collective-permute-done.2.refs_4_
  97.2 0.7 collective-permute-start.10
  97.9 0.1 copy.15
  98.0 0.1 reshape_reshape.3
  98.1 0.1 collective-permute-start
  98.2 0.0 collective-permute-done.8.refs_9_
  98.2 0.0 collective-permute-done.9.refs_10_
  98.2 0.0 collective-permute-done.10.refs_11_
  98.2 0.0 copy-start.2
  98.2 1.0 copy-done.2
  99.2 9.9 %own_products.3 = (f32[11,256,256]{2,1,0:T(8,128)S(1)}, bf16[24,2,256,256]{3,2,1,0:T(8,128)(2,1)S(1)}, s32[48]{0:T(128)S(1)}) custom-call(s32[4]{0:T(128)S(1)} %bitcast.9, s32[10,2]{1,0:T(8,128)S(1)} %copy.22.pairs, s32[20,2]{1,0:T(8,128)S(1)} %copy.21.left_list, s32[24]{0:T(128)S(1)} %get-tuple-element.22.refs_0_, f32[5120,256]{1,0:T(8,128)} %bitcast.12, ...), custom_call_target="tpu_custom_call" | custom-call | bytes 1048576 | tf_op jit(solution)/shard_map/own_products/pallas_call | solution.py:260
  109.1 7.2 %collective-permute-done.late = s32[40]{0:T(128)S(1)} collective-permute-done((s32[40]{0:T(128)S(1)}, s32[40]{0:T(128)S(1)}, u32[]{:S(2)}, u32[]{:S(2)}) %collective-permute-start) | collective-permute-done | bytes 192 | tf_op jit(solution)/shard_map/ppermute | solution.py:344
  116.3 0.0 collective-permute-done.11.left
  116.3 10.9 %last_products.1 = f32[10,256,256]{2,1,0:T(8,128)} custom-call(s32[10,2]{1,0:T(8,128)S(1)} %copy.22.pairs, s32[40]{0:T(128)S(1)} %collective-permute-done.late, s32[48]{0:T(128)S(1)} %get-tuple-element.26.right_list, f32[5120,256]{1,0:T(8,128)} %collective-permute-done.11.left, f32[11,256,256]{2,1,0:T(8,128)S(1)} %get-tuple-element.27.before, ...), custom_call_target="tpu_custom_call" | custom-call | bytes 1048576 | tf_op jit(solution)/shard_map/last_products/pallas_call | solution.py:313
  (1 shorter events, 0.0 us)
Async XLA Ops:
  0.0 116.3 %collective-permute-start.11 = (f32[5120,256]{1,0:T(8,128)}, f32[5120,256]{1,0:T(8,128)}, u32[]{:S(2)}, u32[]{:S(2)}) collective-permute-start(f32[5120,256]{1,0:T(8,128)} %bitcast.10), channel_id=1, source_target_pairs={{0,1},{1,0},{2,3},{3,2},{4,5},{5,4},{6,7},{7,6},{8,9},{9,8},{10,11... | collective-permute-start | bytes 15728648 | tf_op jit(solution)/shard_map/ppermute | solution.py:343
  3.7 77.5 %copy-start.4 = (s32[1,1,10,2]{2,3,1,0:T(2,128)S(1)}, s32[1,1,10,2]{2,3,1,0:T(2,128)}, u32[]{:S(2)}) copy-start(s32[1,1,10,2]{2,3,1,0:T(2,128)} %param.10) | copy-start | bytes 244
  3.7 77.6 %copy-start.3 = (s32[1,1,2,10,2]{3,4,2,1,0:T(2,128)S(1)}, s32[1,1,2,10,2]{3,4,2,1,0:T(2,128)}, u32[]{:S(2)}) copy-start(s32[1,1,2,10,2]{3,4,2,1,0:T(2,128)} %param.7) | copy-start | bytes 484
  3.7 81.2 %copy-start.1 = (s32[1,4]{1,0:T(1,128)S(1)}, s32[1,4]{1,0:T(1,128)}, u32[]{:S(2)}) copy-start(s32[1,4]{1,0:T(1,128)} %param.11) | copy-start | bytes 52
  7.2 77.7 %copy-start = (f32[3080,256]{1,0:T(8,128)}, f32[3080,256]{1,0:T(8,128)S(1)}, u32[]{:S(2)}) copy-start(f32[3080,256]{1,0:T(8,128)S(1)} %get-tuple-element.18.refs_1_) | copy-start | bytes 9461764
  7.3 77.7 %collective-permute-start.5 = (f32[3080,256]{1,0:T(8,128)S(1)}, f32[3080,256]{1,0:T(8,128)}, u32[]{:S(2)}, u32[]{:S(2)}) collective-permute-start(f32[3080,256]{1,0:T(8,128)S(1)} %get-tuple-element.18.refs_1_), channel_id=1, source_target_pairs={{0,26},{2,0},{4,30},{6,4},{8,2},{10,8},{12,6},{14,12},{16,10},{18,... | collective-permute-start | bytes 9461768 | tf_op jit(solution)/shard_map/ppermute | solution.py:352
  10.1 46.2 %collective-permute-start.3 = (f32[1032,256]{1,0:T(8,128)S(1)}, f32[1032,256]{1,0:T(8,128)}, u32[]{:S(2)}, u32[]{:S(2)}) collective-permute-start(f32[1032,256]{1,0:T(8,128)S(1)} %get-tuple-element.19), channel_id=1, source_target_pairs={{0,30},{2,4},{4,2},{6,0},{8,6},{10,12},{12,10},{14,8},{16,14},{18,... | collective-permute-start | bytes 3170312 | tf_op jit(solution)/shard_map/ppermute | solution.py:352
  12.0 55.6 %collective-permute-start.4 = (f32[1032,256]{1,0:T(8,128)S(1)}, f32[1032,256]{1,0:T(8,128)}, u32[]{:S(2)}, u32[]{:S(2)}) collective-permute-start(f32[1032,256]{1,0:T(8,128)S(1)} %get-tuple-element.20), channel_id=1, source_target_pairs={{0,30},{2,4},{4,2},{6,0},{8,6},{10,12},{12,10},{14,8},{16,14},{18,... | collective-permute-start | bytes 3170312 | tf_op jit(solution)/shard_map/ppermute | solution.py:352
  12.2 68.9 %collective-permute-start.1 = (f32[1032,256]{1,0:T(8,128)S(1)}, f32[1032,256]{1,0:T(8,128)}, u32[]{:S(2)}, u32[]{:S(2)}) collective-permute-start(f32[1032,256]{1,0:T(8,128)S(1)} %get-tuple-element.17), channel_id=1, source_target_pairs={{0,30},{2,4},{4,2},{6,0},{8,6},{10,12},{12,10},{14,8},{16,14},{18,... | collective-permute-start | bytes 3170312 | tf_op jit(solution)/shard_map/ppermute | solution.py:352
  56.3 25.2 %collective-permute-start.6 = (f32[1032,256]{1,0:T(8,128)}, f32[1032,256]{1,0:T(8,128)}, u32[]{:S(2)}, u32[]{:S(2)}) collective-permute-start(f32[1032,256]{1,0:T(8,128)} %collective-permute-done.3.refs_2_.refs_5_), channel_id=1, source_target_pairs={{0,2},{2,0},{4,30},{6,4},{8,10},{10,8},{12,6},{14,12},{16,18},{18,... | collective-permute-start | bytes 3170312 | tf_op jit(solution)/shard_map/ppermute | solution.py:352
  67.6 15.6 %collective-permute-start.7 = (f32[1032,256]{1,0:T(8,128)}, f32[1032,256]{1,0:T(8,128)}, u32[]{:S(2)}, u32[]{:S(2)}) collective-permute-start(f32[1032,256]{1,0:T(8,128)} %collective-permute-done.4.refs_3_.refs_6_), channel_id=1, source_target_pairs={{0,2},{2,0},{4,30},{6,4},{8,10},{10,8},{12,6},{14,12},{16,18},{18,... | collective-permute-start | bytes 3170312 | tf_op jit(solution)/shard_map/ppermute | solution.py:352
  81.1 16.1 %collective-permute-start.2 = (f32[1032,256]{1,0:T(8,128)}, f32[1032,256]{1,0:T(8,128)}, u32[]{:S(2)}, u32[]{:S(2)}) collective-permute-start(f32[1032,256]{1,0:T(8,128)} %collective-permute-done.1.refs_4_.refs_7_), channel_id=1, source_target_pairs={{0,2},{2,0},{4,30},{6,4},{8,10},{10,8},{12,6},{14,12},{16,18},{18,... | collective-permute-start | bytes 3170312 | tf_op jit(solution)/shard_map/ppermute | solution.py:352
  81.5 16.7 %collective-permute-start.8 = (f32[1032,256]{1,0:T(8,128)}, f32[1032,256]{1,0:T(8,128)}, u32[]{:S(2)}, u32[]{:S(2)}) collective-permute-start(f32[1032,256]{1,0:T(8,128)} %collective-permute-done.6.refs_2_), channel_id=1, source_target_pairs={{6,4},{14,12},{22,20},{30,28},{7,5},{15,13},{23,21},{31,29}} | collective-permute-start | bytes 3170312 | tf_op jit(solution)/shard_map/ppermute | solution.py:362
  83.2 15.0 %collective-permute-start.9 = (f32[1032,256]{1,0:T(8,128)}, f32[1032,256]{1,0:T(8,128)}, u32[]{:S(2)}, u32[]{:S(2)}) collective-permute-start(f32[1032,256]{1,0:T(8,128)} %collective-permute-done.7.refs_3_), channel_id=1, source_target_pairs={{6,4},{14,12},{22,20},{30,28},{7,5},{15,13},{23,21},{31,29}} | collective-permute-start | bytes 3170312 | tf_op jit(solution)/shard_map/ppermute | solution.py:362
  97.2 1.0 collective-permute-start.10
  98.1 18.2 %collective-permute-start = (s32[40]{0:T(128)S(1)}, s32[40]{0:T(128)S(1)}, u32[]{:S(2)}, u32[]{:S(2)}) collective-permute-start(s32[40]{0:T(128)S(1)} %reshape_reshape.3), channel_id=1, source_target_pairs={{0,1},{1,0},{2,3},{3,2},{4,5},{5,4},{6,7},{7,6},{8,9},{9,8},{10,11... | collective-permute-start | bytes 488 | tf_op jit(solution)/shard_map/ppermute | solution.py:344
  98.2 1.0 copy-start.2

commit v7 on v6

--- a/solution.py
+++ b/solution.py
@@ -15,6 +15,7 @@
 SHARES = (4, 8, 12)
 X_PARTS = len(SHARES)
 FETCH = 5
+WIDE, NARROW = 8, 4
 VMEM = pl.BlockSpec(memory_space=pltpu.VMEM)
 SMEM = pl.BlockSpec(memory_space=pltpu.SMEM)
 
@@ -130,12 +131,14 @@
     place, column = lax.axis_index("loop") % 4, lax.axis_index("bcast")
     mark = slot * n_x if last and chooses else 0
 
-    own_copies = [pltpu.make_async_copy(left.at[pl.ds(slot * n_left * bs, n_left * bs)], left_rows, sems.at[0])]
+    half = n_left // 2
+    margins = []
+    for q, (lo, n) in enumerate(((0, half), (half, n_left - half))):
+        source = left.at[pl.ds((slot * n_left + lo) * bs, n * bs)]
+        margins.append(pltpu.make_async_copy(source, left_rows.at[pl.ds(lo * bs, n * bs)], sems.at[q]))
     if adds:
-        own_copies.append(pltpu.make_async_copy(acc_before, acc, sems.at[1]))
-        own_copies.append(pltpu.make_async_copy(chosen_before, chosen.at[pl.ds(0, mark)], sems.at[2]))
-    for copy in own_copies:
-        copy.start()
+        sums_copy = pltpu.make_async_copy(acc_before, acc, sems.at[2])
+        chosen_copy = pltpu.make_async_copy(chosen_before, chosen.at[pl.ds(0, mark)], sems.at[3])
 
     def fetch(at, parts, rows, lists):
         copies, entry = [], 0
@@ -151,8 +154,8 @@
 
     def copies_of(parts, here):
         if here:
-            return fetch(6, parts, here_rows, here_lists)
-        return fetch(6 + 2 * X_PARTS, parts, there_rows, there_lists)
+            return fetch(7, parts, here_rows, here_lists)
+        return fetch(7 + 2 * X_PARTS, parts, there_rows, there_lists)
 
     def place_in(lists, parts):
         at = [(p, j) for p, array in enumerate(parts) for j in range(arrays[array].shape[0] // bs)]
@@ -166,9 +169,10 @@
             if chooses:
                 pl.when(applies & jnp.logical_not(mine))(functools.partial(then, parts, False))
 
-    def start(parts, here):
-        for copy in copies_of(parts, here):
-            copy.start()
+    def start(wanted, parts, here):
+        if here == wanted:
+            for copy in copies_of(parts, here):
+                copy.start()
 
     def land(wanted, parts, here):
         if here != wanted:
@@ -186,7 +190,11 @@
     def left_place(i):
         return left_list[slot * n_left + i, 0], left_list[slot * n_left + i, 1] * CB
 
-    each(start)
+    margins[0].start()
+    each(functools.partial(start, True))
+    if adds:
+        sums_copy.start()
+    margins[1].start()
     fill_map(o_map, RB * CB, lambda m, d: pairs[m, d], n_out, CB)
     if adds:
         for q in range(2 * slot * n_x):
@@ -194,16 +202,22 @@
     else:
         acc[...] = jnp.zeros_like(acc)
     each(functools.partial(land, True))
-    for copy in own_copies:
-        copy.wait()
+    if adds:
+        sums_copy.wait()
+        chosen_copy.start()
+    if chooses:
+        each(functools.partial(start, False))
+    arrivals = [(half, margins[0].wait), (n_left - half, margins[1].wait)]
     add_products(
-        acc, n_out, bs, (r_map, o_map), todo, left_place, n_left, left_rows, lambda j: halves(block(here_rows, j, bs))
+        acc, n_out, bs, (r_map, o_map), todo, left_place, n_left, left_rows, lambda j: halves(block(here_rows, j, bs)), arrivals
     )
+    if adds:
+        chosen_copy.wait()
     if not chooses:
         return
     out_copies = []
     if not last:
-        out_copies.append(pltpu.make_async_copy(acc, acc_out, sems.at[3]))
+        out_copies.append(pltpu.make_async_copy(acc, acc_out, sems.at[4]))
         out_copies[0].start()
     each(functools.partial(land, False))
 
@@ -215,7 +229,7 @@
         lax.fori_loop(lo, hi, split, 0)
         if not last:
             rows = pl.ds(lo, hi - lo)
-            out_copies.append(pltpu.make_async_copy(chosen.at[rows], chosen_out.at[rows], sems.at[4 + q]))
+            out_copies.append(pltpu.make_async_copy(chosen.at[rows], chosen_out.at[rows], sems.at[5 + q]))
             out_copies[-1].start()
     for copy in out_copies:
         copy.wait()
@@ -253,7 +267,7 @@
         pltpu.SMEM(((KB + 1) * CB,), jnp.int32),
         pltpu.SMEM((RB * CB,), jnp.int32),
         pltpu.SMEM((n_left * CB + 4,), jnp.int32),
-        pltpu.SemaphoreType.DMA((6 + 4 * X_PARTS,)),
+        pltpu.SemaphoreType.DMA((7 + 4 * X_PARTS,)),
     ]
     if not last:
         scratch += [pltpu.VMEM(acc_shape, jnp.float32), pltpu.VMEM(chosen_shape, jnp.bfloat16)]
@@ -273,18 +287,18 @@
 LAST_LIMIT = 24 * 2**20
 
 
-def last_kernel(n_s, pairs, late, right_list, left, before, chosen, out, acc, left_rows, r_map, o_map, todo, sems):
+def last_kernel(n_s, pairs, late, right_list, left, before, chosen, out, acc, left_rows, maps, todo, sems):
+    r_map, o_map, l_map = maps
     n_out, bs = pairs.shape[0], left.shape[-1]
-    n_right = chosen.shape[0]
-    depth = left.shape[0] // (n_s * bs)
+    n_right, n_left = chosen.shape[0], left.shape[0] // bs
+    depth = n_left // n_s
     n_x = n_right // depth
-    n_left = left.shape[0] // bs
-    arrivals = []
-    for q, (lo, hi) in enumerate(zip(range(0, n_left, FETCH), [*range(FETCH, n_left, FETCH), n_left])):
-        rows = pl.ds(lo * bs, (hi - lo) * bs)
-        copy = pltpu.make_async_copy(left.at[rows], left_rows.at[rows], sems.at[n_out + q])
-        copy.start()
-        arrivals.append((hi - lo, copy.wait))
+    starts = list(range(0, n_left, FETCH))
+    fetched = []
+    for q, lo in enumerate(starts):
+        rows = pl.ds(lo * bs, min(FETCH, n_left - lo) * bs)
+        fetched.append(pltpu.make_async_copy(left.at[rows], left_rows.at[rows], sems.at[n_out + q]))
+        fetched[q].start()
     fill_map(o_map, RB * CB, lambda m, d: pairs[m, d], n_out, CB)
     for cell in range(r_map.shape[0]):
         r_map[cell] = -1
@@ -293,17 +307,72 @@
     for m in range(n_out):
         acc[m] = before[m]
 
-    def left_place(i):
-        return late[2 * i], (i // n_s * (KB + 1) + late[2 * i + 1]) * CB
-
-    add_products(
-        acc, n_out, bs, (r_map, o_map), todo, left_place, n_left, left_rows, lambda j: (chosen[j, 0], chosen[j, 1]), arrivals
-    )
-    copies = [pltpu.make_async_copy(acc.at[m], out.at[m], sems.at[m]) for m in range(n_out)]
-    for copy in copies:
-        copy.start()
-    for copy in copies:
+    def note(count, i, j, m):
+        todo[count] = (i * 64 + jnp.maximum(j, 0)) * 64 + jnp.maximum(m, 0)
+        return count + ((i >= 0) & (j >= 0) & (m >= 0)).astype(jnp.int32)
+
+    def collect(i, count):
+        row, base = late[2 * i], (i // n_s * (KB + 1) + late[2 * i + 1]) * CB
+        for c in range(CB):
+            count = note(count, i, r_map[base + c], o_map[row * CB + c])
+        return count
+
+    count, ends = jnp.int32(0), []
+    for lo, hi in zip(starts, starts[1:]):
+        count = lax.fori_loop(lo, hi, collect, count)
+        ends.append(count // WIDE)
+    ordered = count
+    slots = range(starts[-1] // n_s, depth)
+    for cell in range(l_map.shape[0]):
+        l_map[cell] = -1
+    for i in range(starts[-1], n_left):
+        l_map[(i // n_s - slots[0]) * RB * KB + late[2 * i] * KB + late[2 * i + 1]] = i
+
+    def gather(m, count):
+        row, c = pairs[m, 0], pairs[m, 1]
+        for slot in slots:
+            for k in range(KB):
+                i = l_map[(slot - slots[0]) * RB * KB + row * KB + k]
+                count = note(count, i, r_map[(slot * (KB + 1) + k) * CB + c], m)
+        return count
+
+    count = lax.fori_loop(0, n_out, gather, count)
+    for u in range(2 * NARROW):
+        todo[count + u] = n_out
+
+    def product(code):
+        i, j, m = code // 4096, (code // 64) % 64, code % 64
+        left_high, left_low = halves(block(left_rows, i, bs))
+        high, low = chosen[j, 0], chosen[j, 1]
+        acc[m] += dot(left_high, high) + dot(left_high, low) + dot(left_low, high)
+
+    def several(q, carry):
+        for u in range(WIDE):
+            product(todo[q * WIDE + u])
+        return carry
+
+    def send(m, carry):
+        pltpu.make_async_copy(acc.at[m], out.at[m], sems.at[m]).start()
+        return carry
+
+    def several_and_send(q, sent):
+        for u in range(NARROW):
+            product(todo[q * NARROW + u])
+        following = (q + 1) * NARROW
+        done = jnp.where(following >= ordered, todo[following] % 64, sent)
+        lax.fori_loop(sent, done, send, 0)
+        return done
+
+    at = 0
+    for copy, end in zip(fetched, ends):
         copy.wait()
+        lax.fori_loop(at, end, several, 0)
+        at = end
+    fetched[-1].wait()
+    sent = lax.fori_loop(at * (WIDE // NARROW), (count + NARROW - 1) // NARROW, several_and_send, jnp.int32(0))
+    lax.fori_loop(sent, n_out, send, 0)
+    for m in range(n_out):
+        pltpu.make_async_copy(acc.at[m], out.at[m], sems.at[m]).wait()
 
 
 def last_products(pairs, late, left, n_s, acc, chosen, right_list):
@@ -318,9 +387,8 @@
         scratch_shapes=[
             pltpu.VMEM(acc.shape, acc.dtype),
             pltpu.VMEM(left.shape, left.dtype),
-            pltpu.SMEM((depth * (KB + 1) * CB,), jnp.int32),
-            pltpu.SMEM((RB * CB,), jnp.int32),
-            pltpu.SMEM((depth * n_s * CB + 8,), jnp.int32),
+            [pltpu.SMEM((size,), jnp.int32) for size in (depth * (KB + 1) * CB, RB * CB, depth * RB * KB)],
+            pltpu.SMEM((depth * n_s * CB + 2 * NARROW,), jnp.int32),
             pltpu.SemaphoreType.DMA((n_out + pl.cdiv(depth * n_s, FETCH),)),
         ],
         compiler_params=pltpu.CompilerParams(vmem_limit_bytes=LAST_LIMIT),

time: 126 us -> 126 us (level); the launches traced: 127 us -> 124 us
  Pallas kernels: 36.6 us -> 30 us
  waiting for transfers between devices: 74.7 us -> 77.9 us
    pallas_call x2, Pallas kernels: 22.1 us -> 18.5 us  [own_products(): pl.pallas_call(functools.partial(own_kernel, slot, n_left, n_x, plan, len...]
    ppermute x1, waiting for transfers between devices: 7.22 us -> 10.4 us  [per_device(): their_list = lax.ppermute(s_own_list.reshape(-1), 'bcast', partner)]
    pallas_call x1, Pallas kernels: 10.9 us -> 7.99 us  [last_products(): pl.pallas_call(functools.partial(last_kernel, n_s), in_specs=[SMEM] * 3 +...]
  transfers between devices with their start and end apart: 12 -> 12, of which waited for: 4 -> 4; matrix products, arithmetic and copies ran while one was open for 1% -> 1% of each run, Pallas kernels for 20% -> 18%
where the time goes in v7:
time: 126 us; the launch traced here: 124 us
  waiting for transfers between devices  77.9 us (62%)
  Pallas kernels  30 us (24%)
  starting transfers between devices  14.2 us (11%)
  local copies, waits for them, and re-layouts  2.22 us (2%)
    ppermute x7, waiting for transfers between devices, moved(): lax.ppermute(part, 'loop', [(g, (g + to[g % 4]) % length) for g in range(...  67.5 us
    pallas_call x2, Pallas kernels, own_products(): pl.pallas_call(functools.partial(own_kernel, slot, n_left, n_x, plan, len...  18.5 us
    ppermute x1, waiting for transfers between devices, per_device(): their_list = lax.ppermute(s_own_list.reshape(-1), 'bcast', partner)  10.4 us
    pallas_call x1, Pallas kernels, last_products(): pl.pallas_call(functools.partial(last_kernel, n_s), in_specs=[SMEM] * 3 +...  7.99 us
    ppermute x7, starting transfers between devices, moved(): lax.ppermute(part, 'loop', [(g, (g + to[g % 4]) % length) for g in range(...  6.49 us
    ppermute x3, starting transfers between devices, last_choice(): lax.ppermute(part, 'loop', [(g, g - 1) for g in range(3, length, 4)])  4.12 us
    pallas_call x1, Pallas kernels, pack(): pl.pallas_call(functools.partial(pack_kernel, cuts), in_specs=[SMEM, pl.B...  3.5 us
    ppermute x1, starting transfers between devices, per_device(): came = lax.ppermute(s_own, 'bcast', partner)  2.97 us
  transfers between devices with their start and end apart: 12, of which 4 were waited for; matrix products, arithmetic and copies ran while one was open for 1% of the time, Pallas kernels for 18%

profile of v7, /device:TPU:0, one launch (start us, length us, event | category | flops | bytes accessed | tf_op | source)
XLA Modules:
  0.0 124.3 jit_solution(8318442068137515405)
XLA Ops:
  0.0 3.0 %collective-permute-start.11 = (f32[5120,256]{1,0:T(8,128)}, f32[5120,256]{1,0:T(8,128)}, u32[]{:S(2)}, u32[]{:S(2)}) collective-permute-start(f32[5120,256]{1,0:T(8,128)} %bitcast.10), channel_id=1, source_target_pairs={{0,1},{1,0},{2,3},{3,2},{4,5},{5,4},{6,7},{7,6},{8,9},{9,8},{10,11... | collective-permute-start | bytes 15728648 | tf_op jit(solution)/shard_map/ppermute | solution.py:411
  3.0 0.8 copy.17.places
  3.7 0.0 copy-start.4
  3.7 0.0 copy-start.3
  3.7 0.0 copy-start.1
  3.7 3.5 %pack.1 = (f32[3080,256]{1,0:T(8,128)S(1)}, f32[1032,256]{1,0:T(8,128)S(1)}, f32[1032,256]{1,0:T(8,128)S(1)}, f32[1032,256]{1,0:T(8,128)S(1)}) custom-call(s32[12,2]{1,0:T(8,128)S(1)} %copy.17.places, f32[3072,256]{1,0:T(8,128)} %bitcast.13), custom_call_target="tpu_custom_call" | custom-call | bytes 1048576 | tf_op jit(solution)/shard_map/pack/pallas_call | solution.py:47
  7.2 0.0 copy-start
  7.3 2.8 %collective-permute-start.5 = (f32[3080,256]{1,0:T(8,128)S(1)}, f32[3080,256]{1,0:T(8,128)}, u32[]{:S(2)}, u32[]{:S(2)}) collective-permute-start(f32[3080,256]{1,0:T(8,128)S(1)} %get-tuple-element.18.refs_1_), channel_id=1, source_target_pairs={{0,26},{2,0},{4,30},{6,4},{8,2},{10,8},{12,6},{14,12},{16,10},{18,... | collective-permute-start | bytes 9461768 | tf_op jit(solution)/shard_map/ppermute | solution.py:420
  10.1 1.9 %collective-permute-start.3 = (f32[1032,256]{1,0:T(8,128)S(1)}, f32[1032,256]{1,0:T(8,128)}, u32[]{:S(2)}, u32[]{:S(2)}) collective-permute-start(f32[1032,256]{1,0:T(8,128)S(1)} %get-tuple-element.19), channel_id=1, source_target_pairs={{0,30},{2,4},{4,2},{6,0},{8,6},{10,12},{12,10},{14,8},{16,14},{18,... | collective-permute-start | bytes 3170312 | tf_op jit(solution)/shard_map/ppermute | solution.py:420
  12.0 0.2 collective-permute-start.4
  12.2 1.4 %collective-permute-start.1 = (f32[1032,256]{1,0:T(8,128)S(1)}, f32[1032,256]{1,0:T(8,128)}, u32[]{:S(2)}, u32[]{:S(2)}) collective-permute-start(f32[1032,256]{1,0:T(8,128)S(1)} %get-tuple-element.17), channel_id=1, source_target_pairs={{0,30},{2,4},{4,2},{6,0},{8,6},{10,12},{12,10},{14,8},{16,14},{18,... | collective-permute-start | bytes 3170312 | tf_op jit(solution)/shard_map/ppermute | solution.py:420
  13.6 42.7 %collective-permute-done.3.refs_2_.refs_5_ = f32[1032,256]{1,0:T(8,128)} collective-permute-done((f32[1032,256]{1,0:T(8,128)S(1)}, f32[1032,256]{1,0:T(8,128)}, u32[]{:S(2)}, u32[]{:S(2)}) %collective-permute-start.3) | collective-permute-done | bytes 1056800 | tf_op jit(solution)/shard_map/ppermute | solution.py:420
  56.3 0.0 collective-permute-start.6
  56.3 11.3 %collective-permute-done.4.refs_3_.refs_6_ = f32[1032,256]{1,0:T(8,128)} collective-permute-done((f32[1032,256]{1,0:T(8,128)S(1)}, f32[1032,256]{1,0:T(8,128)}, u32[]{:S(2)}, u32[]{:S(2)}) %collective-permute-start.4) | collective-permute-done | bytes 1056800 | tf_op jit(solution)/shard_map/ppermute | solution.py:420
  67.6 0.0 collective-permute-start.7
  67.6 13.5 %collective-permute-done.1.refs_4_.refs_7_ = f32[1032,256]{1,0:T(8,128)} collective-permute-done((f32[1032,256]{1,0:T(8,128)S(1)}, f32[1032,256]{1,0:T(8,128)}, u32[]{:S(2)}, u32[]{:S(2)}) %collective-permute-start.1) | collective-permute-done | bytes 1056800 | tf_op jit(solution)/shard_map/ppermute | solution.py:420
  81.1 0.2 collective-permute-start.2
  81.2 0.0 copy-done.4
  81.2 0.1 copy.22.pairs
  81.3 0.0 copy-done.3
  81.3 0.1 reshape.9
  81.4 0.1 copy.21.left_list
  81.5 0.0 collective-permute-done.6.refs_2_
  81.5 1.7 %collective-permute-start.8 = (f32[1032,256]{1,0:T(8,128)}, f32[1032,256]{1,0:T(8,128)}, u32[]{:S(2)}, u32[]{:S(2)}) collective-permute-start(f32[1032,256]{1,0:T(8,128)} %collective-permute-done.6.refs_2_), channel_id=1, source_target_pairs={{6,4},{14,12},{22,20},{30,28},{7,5},{15,13},{23,21},{31,29}} | collective-permute-start | bytes 3170312 | tf_op jit(solution)/shard_map/ppermute | solution.py:430
  83.2 0.0 collective-permute-done.7.refs_3_
  83.2 1.7 %collective-permute-start.9 = (f32[1032,256]{1,0:T(8,128)}, f32[1032,256]{1,0:T(8,128)}, u32[]{:S(2)}, u32[]{:S(2)}) collective-permute-start(f32[1032,256]{1,0:T(8,128)} %collective-permute-done.7.refs_3_), channel_id=1, source_target_pairs={{6,4},{14,12},{22,20},{30,28},{7,5},{15,13},{23,21},{31,29}} | collective-permute-start | bytes 3170312 | tf_op jit(solution)/shard_map/ppermute | solution.py:430
  84.9 0.0 collective-permute-done.5.refs_5_.refs_8_
  84.9 0.0 copy-done
  84.9 0.0 copy-done.1
  84.9 9.0 %own_products.2 = (f32[11,256,256]{2,1,0:T(8,128)}, bf16[12,2,256,256]{3,2,1,0:T(8,128)(2,1)}, s32[24]{0:T(128)S(1)}) custom-call(s32[4]{0:T(128)S(1)} %bitcast.8, s32[10,2]{1,0:T(8,128)S(1)} %copy.22.pairs, s32[20,2]{1,0:T(8,128)S(1)} %copy.21.left_list, f32[5120,256]{1,0:T(8,128)} %bitcast.11, f32[3080,256]{1,0:T(8,128)} %copy-done, ...), custom_call_target="tpu_custom_call" | custom-call | bytes 1048576 | tf_op jit(solution)/shard_map/own_products/pallas_call | solution.py:274
  93.9 0.0 collective-permute-done.2.refs_4_
  93.9 0.7 collective-permute-start.10
  94.6 0.1 copy.15
  94.8 0.1 reshape_reshape.3
  94.8 0.6 collective-permute-start
  95.4 0.0 collective-permute-done.8.refs_9_
  95.4 0.0 collective-permute-done.9.refs_10_
  95.4 0.0 collective-permute-done.10.refs_11_
  95.4 0.0 copy-start.2
  95.5 1.0 copy-done.2
  96.4 9.5 %own_products.3 = (f32[11,256,256]{2,1,0:T(8,128)S(1)}, bf16[24,2,256,256]{3,2,1,0:T(8,128)(2,1)S(1)}, s32[48]{0:T(128)S(1)}) custom-call(s32[4]{0:T(128)S(1)} %bitcast.9, s32[10,2]{1,0:T(8,128)S(1)} %copy.22.pairs, s32[20,2]{1,0:T(8,128)S(1)} %copy.21.left_list, s32[24]{0:T(128)S(1)} %get-tuple-element.22.refs_0_, f32[5120,256]{1,0:T(8,128)} %bitcast.12, ...), custom_call_target="tpu_custom_call" | custom-call | bytes 1048576 | tf_op jit(solution)/shard_map/own_products/pallas_call | solution.py:274
  105.9 10.4 %collective-permute-done.late = s32[40]{0:T(128)S(1)} collective-permute-done((s32[40]{0:T(128)S(1)}, s32[40]{0:T(128)S(1)}, u32[]{:S(2)}, u32[]{:S(2)}) %collective-permute-start) | collective-permute-done | bytes 192 | tf_op jit(solution)/shard_map/ppermute | solution.py:412
  116.3 0.0 collective-permute-done.11.left
  116.3 8.0 %last_products.1 = f32[10,256,256]{2,1,0:T(8,128)} custom-call(s32[10,2]{1,0:T(8,128)S(1)} %copy.22.pairs, s32[40]{0:T(128)S(1)} %collective-permute-done.late, s32[48]{0:T(128)S(1)} %get-tuple-element.26.right_list, f32[5120,256]{1,0:T(8,128)} %collective-permute-done.11.left, f32[11,256,256]{2,1,0:T(8,128)S(1)} %get-tuple-element.27.before, ...), custom_call_target="tpu_custom_call" | custom-call | bytes 1048576 | tf_op jit(solution)/shard_map/last_products/pallas_call | solution.py:382
  (1 shorter events, 0.0 us)
Async XLA Ops:
  0.0 116.3 %collective-permute-start.11 = (f32[5120,256]{1,0:T(8,128)}, f32[5120,256]{1,0:T(8,128)}, u32[]{:S(2)}, u32[]{:S(2)}) collective-permute-start(f32[5120,256]{1,0:T(8,128)} %bitcast.10), channel_id=1, source_target_pairs={{0,1},{1,0},{2,3},{3,2},{4,5},{5,4},{6,7},{7,6},{8,9},{9,8},{10,11... | collective-permute-start | bytes 15728648 | tf_op jit(solution)/shard_map/ppermute | solution.py:411
  3.7 77.5 %copy-start.4 = (s32[1,1,10,2]{2,3,1,0:T(2,128)S(1)}, s32[1,1,10,2]{2,3,1,0:T(2,128)}, u32[]{:S(2)}) copy-start(s32[1,1,10,2]{2,3,1,0:T(2,128)} %param.10) | copy-start | bytes 244
  3.7 77.6 %copy-start.3 = (s32[1,1,2,10,2]{3,4,2,1,0:T(2,128)S(1)}, s32[1,1,2,10,2]{3,4,2,1,0:T(2,128)}, u32[]{:S(2)}) copy-start(s32[1,1,2,10,2]{3,4,2,1,0:T(2,128)} %param.7) | copy-start | bytes 484
  3.7 81.2 %copy-start.1 = (s32[1,4]{1,0:T(1,128)S(1)}, s32[1,4]{1,0:T(1,128)}, u32[]{:S(2)}) copy-start(s32[1,4]{1,0:T(1,128)} %param.11) | copy-start | bytes 52
  7.2 77.7 %copy-start = (f32[3080,256]{1,0:T(8,128)}, f32[3080,256]{1,0:T(8,128)S(1)}, u32[]{:S(2)}) copy-start(f32[3080,256]{1,0:T(8,128)S(1)} %get-tuple-element.18.refs_1_) | copy-start | bytes 9461764
  7.3 77.7 %collective-permute-start.5 = (f32[3080,256]{1,0:T(8,128)S(1)}, f32[3080,256]{1,0:T(8,128)}, u32[]{:S(2)}, u32[]{:S(2)}) collective-permute-start(f32[3080,256]{1,0:T(8,128)S(1)} %get-tuple-element.18.refs_1_), channel_id=1, source_target_pairs={{0,26},{2,0},{4,30},{6,4},{8,2},{10,8},{12,6},{14,12},{16,10},{18,... | collective-permute-start | bytes 9461768 | tf_op jit(solution)/shard_map/ppermute | solution.py:420
  10.1 46.2 %collective-permute-start.3 = (f32[1032,256]{1,0:T(8,128)S(1)}, f32[1032,256]{1,0:T(8,128)}, u32[]{:S(2)}, u32[]{:S(2)}) collective-permute-start(f32[1032,256]{1,0:T(8,128)S(1)} %get-tuple-element.19), channel_id=1, source_target_pairs={{0,30},{2,4},{4,2},{6,0},{8,6},{10,12},{12,10},{14,8},{16,14},{18,... | collective-permute-start | bytes 3170312 | tf_op jit(solution)/shard_map/ppermute | solution.py:420
  12.0 55.6 %collective-permute-start.4 = (f32[1032,256]{1,0:T(8,128)S(1)}, f32[1032,256]{1,0:T(8,128)}, u32[]{:S(2)}, u32[]{:S(2)}) collective-permute-start(f32[1032,256]{1,0:T(8,128)S(1)} %get-tuple-element.20), channel_id=1, source_target_pairs={{0,30},{2,4},{4,2},{6,0},{8,6},{10,12},{12,10},{14,8},{16,14},{18,... | collective-permute-start | bytes 3170312 | tf_op jit(solution)/shard_map/ppermute | solution.py:420
  12.2 68.9 %collective-permute-start.1 = (f32[1032,256]{1,0:T(8,128)S(1)}, f32[1032,256]{1,0:T(8,128)}, u32[]{:S(2)}, u32[]{:S(2)}) collective-permute-start(f32[1032,256]{1,0:T(8,128)S(1)} %get-tuple-element.17), channel_id=1, source_target_pairs={{0,30},{2,4},{4,2},{6,0},{8,6},{10,12},{12,10},{14,8},{16,14},{18,... | collective-permute-start | bytes 3170312 | tf_op jit(solution)/shard_map/ppermute | solution.py:420
  56.3 25.2 %collective-permute-start.6 = (f32[1032,256]{1,0:T(8,128)}, f32[1032,256]{1,0:T(8,128)}, u32[]{:S(2)}, u32[]{:S(2)}) collective-permute-start(f32[1032,256]{1,0:T(8,128)} %collective-permute-done.3.refs_2_.refs_5_), channel_id=1, source_target_pairs={{0,2},{2,0},{4,30},{6,4},{8,10},{10,8},{12,6},{14,12},{16,18},{18,... | collective-permute-start | bytes 3170312 | tf_op jit(solution)/shard_map/ppermute | solution.py:420
  67.6 15.6 %collective-permute-start.7 = (f32[1032,256]{1,0:T(8,128)}, f32[1032,256]{1,0:T(8,128)}, u32[]{:S(2)}, u32[]{:S(2)}) collective-permute-start(f32[1032,256]{1,0:T(8,128)} %collective-permute-done.4.refs_3_.refs_6_), channel_id=1, source_target_pairs={{0,2},{2,0},{4,30},{6,4},{8,10},{10,8},{12,6},{14,12},{16,18},{18,... | collective-permute-start | bytes 3170312 | tf_op jit(solution)/shard_map/ppermute | solution.py:420
  81.1 12.8 %collective-permute-start.2 = (f32[1032,256]{1,0:T(8,128)}, f32[1032,256]{1,0:T(8,128)}, u32[]{:S(2)}, u32[]{:S(2)}) collective-permute-start(f32[1032,256]{1,0:T(8,128)} %collective-permute-done.1.refs_4_.refs_7_), channel_id=1, source_target_pairs={{0,2},{2,0},{4,30},{6,4},{8,10},{10,8},{12,6},{14,12},{16,18},{18,... | collective-permute-start | bytes 3170312 | tf_op jit(solution)/shard_map/ppermute | solution.py:420
  81.5 13.9 %collective-permute-start.8 = (f32[1032,256]{1,0:T(8,128)}, f32[1032,256]{1,0:T(8,128)}, u32[]{:S(2)}, u32[]{:S(2)}) collective-permute-start(f32[1032,256]{1,0:T(8,128)} %collective-permute-done.6.refs_2_), channel_id=1, source_target_pairs={{6,4},{14,12},{22,20},{30,28},{7,5},{15,13},{23,21},{31,29}} | collective-permute-start | bytes 3170312 | tf_op jit(solution)/shard_map/ppermute | solution.py:430
  83.2 12.2 %collective-permute-start.9 = (f32[1032,256]{1,0:T(8,128)}, f32[1032,256]{1,0:T(8,128)}, u32[]{:S(2)}, u32[]{:S(2)}) collective-permute-start(f32[1032,256]{1,0:T(8,128)} %collective-permute-done.7.refs_3_), channel_id=1, source_target_pairs={{6,4},{14,12},{22,20},{30,28},{7,5},{15,13},{23,21},{31,29}} | collective-permute-start | bytes 3170312 | tf_op jit(solution)/shard_map/ppermute | solution.py:430
  93.9 1.5 %collective-permute-start.10 = (f32[1032,256]{1,0:T(8,128)}, f32[1032,256]{1,0:T(8,128)S(1)}, u32[]{:S(2)}, u32[]{:S(2)}) collective-permute-start(f32[1032,256]{1,0:T(8,128)} %collective-permute-done.2.refs_4_), channel_id=1, source_target_pairs={{6,4},{14,12},{22,20},{30,28},{7,5},{15,13},{23,21},{31,29}} | collective-permute-start | bytes 3170312 | tf_op jit(solution)/shard_map/ppermute | solution.py:430
  94.8 21.5 %collective-permute-start = (s32[40]{0:T(128)S(1)}, s32[40]{0:T(128)S(1)}, u32[]{:S(2)}, u32[]{:S(2)}) collective-permute-start(s32[40]{0:T(128)S(1)} %reshape_reshape.3), channel_id=1, source_target_pairs={{0,1},{1,0},{2,3},{3,2},{4,5},{5,4},{6,7},{7,6},{8,9},{9,8},{10,11... | collective-permute-start | bytes 488 | tf_op jit(solution)/shard_map/ppermute | solution.py:412
  95.4 1.0 copy-start.2

commit v8 on v7

--- a/solution.py
+++ b/solution.py
@@ -298,7 +298,7 @@
     for q, lo in enumerate(starts):
         rows = pl.ds(lo * bs, min(FETCH, n_left - lo) * bs)
         fetched.append(pltpu.make_async_copy(left.at[rows], left_rows.at[rows], sems.at[n_out + q]))
-        fetched[q].start()
+    fetched[0].start()
     fill_map(o_map, RB * CB, lambda m, d: pairs[m, d], n_out, CB)
     for cell in range(r_map.shape[0]):
         r_map[cell] = -1
@@ -306,6 +306,7 @@
         r_map[(j // n_x * (KB + 1) + right_list[2 * j]) * CB + right_list[2 * j + 1]] = j
     for m in range(n_out):
         acc[m] = before[m]
+    fetched[1].start()
 
     def note(count, i, j, m):
         todo[count] = (i * 64 + jnp.maximum(j, 0)) * 64 + jnp.maximum(m, 0)
@@ -344,7 +345,10 @@
         i, j, m = code // 4096, (code // 64) % 64, code % 64
         left_high, left_low = halves(block(left_rows, i, bs))
         high, low = chosen[j, 0], chosen[j, 1]
-        acc[m] += dot(left_high, high) + dot(left_high, low) + dot(left_low, high)
+        for z in range(0, bs, bs // 2):
+            part = slice(z, z + bs // 2)
+            first, second = left_high[part], left_low[part]
+            acc[m, part] += dot(first, high) + dot(first, low) + dot(second, high)
 
     def several(q, carry):
         for u in range(WIDE):
@@ -366,6 +370,9 @@
     at = 0
     for copy, end in zip(fetched, ends):
         copy.wait()
+        if copy is fetched[0]:
+            for later in fetched[2:]:
+                later.start()
         lax.fori_loop(at, end, several, 0)
         at = end
     fetched[-1].wait()

time: 126 us -> 125 us (level); the launches traced: 124 us -> 125 us
  transfers between devices with their start and end apart: 12 -> 12, of which waited for: 4 -> 4; matrix products, arithmetic and copies ran while one was open for 1% -> 1% of each run, Pallas kernels for 18% -> 17%
where the time goes in v8:
time: 125 us
  waiting for transfers between devices  79 us (63%)
  Pallas kernels  30.4 us (24%)
  starting transfers between devices  13.6 us (11%)
  local copies, waits for them, and re-layouts  2.22 us (2%)
    ppermute x7, waiting for transfers between devices, moved(): lax.ppermute(part, 'loop', [(g, (g + to[g % 4]) % length) for g in range(...  67.5 us
    pallas_call x2, Pallas kernels, own_products(): pl.pallas_call(functools.partial(own_kernel, slot, n_left, n_x, plan, len...  17.9 us
    ppermute x1, waiting for transfers between devices, per_device(): their_list = lax.ppermute(s_own_list.reshape(-1), 'bcast', partner)  11.5 us
    pallas_call x1, Pallas kernels, last_products(): pl.pallas_call(functools.partial(last_kernel, n_s), in_specs=[SMEM] * 3 +...  9.04 us
    ppermute x7, starting transfers between devices, moved(): lax.ppermute(part, 'loop', [(g, (g + to[g % 4]) % length) for g in range(...  6.49 us
    ppermute x3, starting transfers between devices, last_choice(): lax.ppermute(part, 'loop', [(g, g - 1) for g in range(3, length, 4)])  4.12 us
    pallas_call x1, Pallas kernels, pack(): pl.pallas_call(functools.partial(pack_kernel, cuts), in_specs=[SMEM, pl.B...  3.5 us
    ppermute x1, starting transfers between devices, per_device(): came = lax.ppermute(s_own, 'bcast', partner)  2.97 us
  transfers between devices with their start and end apart: 12, of which 4 were waited for; matrix products, arithmetic and copies ran while one was open for 1% of the time, Pallas kernels for 17%

profile of v8, /device:TPU:0, one launch (start us, length us, event | category | flops | bytes accessed | tf_op | source)
XLA Modules:
  0.0 125.4 jit_solution(9778358716171415791)
XLA Ops:
  0.0 3.0 %collective-permute-start.11 = (f32[5120,256]{1,0:T(8,128)}, f32[5120,256]{1,0:T(8,128)}, u32[]{:S(2)}, u32[]{:S(2)}) collective-permute-start(f32[5120,256]{1,0:T(8,128)} %bitcast.10), channel_id=1, source_target_pairs={{0,1},{1,0},{2,3},{3,2},{4,5},{5,4},{6,7},{7,6},{8,9},{9,8},{10,11... | collective-permute-start | bytes 15728648 | tf_op jit(solution)/shard_map/ppermute | solution.py:418
  3.0 0.8 copy.17.places
  3.7 0.0 copy-start.4
  3.7 0.0 copy-start.3
  3.7 0.0 copy-start.1
  3.7 3.5 %pack.1 = (f32[3080,256]{1,0:T(8,128)S(1)}, f32[1032,256]{1,0:T(8,128)S(1)}, f32[1032,256]{1,0:T(8,128)S(1)}, f32[1032,256]{1,0:T(8,128)S(1)}) custom-call(s32[12,2]{1,0:T(8,128)S(1)} %copy.17.places, f32[3072,256]{1,0:T(8,128)} %bitcast.13), custom_call_target="tpu_custom_call" | custom-call | bytes 1048576 | tf_op jit(solution)/shard_map/pack/pallas_call | solution.py:47
  7.2 0.0 copy-start
  7.3 2.8 %collective-permute-start.5 = (f32[3080,256]{1,0:T(8,128)S(1)}, f32[3080,256]{1,0:T(8,128)}, u32[]{:S(2)}, u32[]{:S(2)}) collective-permute-start(f32[3080,256]{1,0:T(8,128)S(1)} %get-tuple-element.18.refs_1_), channel_id=1, source_target_pairs={{0,26},{2,0},{4,30},{6,4},{8,2},{10,8},{12,6},{14,12},{16,10},{18,... | collective-permute-start | bytes 9461768 | tf_op jit(solution)/shard_map/ppermute | solution.py:427
  10.1 1.9 %collective-permute-start.3 = (f32[1032,256]{1,0:T(8,128)S(1)}, f32[1032,256]{1,0:T(8,128)}, u32[]{:S(2)}, u32[]{:S(2)}) collective-permute-start(f32[1032,256]{1,0:T(8,128)S(1)} %get-tuple-element.19), channel_id=1, source_target_pairs={{0,30},{2,4},{4,2},{6,0},{8,6},{10,12},{12,10},{14,8},{16,14},{18,... | collective-permute-start | bytes 3170312 | tf_op jit(solution)/shard_map/ppermute | solution.py:427
  12.0 0.2 collective-permute-start.4
  12.2 1.4 %collective-permute-start.1 = (f32[1032,256]{1,0:T(8,128)S(1)}, f32[1032,256]{1,0:T(8,128)}, u32[]{:S(2)}, u32[]{:S(2)}) collective-permute-start(f32[1032,256]{1,0:T(8,128)S(1)} %get-tuple-element.17), channel_id=1, source_target_pairs={{0,30},{2,4},{4,2},{6,0},{8,6},{10,12},{12,10},{14,8},{16,14},{18,... | collective-permute-start | bytes 3170312 | tf_op jit(solution)/shard_map/ppermute | solution.py:427
  13.6 42.7 %collective-permute-done.3.refs_2_.refs_5_ = f32[1032,256]{1,0:T(8,128)} collective-permute-done((f32[1032,256]{1,0:T(8,128)S(1)}, f32[1032,256]{1,0:T(8,128)}, u32[]{:S(2)}, u32[]{:S(2)}) %collective-permute-start.3) | collective-permute-done | bytes 1056800 | tf_op jit(solution)/shard_map/ppermute | solution.py:427
  56.3 0.0 collective-permute-start.6
  56.3 11.3 %collective-permute-done.4.refs_3_.refs_6_ = f32[1032,256]{1,0:T(8,128)} collective-permute-done((f32[1032,256]{1,0:T(8,128)S(1)}, f32[1032,256]{1,0:T(8,128)}, u32[]{:S(2)}, u32[]{:S(2)}) %collective-permute-start.4) | collective-permute-done | bytes 1056800 | tf_op jit(solution)/shard_map/ppermute | solution.py:427
  67.6 0.0 collective-permute-start.7
  67.6 13.5 %collective-permute-done.1.refs_4_.refs_7_ = f32[1032,256]{1,0:T(8,128)} collective-permute-done((f32[1032,256]{1,0:T(8,128)S(1)}, f32[1032,256]{1,0:T(8,128)}, u32[]{:S(2)}, u32[]{:S(2)}) %collective-permute-start.1) | collective-permute-done | bytes 1056800 | tf_op jit(solution)/shard_map/ppermute | solution.py:427
  81.1 0.2 collective-permute-start.2
  81.2 0.0 copy-done.4
  81.2 0.1 copy.22.pairs
  81.3 0.0 copy-done.3
  81.3 0.1 reshape.9
  81.4 0.1 copy.21.left_list
  81.5 0.0 collective-permute-done.6.refs_2_
  81.5 1.7 %collective-permute-start.8 = (f32[1032,256]{1,0:T(8,128)}, f32[1032,256]{1,0:T(8,128)}, u32[]{:S(2)}, u32[]{:S(2)}) collective-permute-start(f32[1032,256]{1,0:T(8,128)} %collective-permute-done.6.refs_2_), channel_id=1, source_target_pairs={{6,4},{14,12},{22,20},{30,28},{7,5},{15,13},{23,21},{31,29}} | collective-permute-start | bytes 3170312 | tf_op jit(solution)/shard_map/ppermute | solution.py:437
  83.2 0.0 collective-permute-done.7.refs_3_
  83.2 1.7 %collective-permute-start.9 = (f32[1032,256]{1,0:T(8,128)}, f32[1032,256]{1,0:T(8,128)}, u32[]{:S(2)}, u32[]{:S(2)}) collective-permute-start(f32[1032,256]{1,0:T(8,128)} %collective-permute-done.7.refs_3_), channel_id=1, source_target_pairs={{6,4},{14,12},{22,20},{30,28},{7,5},{15,13},{23,21},{31,29}} | collective-permute-start | bytes 3170312 | tf_op jit(solution)/shard_map/ppermute | solution.py:437
  84.9 0.0 collective-permute-done.5.refs_5_.refs_8_
  84.9 0.0 copy-done
  84.9 0.0 copy-done.1
  84.9 9.6 %own_products.2 = (f32[11,256,256]{2,1,0:T(8,128)}, bf16[12,2,256,256]{3,2,1,0:T(8,128)(2,1)}, s32[24]{0:T(128)S(1)}) custom-call(s32[4]{0:T(128)S(1)} %bitcast.8, s32[10,2]{1,0:T(8,128)S(1)} %copy.22.pairs, s32[20,2]{1,0:T(8,128)S(1)} %copy.21.left_list, f32[5120,256]{1,0:T(8,128)} %bitcast.11, f32[3080,256]{1,0:T(8,128)} %copy-done, ...), custom_call_target="tpu_custom_call" | custom-call | bytes 1048576 | tf_op jit(solution)/shard_map/own_products/pallas_call | solution.py:274
  94.6 0.0 collective-permute-done.2.refs_4_
  94.6 0.7 collective-permute-start.10
  95.3 0.1 copy.15
  95.4 0.1 reshape_reshape.3
  95.5 0.1 collective-permute-start
  95.6 0.0 collective-permute-done.8.refs_9_
  95.6 0.0 collective-permute-done.9.refs_10_
  95.6 0.0 collective-permute-done.10.refs_11_
  95.6 0.0 copy-start.2
  95.6 1.0 copy-done.2
  96.6 8.2 %own_products.3 = (f32[11,256,256]{2,1,0:T(8,128)S(1)}, bf16[24,2,256,256]{3,2,1,0:T(8,128)(2,1)S(1)}, s32[48]{0:T(128)S(1)}) custom-call(s32[4]{0:T(128)S(1)} %bitcast.9, s32[10,2]{1,0:T(8,128)S(1)} %copy.22.pairs, s32[20,2]{1,0:T(8,128)S(1)} %copy.21.left_list, s32[24]{0:T(128)S(1)} %get-tuple-element.22.refs_0_, f32[5120,256]{1,0:T(8,128)} %bitcast.12, ...), custom_call_target="tpu_custom_call" | custom-call | bytes 1048576 | tf_op jit(solution)/shard_map/own_products/pallas_call | solution.py:274
  104.8 11.5 %collective-permute-done.late = s32[40]{0:T(128)S(1)} collective-permute-done((s32[40]{0:T(128)S(1)}, s32[40]{0:T(128)S(1)}, u32[]{:S(2)}, u32[]{:S(2)}) %collective-permute-start) | collective-permute-done | bytes 192 | tf_op jit(solution)/shard_map/ppermute | solution.py:419
  116.3 0.0 collective-permute-done.11.left
  116.3 9.0 %last_products.1 = f32[10,256,256]{2,1,0:T(8,128)} custom-call(s32[10,2]{1,0:T(8,128)S(1)} %copy.22.pairs, s32[40]{0:T(128)S(1)} %collective-permute-done.late, s32[48]{0:T(128)S(1)} %get-tuple-element.26.right_list, f32[5120,256]{1,0:T(8,128)} %collective-permute-done.11.left, f32[11,256,256]{2,1,0:T(8,128)S(1)} %get-tuple-element.27.before, ...), custom_call_target="tpu_custom_call" | custom-call | bytes 1048576 | tf_op jit(solution)/shard_map/last_products/pallas_call | solution.py:389
  (1 shorter events, 0.0 us)
Async XLA Ops:
  0.0 116.3 %collective-permute-start.11 = (f32[5120,256]{1,0:T(8,128)}, f32[5120,256]{1,0:T(8,128)}, u32[]{:S(2)}, u32[]{:S(2)}) collective-permute-start(f32[5120,256]{1,0:T(8,128)} %bitcast.10), channel_id=1, source_target_pairs={{0,1},{1,0},{2,3},{3,2},{4,5},{5,4},{6,7},{7,6},{8,9},{9,8},{10,11... | collective-permute-start | bytes 15728648 | tf_op jit(solution)/shard_map/ppermute | solution.py:418
  3.7 77.5 %copy-start.4 = (s32[1,1,10,2]{2,3,1,0:T(2,128)S(1)}, s32[1,1,10,2]{2,3,1,0:T(2,128)}, u32[]{:S(2)}) copy-start(s32[1,1,10,2]{2,3,1,0:T(2,128)} %param.10) | copy-start | bytes 244
  3.7 77.6 %copy-start.3 = (s32[1,1,2,10,2]{3,4,2,1,0:T(2,128)S(1)}, s32[1,1,2,10,2]{3,4,2,1,0:T(2,128)}, u32[]{:S(2)}) copy-start(s32[1,1,2,10,2]{3,4,2,1,0:T(2,128)} %param.7) | copy-start | bytes 484
  3.7 81.2 %copy-start.1 = (s32[1,4]{1,0:T(1,128)S(1)}, s32[1,4]{1,0:T(1,128)}, u32[]{:S(2)}) copy-start(s32[1,4]{1,0:T(1,128)} %param.11) | copy-start | bytes 52
  7.2 77.7 %copy-start = (f32[3080,256]{1,0:T(8,128)}, f32[3080,256]{1,0:T(8,128)S(1)}, u32[]{:S(2)}) copy-start(f32[3080,256]{1,0:T(8,128)S(1)} %get-tuple-element.18.refs_1_) | copy-start | bytes 9461764
  7.3 77.7 %collective-permute-start.5 = (f32[3080,256]{1,0:T(8,128)S(1)}, f32[3080,256]{1,0:T(8,128)}, u32[]{:S(2)}, u32[]{:S(2)}) collective-permute-start(f32[3080,256]{1,0:T(8,128)S(1)} %get-tuple-element.18.refs_1_), channel_id=1, source_target_pairs={{0,26},{2,0},{4,30},{6,4},{8,2},{10,8},{12,6},{14,12},{16,10},{18,... | collective-permute-start | bytes 9461768 | tf_op jit(solution)/shard_map/ppermute | solution.py:427
  10.1 46.2 %collective-permute-start.3 = (f32[1032,256]{1,0:T(8,128)S(1)}, f32[1032,256]{1,0:T(8,128)}, u32[]{:S(2)}, u32[]{:S(2)}) collective-permute-start(f32[1032,256]{1,0:T(8,128)S(1)} %get-tuple-element.19), channel_id=1, source_target_pairs={{0,30},{2,4},{4,2},{6,0},{8,6},{10,12},{12,10},{14,8},{16,14},{18,... | collective-permute-start | bytes 3170312 | tf_op jit(solution)/shard_map/ppermute | solution.py:427
  12.0 55.6 %collective-permute-start.4 = (f32[1032,256]{1,0:T(8,128)S(1)}, f32[1032,256]{1,0:T(8,128)}, u32[]{:S(2)}, u32[]{:S(2)}) collective-permute-start(f32[1032,256]{1,0:T(8,128)S(1)} %get-tuple-element.20), channel_id=1, source_target_pairs={{0,30},{2,4},{4,2},{6,0},{8,6},{10,12},{12,10},{14,8},{16,14},{18,... | collective-permute-start | bytes 3170312 | tf_op jit(solution)/shard_map/ppermute | solution.py:427
  12.2 68.9 %collective-permute-start.1 = (f32[1032,256]{1,0:T(8,128)S(1)}, f32[1032,256]{1,0:T(8,128)}, u32[]{:S(2)}, u32[]{:S(2)}) collective-permute-start(f32[1032,256]{1,0:T(8,128)S(1)} %get-tuple-element.17), channel_id=1, source_target_pairs={{0,30},{2,4},{4,2},{6,0},{8,6},{10,12},{12,10},{14,8},{16,14},{18,... | collective-permute-start | bytes 3170312 | tf_op jit(solution)/shard_map/ppermute | solution.py:427
  56.3 25.2 %collective-permute-start.6 = (f32[1032,256]{1,0:T(8,128)}, f32[1032,256]{1,0:T(8,128)}, u32[]{:S(2)}, u32[]{:S(2)}) collective-permute-start(f32[1032,256]{1,0:T(8,128)} %collective-permute-done.3.refs_2_.refs_5_), channel_id=1, source_target_pairs={{0,2},{2,0},{4,30},{6,4},{8,10},{10,8},{12,6},{14,12},{16,18},{18,... | collective-permute-start | bytes 3170312 | tf_op jit(solution)/shard_map/ppermute | solution.py:427
  67.6 15.6 %collective-permute-start.7 = (f32[1032,256]{1,0:T(8,128)}, f32[1032,256]{1,0:T(8,128)}, u32[]{:S(2)}, u32[]{:S(2)}) collective-permute-start(f32[1032,256]{1,0:T(8,128)} %collective-permute-done.4.refs_3_.refs_6_), channel_id=1, source_target_pairs={{0,2},{2,0},{4,30},{6,4},{8,10},{10,8},{12,6},{14,12},{16,18},{18,... | collective-permute-start | bytes 3170312 | tf_op jit(solution)/shard_map/ppermute | solution.py:427
  81.1 13.5 %collective-permute-start.2 = (f32[1032,256]{1,0:T(8,128)}, f32[1032,256]{1,0:T(8,128)}, u32[]{:S(2)}, u32[]{:S(2)}) collective-permute-start(f32[1032,256]{1,0:T(8,128)} %collective-permute-done.1.refs_4_.refs_7_), channel_id=1, source_target_pairs={{0,2},{2,0},{4,30},{6,4},{8,10},{10,8},{12,6},{14,12},{16,18},{18,... | collective-permute-start | bytes 3170312 | tf_op jit(solution)/shard_map/ppermute | solution.py:427
  81.5 14.1 %collective-permute-start.8 = (f32[1032,256]{1,0:T(8,128)}, f32[1032,256]{1,0:T(8,128)}, u32[]{:S(2)}, u32[]{:S(2)}) collective-permute-start(f32[1032,256]{1,0:T(8,128)} %collective-permute-done.6.refs_2_), channel_id=1, source_target_pairs={{6,4},{14,12},{22,20},{30,28},{7,5},{15,13},{23,21},{31,29}} | collective-permute-start | bytes 3170312 | tf_op jit(solution)/shard_map/ppermute | solution.py:437
  83.2 12.4 %collective-permute-start.9 = (f32[1032,256]{1,0:T(8,128)}, f32[1032,256]{1,0:T(8,128)}, u32[]{:S(2)}, u32[]{:S(2)}) collective-permute-start(f32[1032,256]{1,0:T(8,128)} %collective-permute-done.7.refs_3_), channel_id=1, source_target_pairs={{6,4},{14,12},{22,20},{30,28},{7,5},{15,13},{23,21},{31,29}} | collective-permute-start | bytes 3170312 | tf_op jit(solution)/shard_map/ppermute | solution.py:437
  94.6 1.0 collective-permute-start.10
  95.5 20.8 %collective-permute-start = (s32[40]{0:T(128)S(1)}, s32[40]{0:T(128)S(1)}, u32[]{:S(2)}, u32[]{:S(2)}) collective-permute-start(s32[40]{0:T(128)S(1)} %reshape_reshape.3), channel_id=1, source_target_pairs={{0,1},{1,0},{2,3},{3,2},{4,5},{5,4},{6,7},{7,6},{8,9},{9,8},{10,11... | collective-permute-start | bytes 488 | tf_op jit(solution)/shard_map/ppermute | solution.py:419
  95.6 1.0 copy-start.2
